TPU v7x, 256 devices: a whole 4x4x8 slice. The times are simulated.
256 devices in a mesh: dp: 4 (over y), expert: 64 (over x, z, core).
Axes of the slice: x: 4, y: 4, z: 8, core: 2. Of those that a mesh axis runs over, the one named last changes fastest.
Arguments:
- tokens: bfloat16 [8192, 3584], P('expert', 'dp'), may hold values from -6 to 6
- cotangent: bfloat16 [8192, 3584], P('expert', 'dp'), may hold values from -6 to 6
- expert_ids: int32 [8192, 4], P('expert'), may hold values from 0 to 55, all different within a row; in each aligned block of 128 rows (0 to 127, 128 to 255, ...) at most 11 rows name the same one
- gate_probs: bfloat16 [8192, 4], P('expert'), may hold values from 0.049804688 to 1
- slot_expert: int32 [64], replicated, may hold values from 0 to 55, as said below
- w_gate: bfloat16 [64, 3584, 1024], P('expert', None, 'dp'), as said below
- w_up: bfloat16 [64, 3584, 1024], P('expert', None, 'dp'), as said below
- w_down: bfloat16 [64, 1024, 3584], P('expert', 'dp'), as said below
Outputs:
- d_tokens: bfloat16 [8192, 3584], P('expert', 'dp')
- d_probs: float32 [8192, 4], P('expert')
- grad_gate: bfloat16 [64, 3584, 1024], P('expert', None, 'dp')
- grad_up: bfloat16 [64, 3584, 1024], P('expert', None, 'dp')
- grad_down: bfloat16 [64, 1024, 3584], P('expert', 'dp')
Inputs may be any that keep to these rules, and one draw needn't show every extreme that they name: `expert_ids`: in each aligned block of 128 rows no expert is named by more than 11 rows, a bound that some block reaches. `slot_expert`: every expert appears once or twice; an expert that appears twice holds slots 2 j and 2 j + 1 for some j, and 8 experts appear twice. `w_gate`: slots that hold the same expert hold equal weights. `w_up`: slots that hold the same expert hold equal weights. `w_down`: slots that hold the same expert hold equal weights.
All inputs are finite; a program needn't handle non-finite values.
Results may differ from a plain program's by a relative error of at most 0.015.
Values may be sent and summed in bfloat16 or wider, within the bound.
No kernel may reach another device: no remote copies, remote signals or barrier semaphores. Data moves between devices by JAX's collectives and lax.ppermute only.
A program may use at most 256 MiB of HBM per device.

v0:
```python
import jax
import jax.numpy as jnp
from jax import lax
from jax.sharding import PartitionSpec as P


def partner_2(x, axis, apart):
    return lax.ppermute(x, axis, [(i, i ^ 1 << apart) for i in range(lax.axis_size(axis))])


def silu_parts(gate):
    sig = jax.nn.sigmoid(gate)
    return (gate * sig, sig * (1.0 + gate * (1.0 - sig)))


def contract(left, right, left_dim, right_dim):
    return lax.dot_general(
        left, right, (((left_dim,), (right_dim,)), ((), ())), preferred_element_type=jnp.float32
    )


def shards(tokens, cotangent, expert_ids, gate_probs, slot_expert, w_gate, w_up, w_down):
    slots = lax.axis_size("expert")
    here = lax.axis_index("expert")
    tok_rows, quarter = tokens.shape
    top = expert_ids.shape[1]
    experts = slots - max(2, slots // 8)
    capacity = max(2, 5 * tok_rows * top // (4 * experts))
    width = w_gate.shape[1]
    assigns = tok_rows * top
    tile = 128
    flat_ids = expert_ids.reshape(assigns)
    flat_probs = gate_probs.reshape(assigns)
    expert_range = jnp.arange(experts, dtype=jnp.int32)
    holds = (slot_expert[None, :] == expert_range[:, None]).astype(jnp.int32)
    first_slot = jnp.argmax(holds, axis=1)
    last_slot = slots - 1 - jnp.argmax(holds[:, ::-1], axis=1)
    picks = (flat_ids[:, None] == expert_range[None, :]).astype(jnp.int32)
    before = jnp.cumsum(picks, axis=0) - picks
    rank = jnp.sum(before * picks, axis=1)
    slot_one = jnp.sum(picks * first_slot[None, :], axis=1)
    slot_two = jnp.sum(picks * last_slot[None, :], axis=1)
    paired = slot_one != slot_two
    shifted = rank + here % 2
    target = jnp.where(paired & (shifted % 2 == 1), slot_two, slot_one)
    place = jnp.where(paired, shifted // 2, rank)
    flat_pos = target * capacity + place
    total = slots * capacity
    source_row = (
        jnp.full((total,), tok_rows, jnp.int32)
        .at[flat_pos]
        .set(jnp.arange(assigns, dtype=jnp.int32) // top)
    )
    send_probs = (
        jnp.zeros((total,), jnp.bfloat16).at[flat_pos].set(flat_probs).reshape(slots, capacity)
    )

    def pack(rows):
        padded = jnp.concatenate([rows, jnp.zeros((1, rows.shape[1]), rows.dtype)], axis=0)
        return padded[source_row].reshape(slots, capacity, rows.shape[1])

    part_x, part_dy, recv_p = (
        lax.all_to_all(pack(tokens), "expert", split_axis=0, concat_axis=0, tiled=True),
        lax.all_to_all(pack(cotangent), "expert", split_axis=0, concat_axis=0, tiled=True),
        lax.all_to_all(send_probs, "expert", split_axis=0, concat_axis=0, tiled=True),
    )
    recv_x, recv_dy = (
        lax.all_gather(part_x, "dp", axis=2, tiled=True),
        lax.all_gather(part_dy, "dp", axis=2, tiled=True),
    )
    padded_total = (total + tile - 1) // tile * tile
    rows_x = recv_x.reshape(total, width)
    rows_dy = recv_dy.reshape(total, width)
    rows_p = recv_p.reshape(total)
    wg = w_gate[0]
    wu = w_up[0]
    wd = w_down[0]
    share = wg.shape[1]
    extra = padded_total - total
    work_x = jnp.concatenate([rows_x, jnp.zeros((extra, width), rows_x.dtype)], axis=0)
    work_dy = jnp.concatenate([rows_dy, jnp.zeros((extra, width), rows_dy.dtype)], axis=0)
    work_p = jnp.concatenate([rows_p, jnp.zeros((extra,), rows_p.dtype)], axis=0)
    tiles = padded_total // tile

    def tile_step(index, carry):
        acc_gate, acc_up, acc_down, pieces, scores = carry
        start = index * tile
        xs = lax.dynamic_slice_in_dim(work_x, start, tile, 0)
        dys = lax.dynamic_slice_in_dim(work_dy, start, tile, 0)
        probs = lax.dynamic_slice_in_dim(work_p, start, tile, 0)
        gate = jnp.dot(xs, wg, preferred_element_type=jnp.float32)
        up = jnp.dot(xs, wu, preferred_element_type=jnp.float32)
        act, slope = silu_parts(gate)
        hidden = (act * up).astype(jnp.bfloat16)
        out = jnp.dot(hidden, wd, preferred_element_type=jnp.float32)
        score = jnp.sum(dys.astype(jnp.float32) * out, axis=1)
        d_out = (probs.astype(jnp.float32)[:, None] * dys.astype(jnp.float32)).astype(jnp.bfloat16)
        d_hidden = contract(d_out, wd, 1, 1)
        d_gate_pre = (d_hidden * up * slope).astype(jnp.bfloat16)
        d_up_pre = (d_hidden * act).astype(jnp.bfloat16)
        acc_down = acc_down + contract(hidden, d_out, 0, 0)
        acc_gate = acc_gate + contract(xs, d_gate_pre, 0, 0)
        acc_up = acc_up + contract(xs, d_up_pre, 0, 0)
        piece = contract(d_gate_pre, wg, 1, 1) + contract(d_up_pre, wu, 1, 1)
        pieces = lax.dynamic_update_slice_in_dim(pieces, piece.astype(jnp.bfloat16), start, 0)
        scores = lax.dynamic_update_slice_in_dim(scores, score, start, 0)
        return (acc_gate, acc_up, acc_down, pieces, scores)

    init = (
        jnp.zeros((width, share), jnp.float32),
        jnp.zeros((width, share), jnp.float32),
        jnp.zeros((share, width), jnp.float32),
        jnp.zeros((padded_total, width), jnp.bfloat16),
        jnp.zeros((padded_total,), jnp.float32),
    )
    acc_gate, acc_up, acc_down, pieces, scores = lax.fori_loop(0, tiles, tile_step, init)
    row_pieces = pieces[:total]
    row_scores = scores[:total]
    summed = lax.psum_scatter(
        row_pieces.reshape(slots, capacity, width), "dp", scatter_dimension=2, tiled=True
    ).astype(jnp.float32)
    total_scores = lax.psum(row_scores.reshape(slots, capacity), "dp")
    back_x, back_s = (
        lax.all_to_all(
            summed.astype(jnp.bfloat16), "expert", split_axis=0, concat_axis=0, tiled=True
        ).astype(summed.dtype),
        lax.all_to_all(
            total_scores.astype(jnp.bfloat16), "expert", split_axis=0, concat_axis=0, tiled=True
        ).astype(total_scores.dtype),
    )
    per_assign = back_x.reshape(total, quarter)[flat_pos].reshape(tok_rows, top, quarter)
    d_tokens = jnp.sum(per_assign, axis=1).astype(jnp.bfloat16)
    d_probs = back_s.reshape(total)[flat_pos].reshape(tok_rows, top)
    partner = jnp.bitwise_xor(here, 1)
    same = slot_expert[here] == slot_expert[partner]
    got_gate, got_up, got_down = (
        partner_2(acc_gate.astype(jnp.bfloat16), "expert", 0).astype(acc_gate.dtype),
        partner_2(acc_up.astype(jnp.bfloat16), "expert", 0).astype(acc_up.dtype),
        partner_2(acc_down.astype(jnp.bfloat16), "expert", 0).astype(acc_down.dtype),
    )
    grad_gate = (acc_gate + jnp.where(same, got_gate, 0.0)).astype(jnp.bfloat16)[None]
    grad_up = (acc_up + jnp.where(same, got_up, 0.0)).astype(jnp.bfloat16)[None]
    grad_down = (acc_down + jnp.where(same, got_down, 0.0)).astype(jnp.bfloat16)[None]
    return (d_tokens, d_probs, grad_gate, grad_up, grad_down)


def solution(mesh):
    placed = (
        P("expert", "dp"),
        P("expert", "dp"),
        P("expert", None),
        P("expert", None),
        P(),
        P("expert", None, "dp"),
        P("expert", None, "dp"),
        P("expert", "dp", None),
    )
    return jax.shard_map(
        shards,
        mesh=mesh,
        in_specs=placed,
        out_specs=(
            P("expert", "dp"),
            P("expert", None),
            P("expert", None, "dp"),
            P("expert", None, "dp"),
            P("expert", "dp", None),
        ),
        check_vma=False,
    )
```

profile of v0, /device:TPU:1, one launch (start us, length us, event | category | flops | bytes accessed | tf_op | source)
XLA Modules:
  0.0 708.7 jit_solution(14952302323026890420)
XLA Ops:
  19.6 58.3 %all_to_all.34 = bf16[64,11,896]{2,1,0:T(8,128)(2,1)} all-to-all(bf16[64,11,896]{2,1,0:T(8,128)(2,1)S(1)} %reshape.193), channel_id=1, replica_groups=mesh['dp'=4,'expert'=64] {'expert'}, dimensions={0} | all-to-all | bytes 2523136 | tf_op jit(solution)/shard_map/all_to_all | solution.py:64
  81.6 51.4 %all_to_all.35 = bf16[64,11,896]{2,1,0:T(8,128)(2,1)} all-to-all(bf16[64,11,896]{2,1,0:T(8,128)(2,1)S(1)} %reshape.189), channel_id=1, replica_groups=mesh['dp'=4,'expert'=64] {'expert'}, dimensions={0} | all-to-all | bytes 2523136 | tf_op jit(solution)/shard_map/all_to_all | solution.py:63
  133.3 3.8 scatter_custom_fusion.1
  137.9 6.1 all-to-all-start.1
  144.2 9.0 %all-to-all-done.1 = bf16[64,1,11]{2,1,0:T(2,128)(2,1)S(1)} async-done(((bf16[64,1,11]{2,1,0:T(2,128)(2,1)}), bf16[64,1,11]{2,1,0:T(2,128)(2,1)S(1)}, u32[]{:S(2)}, u32[]{:S(2)}) %all-to-all-start.1) | async-done | bytes 1440 | tf_op jit(solution)/shard_map/all_to_all | solution.py:65
  153.5 8.3 %reshape.194 = bf16[704,3584]{1,0:T(8,128)(2,1)} reshape(bf16[64,11,3584]{2,1,0:T(8,128)(2,1)} %all-gather.5.cloned.1.call-done) | data formatting | bytes 10092544 | tf_op jit(solution)/shard_map/reshape | solution.py:73
  161.8 5.2 concatenate.19
  167.0 64.7 %all-gather.3.cloned.1.call-done = bf16[64,11,3584]{2,1,0:T(8,128)(2,1)} async-done(((bf16[64,11,896]{2,1,0:T(8,128)(2,1)}), bf16[64,11,3584]{2,1,0:T(8,128)(2,1)}) %all-gather.3.cloned.1.call-update) | async-done | bytes 5046288 | tf_op jit(solution)/shard_map/all_gather | solution.py:68
  231.6 8.2 %reshape.190 = bf16[704,3584]{1,0:T(8,128)(2,1)} reshape(bf16[64,11,3584]{2,1,0:T(8,128)(2,1)} %all-gather.3.cloned.1.call-done) | data formatting | bytes 10092544 | tf_op jit(solution)/shard_map/reshape | solution.py:72
  239.8 5.2 concatenate.16
  247.7 131.0 %while.22 = (s32[]{:T(128)}, f32[3584,256]{1,0:T(8,128)}, f32[3584,256]{1,0:T(8,128)}, f32[256,3584]{1,0:T(8,128)}, bf16[768,3584]{1,0:T(8,128)(2,1)}, /*index=5...) while((s32[]{:T(128)}, f32[3584,256]{1,0:T(8,128)}, ...), condition=%wide.region_11.12_spmd.clone, body=%wide.region_9.11_spmd.clone.sunk | while | flops 2124972032 | bytes 155258640 | solution.py:116
  378.7 5.0 slice.14
  383.6 8.0 %reshape.195 = bf16[64,11,3584]{2,1,0:T(8,128)(2,1)} reshape(bf16[704,3584]{1,0:T(8,128)(2,1)} %slice.14) | data formatting | bytes 10092544 | tf_op jit(solution)/shard_map/reshape | solution.py:120
  391.7 50.7 %copy.32 = bf16[64,11,3584]{1,0,2:T(8,128)(2,1)} copy(bf16[64,11,3584]{2,1,0:T(8,128)(2,1)} %reshape.195) | data formatting | bytes 10092544
  442.4 78.6 %reshape.254 = bf16[3584,704]{1,0:T(8,128)(2,1)} reshape(bf16[3584,64,11]{2,1,0:T(8,128)(2,1)} %bitcast.77) | data formatting | bytes 10092544
  521.0 3.6 convert_element_type.116
  526.8 12.8 %psum.7 = bf16[64,11]{1,0:T(8,128)(2,1)S(1)} all-reduce(f32[64,11]{1,0:T(8,128)S(1)} %reshape.199), channel_id=1, replica_groups=mesh['dp'=4,'expert'=64] {'dp'}, use_global_device_ids=true, to_apply=%region_14.15 | all-reduce | flops 704 | bytes 4224 | tf_op jit(solution)/shard_map/psum | solution.py:122
  540.3 13.8 %all-to-all-start.4 = ((bf16[64,1,11]{2,1,0:T(2,128)(2,1)}), bf16[64,1,11]{2,1,0:T(2,128)(2,1)S(1)}, u32[]{:S(2)}, u32[]{:S(2)}) async-start(bf16[64,1,11]{2,1,0:T(2,128)(2,1)} %copy.30), calls=%async_computation.4 | async-start | bytes 65536 | tf_op jit(solution)/shard_map/all_to_all | solution.py:127
  566.6 15.7 %reduce-scatter.4.cloned.1.call-done = bf16[896,704]{1,0:T(8,128)(2,1)} async-done(((bf16[3584,704]{1,0:T(8,128)(2,1)}), bf16[896,704]{1,0:T(8,128)(2,1)}) %reduce-scatter.4.cloned.1.call-update) | async-done | bytes 1261584
  582.3 35.3 %reshape.255 = bf16[896,64,11]{2,1,0:T(8,128)(2,1)} reshape(bf16[896,704]{1,0:T(8,128)(2,1)} %reduce-scatter.4.cloned.1.call-done) | data formatting | bytes 2523136
  617.6 19.6 %copy.33 = bf16[64,11,896]{2,1,0:T(8,128)(2,1)} copy(bf16[64,11,896]{1,0,2:T(8,128)(2,1)} %bitcast.80) | data formatting | bytes 2523136
  637.3 10.8 %all-to-all-start.3 = ((bf16[64,11,896]{2,1,0:T(8,128)(2,1)}), bf16[64,11,896]{2,1,0:T(8,128)(2,1)}, u32[]{:S(2)}, u32[]{:S(2)}) async-start(bf16[64,11,896]{2,1,0:T(8,128)(2,1)} %copy.33), calls=%async_computation.3 | async-start | bytes 3670016 | tf_op jit(solution)/shard_map/all_to_all | solution.py:124
  648.0 4.4 fusion.22
  658.3 35.1 %all-to-all-done.3 = bf16[64,11,896]{2,1,0:T(8,128)(2,1)} async-done(((bf16[64,11,896]{2,1,0:T(8,128)(2,1)}), bf16[64,11,896]{2,1,0:T(8,128)(2,1)}, u32[]{:S(2)}, u32[]{:S(2)}) %all-to-all-start.3) | async-done | bytes 1261600 | tf_op jit(solution)/shard_map/all_to_all | solution.py:124
  (255 shorter events, 179.1 us)
Async XLA Ops:
  7.2 146.3 %all-gather.5.cloned.1.call-start = ((), (), s32[]{:S(2)}) async-start(), calls=%async_computation.7 | async-start | bytes 9175040 | tf_op jit(solution)/shard_map/all_gather | solution.py:69
  19.1 58.9 %copy-start.13 = (bf16[128,896]{1,0:T(8,128)(2,1)S(1)}, bf16[128,896]{1,0:T(8,128)(2,1)}, u32[]{:S(2)}) copy-start(bf16[128,896]{1,0:T(8,128)(2,1)} %param.10) | copy-start | bytes 688132
  77.9 153.7 %all-gather.3.cloned.1.call-start = ((), (), s32[]{:S(2)}) async-start(), calls=%async_computation.6 | async-start | bytes 9175040 | tf_op jit(solution)/shard_map/all_gather | solution.py:68
  81.1 51.9 %copy-start.15 = (bf16[128,4]{0,1:T(4,128)(2,1)S(1)}, bf16[128,4]{0,1:T(4,128)(2,1)}, u32[]{:S(2)}) copy-start(bf16[128,4]{0,1:T(4,128)(2,1)} %param.13) | copy-start | bytes 3076
  137.9 15.3 %all-to-all-start.1 = ((bf16[64,1,11]{2,1,0:T(2,128)(2,1)}), bf16[64,1,11]{2,1,0:T(2,128)(2,1)S(1)}, u32[]{:S(2)}, u32[]{:S(2)}) async-start(bf16[64,1,11]{2,1,0:T(2,128)(2,1)} %all_to_all.28), calls=%async_computation.1 | async-start | bytes 65536 | tf_op jit(solution)/shard_map/all_to_all | solution.py:65
  144.0 438.4 %reduce-scatter.4.cloned.1.call-start = ((), (), s32[]{:S(2)}) async-start(), calls=%async_computation.8 | async-start | bytes 6881280
  247.7 4.5 copy-start.11
  260.4 3.6 copy-start.4
  269.6 4.5 copy-start.11
  282.3 3.6 copy-start.4
  291.4 4.5 copy-start.11
  304.1 3.6 copy-start.4
  313.2 4.5 copy-start.11
  325.9 3.6 copy-start.4
  335.0 4.5 copy-start.11
  356.8 4.5 copy-start.11
  521.0 4.3 copy-start.6
  524.6 29.5 %copy-start.14 = (s32[64]{0:T(128)S(1)}, s32[64]{0:T(128)}, u32[]{:S(2)}) copy-start(s32[64]{0:T(128)} %param.14) | copy-start | bytes 772
  524.6 123.4 %collective-permute-start.2 = (bf16[256,3584]{1,0:T(8,128)(2,1)}, bf16[256,3584]{1,0:T(8,128)(2,1)}, u32[]{:S(2)}, u32[]{:S(2)}) collective-permute-start(bf16[256,3584]{1,0:T(8,128)(2,1)} %convert_element_type.116), channel_id=1, source_target_pairs={{0,1},{1,0},{2,3},{3,2},{4,5},{5,4},{6,7},{7,6},{8,9},{9,8},{10,11... | collective-permute-start | bytes 5505032 | tf_op jit(solution)/shard_map/ppermute | solution.py:8
  526.7 125.8 %collective-permute-start.1 = (bf16[3584,256]{1,0:T(8,128)(2,1)}, bf16[3584,256]{1,0:T(8,128)(2,1)S(1)}, u32[]{:S(2)}, u32[]{:S(2)}) collective-permute-start(bf16[3584,256]{1,0:T(8,128)(2,1)} %convert_element_type.113), channel_id=1, source_target_pairs={{0,1},{1,0},{2,3},{3,2},{4,5},{5,4},{6,7},{7,6},{8,9},{9,8},{10,11... | collective-permute-start | bytes 5505032 | tf_op jit(solution)/shard_map/ppermute | solution.py:8
  540.3 23.0 %all-to-all-start.4 = ((bf16[64,1,11]{2,1,0:T(2,128)(2,1)}), bf16[64,1,11]{2,1,0:T(2,128)(2,1)S(1)}, u32[]{:S(2)}, u32[]{:S(2)}) async-start(bf16[64,1,11]{2,1,0:T(2,128)(2,1)} %copy.30), calls=%async_computation.4 | async-start | bytes 65536 | tf_op jit(solution)/shard_map/all_to_all | solution.py:127
  559.5 94.7 %collective-permute-start = (bf16[3584,256]{1,0:T(8,128)(2,1)}, bf16[3584,256]{1,0:T(8,128)(2,1)}, u32[]{:S(2)}, u32[]{:S(2)}) collective-permute-start(bf16[3584,256]{1,0:T(8,128)(2,1)} %convert_element_type.110), channel_id=1, source_target_pairs={{0,1},{1,0},{2,3},{3,2},{4,5},{5,4},{6,7},{7,6},{8,9},{9,8},{10,11... | collective-permute-start | bytes 5505032 | tf_op jit(solution)/shard_map/ppermute | solution.py:8
  637.3 56.1 %all-to-all-start.3 = ((bf16[64,11,896]{2,1,0:T(8,128)(2,1)}), bf16[64,11,896]{2,1,0:T(8,128)(2,1)}, u32[]{:S(2)}, u32[]{:S(2)}) async-start(bf16[64,11,896]{2,1,0:T(8,128)(2,1)} %copy.33), calls=%async_computation.3 | async-start | bytes 3670016 | tf_op jit(solution)/shard_map/all_to_all | solution.py:124
  648.0 4.4 copy-start.7
  (46 other events, 133.6 us)
Sparse Core Ops, SparseCore 0:
  78.1 73.8 all-gather.4
  153.8 77.7 all-gather.2
  521.1 61.1 reduce-scatter.3
where the time goes:
time: 713 us; the launch traced here: 709 us
  local copies, waits for them, and re-layouts  267 us (37%)
  waiting for transfers between devices  128 us (18%)
  blocking collectives  122 us (17%)
  matrix products  118 us (17%)
  starting transfers between devices  32.1 us (5%)
  other arithmetic  24.4 us (3%)
  between operations  15.4 us (2%)
    unnamed x21, local copies, waits for them, and re-layouts  187 us
    dot_general x36, matrix products, contract(): lax.dot_general(left, right, (((left_dim,), (right_dim,)), ((), ())), pre...  88.4 us
    all_gather x1, waiting for transfers between devices, shards(): lax.all_gather(part_x, 'dp', axis=2, tiled=True)  64.7 us
    all_to_all x1, blocking collectives, shards(): lax.all_to_all(pack(cotangent), 'expert', split_axis=0, concat_axis=0, ti...  58.3 us
    all_to_all x1, blocking collectives, shards(): lax.all_to_all(pack(tokens), 'expert', split_axis=0, concat_axis=0, tiled...  51.4 us
    all_to_all x1, waiting for transfers between devices, shards(): lax.all_to_all(summed.astype(jnp.bfloat16), 'expert', split_axis=0, conca...  35.1 us
    unnamed x4, waiting for transfers between devices  15.8 us
  transfers between devices with their start and end apart: 9, of which 5 were waited for; matrix products, arithmetic and copies ran while one was open for 14% of the time, Pallas kernels for 0%

commit v1 on v0

v1 whole, which is shorter than its diff:
```python
import functools

import jax
import jax.numpy as jnp
from jax import lax
from jax.experimental import pallas as pl
from jax.experimental.pallas import tpu as pltpu
from jax.sharding import PartitionSpec as P

F32 = jnp.float32
BF16 = jnp.bfloat16
SLOTS = 64
CAP = 11
BLOCK = 12
TOK = 128
ROWS = SLOTS * CAP
HALF = ROWS // 2
PADDED = SLOTS * BLOCK
QUARTER = 896
WIDTH = 3584
SHARE = 256
N_DP = 4
TILE = 176
TILES = ROWS // TILE
VMEM = pltpu.VMEM


def iota(shape, dim):
    return lax.broadcasted_iota(jnp.int32, shape, dim)


def dot(left, right, left_dim=1, right_dim=0, precision=None):
    return lax.dot_general(
        left, right, (((left_dim,), (right_dim,)), ((), ())),
        precision=precision, preferred_element_type=F32,
    )


def params(mib):
    return pltpu.CompilerParams(vmem_limit_bytes=mib << 20)


def pack_kernel(parity_ref, slot_ref, ids_ref, probs_ref, tok_ref, cot_ref, x_ref, d_ref, code_ref, pick_ref):
    slot = slot_ref[...]
    index = iota((SLOTS, TOK), 0)
    second = (index & 1).astype(F32)
    partner = jnp.where(second > 0, pltpu.roll(slot, 1, 0), pltpu.roll(slot, SLOTS - 1, 0))
    paired = slot == partner
    ids = ids_ref[...].astype(F32)
    probs = probs_ref[...].astype(F32)
    chosen = jnp.zeros((SLOTS, TOK), F32)
    weight = jnp.zeros((SLOTS, TOK), F32)
    for k in range(4):
        here = slot == ids[k:k + 1, :]
        chosen = chosen + jnp.where(here, 1.0, 0.0)
        weight = weight + jnp.where(here, probs[k:k + 1, :], 0.0)
    earlier = jnp.where(iota((TOK, TOK), 0) < iota((TOK, TOK), 1), 1.0, 0.0).astype(BF16)
    rank = dot(chosen.astype(BF16), earlier)
    shifted = rank + parity_ref[0].astype(F32)
    half = jnp.floor(shifted * 0.5)
    taken = jnp.where(paired, jnp.where(shifted - 2.0 * half == second, 1.0, 0.0), 1.0) * chosen
    place = jnp.where(paired, half, rank)
    code = jnp.where(taken > 0, place + 1.0, 0.0)
    code_ref[...] = code
    row, col = iota((PADDED, SLOTS), 0), iota((PADDED, SLOTS), 1) * BLOCK
    spread = jnp.where(row >= col, jnp.where(row < col + BLOCK, 1.0, 0.0), 0.0).astype(BF16)
    number = iota((PADDED, TOK), 0).astype(F32)
    within = number - BLOCK * jnp.floor((number + 0.5) * (1.0 / BLOCK)) + 1.0
    pick = jnp.where(dot(spread, code.astype(BF16)) == within, 1.0, 0.0)
    scaled = pick * dot(spread, weight.astype(BF16))
    pick = pick.astype(BF16)
    pick_ref[...] = pick
    x_ref[...] = dot(pick, tok_ref[...]).astype(BF16)
    d_ref[...] = dot(scaled.astype(BF16), cot_ref[...]).astype(BF16)


def pack(parity, slot, ids, probs, tokens, cotangent):
    whole = pl.BlockSpec(memory_space=VMEM)
    return pl.pallas_call(
        pack_kernel,
        out_shape=(
            jax.ShapeDtypeStruct((PADDED, QUARTER), BF16),
            jax.ShapeDtypeStruct((PADDED, QUARTER), BF16),
            jax.ShapeDtypeStruct((SLOTS, TOK), F32),
            jax.ShapeDtypeStruct((PADDED, TOK), BF16),
        ),
        in_specs=[pl.BlockSpec(memory_space=pltpu.SMEM)] + [whole] * 5,
        out_specs=(whole,) * 4,
        compiler_params=params(24),
        cost_estimate=pl.CostEstimate(flops=400_000_000, bytes_accessed=4_000_000, transcendentals=0),
    )(parity, slot, ids, probs, tokens, cotangent)


def combine_kernel(slot_ref, ids_ref, probs_ref, code_ref, pick_ref, back_ref, dtok_ref, dprob_ref):
    dtok_ref[...] = dot(pick_ref[...], back_ref[...], 0, 0).astype(BF16)
    chosen = jnp.where(
        iota((SLOTS, PADDED), 1) == iota((SLOTS, PADDED), 0) * BLOCK + CAP, 1.0, 0.0
    ).astype(BF16)
    scores = dot(chosen, back_ref[:, 0:TOK]) + dot(chosen, back_ref[:, TOK:2 * TOK])
    code = code_ref[...]
    placed = jnp.zeros((SLOTS, TOK), F32)
    for r in range(CAP):
        placed = placed + jnp.where(code == r + 1.0, scores[:, r:r + 1], 0.0)
    ids = ids_ref[...].astype(F32)
    probs = probs_ref[...].astype(F32)
    slot = slot_ref[...]
    found = [
        jnp.sum(jnp.where(slot == ids[k:k + 1, :], placed, 0.0), axis=0, keepdims=True)
        for k in range(4)
    ]
    dprob_ref[...] = jnp.concatenate(found, axis=0) / probs


def combine(slot, ids, probs, code, pick, back):
    whole = pl.BlockSpec(memory_space=VMEM)
    return pl.pallas_call(
        combine_kernel,
        out_shape=(
            jax.ShapeDtypeStruct((TOK, QUARTER), BF16),
            jax.ShapeDtypeStruct((4, TOK), F32),
        ),
        in_specs=[whole] * 6,
        out_specs=(whole,) * 2,
        compiler_params=params(24),
        cost_estimate=pl.CostEstimate(flops=200_000_000, bytes_accessed=2_000_000, transcendentals=0),
    )(slot, ids, probs, code, pick, back)


def part_specs():
    full = pl.BlockSpec((TILE, QUARTER), lambda m, at: (m, 0))
    low = pl.BlockSpec((TILE, QUARTER), lambda m, at: (jnp.minimum(m, TILES // 2 - 1), 0))
    high = pl.BlockSpec((TILE, QUARTER), lambda m, at: (jnp.maximum(m - TILES // 2, 0), 0))
    return [full, full, full, low, high]


def offset(at_ref, rel):
    return pl.multiple_of(lax.rem(at_ref[0] + rel, N_DP) * QUARTER, 128)


RELS = (0, 3, 1, 2)


def forward_kernel(at_ref, own, below, above, low, high, wg_ref, wu_ref, hid_ref, act_ref, ups_ref):
    m = pl.program_id(0)
    far = jnp.where(m < TILES // 2, low[...], high[...])
    gate = jnp.zeros((TILE, SHARE), F32)
    up = jnp.zeros((TILE, SHARE), F32)
    for rel, part in zip(RELS, (own[...], below[...], above[...], far)):
        where = pl.ds(offset(at_ref, rel), QUARTER)
        gate = gate + dot(part, wg_ref[where, :])
        up = up + dot(part, wu_ref[where, :])
    sig = jax.nn.sigmoid(gate)
    act = gate * sig
    hid_ref[...] = (act * up).astype(BF16)
    act_ref[...] = act
    ups_ref[...] = up * (sig * (1.0 + gate * (1.0 - sig)))


def forward(at, parts, wg, wu):
    tile = pl.BlockSpec((TILE, SHARE), lambda m, at: (m, 0))
    whole = pl.BlockSpec((WIDTH, SHARE), lambda m, at: (0, 0))
    return pl.pallas_call(
        forward_kernel,
        out_shape=(
            jax.ShapeDtypeStruct((ROWS, SHARE), BF16),
            jax.ShapeDtypeStruct((ROWS, SHARE), F32),
            jax.ShapeDtypeStruct((ROWS, SHARE), F32),
        ),
        grid_spec=pltpu.PrefetchScalarGridSpec(
            num_scalar_prefetch=1, grid=(TILES,),
            in_specs=part_specs() + [whole, whole], out_specs=(tile,) * 3,
        ),
        compiler_params=params(32),
        cost_estimate=pl.CostEstimate(
            flops=4 * ROWS * WIDTH * SHARE, bytes_accessed=11_000_000, transcendentals=ROWS * SHARE
        ),
    )(at, *parts, wg, wu)


def backward_kernel(at_ref, own, below, above, low, high, wd_ref, hid_ref, act_ref, ups_ref, dg_ref, du_ref, score_ref):
    m = pl.program_id(0)
    far = jnp.where(m < TILES // 2, low[...], high[...])
    d_hidden = jnp.zeros((TILE, SHARE), F32)
    for rel, part in zip(RELS, (own[...], below[...], above[...], far)):
        d_hidden = d_hidden + dot(part, wd_ref[:, pl.ds(offset(at_ref, rel), QUARTER)], 1, 1)
    dg_ref[...] = (d_hidden * ups_ref[...]).astype(BF16)
    du_ref[...] = (d_hidden * act_ref[...]).astype(BF16)
    score = jnp.sum(hid_ref[...].astype(F32) * d_hidden, axis=1, keepdims=True)
    slots = TILE // CAP
    number = iota((TILE, TOK), 0).astype(F32)
    within = number - CAP * jnp.floor((number + 0.5) * (1.0 / CAP))
    lanes = jnp.where(iota((TILE, TOK), 1).astype(F32) == within, score, 0.0)
    row, col = iota((slots, TILE), 0) * CAP, iota((slots, TILE), 1)
    group = jnp.where(col >= row, jnp.where(col < row + CAP, 1.0, 0.0), 0.0)
    score_ref[...] = dot(group, lanes, precision=lax.Precision.HIGHEST)


def backward(at, parts, wd, hid, act, ups):
    tile = pl.BlockSpec((TILE, SHARE), lambda m, at: (m, 0))
    whole = pl.BlockSpec((SHARE, WIDTH), lambda m, at: (0, 0))
    return pl.pallas_call(
        backward_kernel,
        out_shape=(
            jax.ShapeDtypeStruct((ROWS, SHARE), BF16),
            jax.ShapeDtypeStruct((ROWS, SHARE), BF16),
            jax.ShapeDtypeStruct((SLOTS, TOK), F32),
        ),
        grid_spec=pltpu.PrefetchScalarGridSpec(
            num_scalar_prefetch=1, grid=(TILES,),
            in_specs=part_specs() + [whole, tile, tile, tile],
            out_specs=(tile, tile, pl.BlockSpec((TILE // CAP, TOK), lambda m, at: (m, 0))),
        ),
        compiler_params=params(32),
        cost_estimate=pl.CostEstimate(
            flops=2 * ROWS * WIDTH * SHARE, bytes_accessed=9_000_000, transcendentals=0
        ),
    )(at, *parts, wd, hid, act, ups)


def piece_kernel(n_add, at_ref, dg_ref, du_ref, wg_ref, wu_ref, *refs):
    out_ref = refs[-1]
    total = dot(dg_ref[...], wg_ref[...], 1, 1) + dot(du_ref[...], wu_ref[...], 1, 1)
    for ref in refs[:n_add]:
        total = total + ref[...].astype(F32)
    out_ref[...] = total.astype(BF16)


def piece(at, rel, first, rows, dg, du, wg, wu, adds=()):
    start = first // TILE
    tile = pl.BlockSpec((TILE, SHARE), lambda m, at: (m + start, 0))
    weight = pl.BlockSpec((QUARTER, SHARE), lambda m, at: (lax.rem(at[0] + rel, N_DP), 0))
    out = pl.BlockSpec((TILE, QUARTER), lambda m, at: (m, 0))
    return pl.pallas_call(
        functools.partial(piece_kernel, len(adds)),
        out_shape=jax.ShapeDtypeStruct((rows, QUARTER), BF16),
        grid_spec=pltpu.PrefetchScalarGridSpec(
            num_scalar_prefetch=1, grid=(rows // TILE,),
            in_specs=[tile, tile, weight, weight] + [out] * len(adds), out_specs=out,
        ),
        compiler_params=params(24),
        cost_estimate=pl.CostEstimate(
            flops=4 * rows * QUARTER * SHARE, bytes_accessed=3_000_000, transcendentals=0
        ),
    )(at, dg, du, wg, wu, *adds)


def grads_kernel(at_ref, x0, x1, x2, x3, x4, d0, d1, d2, d3, d4, dg_ref, du_ref, hid_ref, gg_ref, gu_ref, gd_ref):
    dg, du, hid = dg_ref[...], du_ref[...], hid_ref[...]
    step = 128

    def rows_of(parts, cols):
        if len(parts) == 1:
            return parts[0][:, cols]
        return jnp.concatenate([parts[0][:, cols], parts[1][:, cols]], axis=0)

    for rel, xs, ds in zip(RELS, ((x0,), (x1,), (x2,), (x3, x4)), ((d0,), (d1,), (d2,), (d3, d4))):
        base = offset(at_ref, rel)

        def body(c, _, xs=xs, ds=ds, base=base):
            cols = pl.ds(pl.multiple_of(c * step, step), step)
            to = pl.ds(pl.multiple_of(base + c * step, step), step)
            x = rows_of(xs, cols)
            gg_ref[to, :] = dot(x, dg, 0, 0).astype(BF16)
            gu_ref[to, :] = dot(x, du, 0, 0).astype(BF16)
            gd_ref[:, to] = dot(hid, rows_of(ds, cols), 0, 0).astype(BF16)
            return 0

        lax.fori_loop(0, QUARTER // step, body, 0)


def grads(at, xs, ds, dg, du, hid):
    whole = pl.BlockSpec(memory_space=VMEM)
    return pl.pallas_call(
        grads_kernel,
        out_shape=(
            jax.ShapeDtypeStruct((WIDTH, SHARE), BF16),
            jax.ShapeDtypeStruct((WIDTH, SHARE), BF16),
            jax.ShapeDtypeStruct((SHARE, WIDTH), BF16),
        ),
        in_specs=[pl.BlockSpec(memory_space=pltpu.SMEM)] + [whole] * 13,
        out_specs=(whole,) * 3,
        compiler_params=params(32),
        cost_estimate=pl.CostEstimate(
            flops=6 * ROWS * WIDTH * SHARE, bytes_accessed=17_000_000, transcendentals=0
        ),
    )(at, *xs, *ds, dg, du, hid)


def shift(x, by):
    return lax.ppermute(x, "dp", [(i, (i + by) % N_DP) for i in range(N_DP)])


def swap(x):
    return lax.ppermute(x, "expert", [(i, i ^ 1) for i in range(SLOTS)])


def exchange(rows):
    return lax.all_to_all(
        rows.reshape(SLOTS, 3, 4, QUARTER), "expert", split_axis=0, concat_axis=0, tiled=True
    )


def received(rows):
    return rows.reshape(SLOTS, BLOCK, QUARTER)[:, :CAP].reshape(ROWS, QUARTER)


def gather(rows):
    below, above = shift(rows, 1), shift(rows, -1)
    low, high = shift(below[:HALF], 1), shift(above[HALF:], -1)
    return rows, below, above, low, high


def shards(tokens, cotangent, expert_ids, gate_probs, slot_expert, w_gate, w_up, w_down):
    here = lax.axis_index("expert")
    at = lax.axis_index("dp").reshape(1)
    parity = (here % 2).reshape(1)
    wg, wu, wd = w_gate[0], w_up[0], w_down[0]
    ids, probs = expert_ids.T, gate_probs.T
    slot = jnp.broadcast_to(slot_expert.astype(F32)[:, None], (SLOTS, TOK))
    x_rows, d_rows, code, pick = pack(parity, slot, ids, probs, tokens, cotangent)
    xs = gather(received(exchange(x_rows)))
    ds = gather(received(exchange(d_rows)))
    hid, act, ups = forward(at, xs, wg, wu)
    dg, du, score = backward(at, ds, wd, hid, act, ups)

    term = functools.partial(piece, at, dg=dg, du=du, wg=wg, wu=wu)
    far_up = shift(term(2, 0, HALF), 1)
    far_down = shift(term(2, HALF, HALF), -1)
    near_up = shift(term(1, HALF, HALF), 1)
    near_down = shift(term(3, 0, HALF), -1)
    last_up = shift(term(1, 0, HALF, adds=(far_up,)), 1)
    last_down = shift(term(3, HALF, HALF, adds=(far_down,)), -1)
    total = jnp.concatenate(
        [
            term(0, 0, HALF, adds=(near_down, last_up)),
            term(0, HALF, HALF, adds=(near_up, last_down)),
        ],
        axis=0,
    )
    score = (score + shift(score, 2)) + (shift(score, 1) + shift(score, -1))
    high = lax.reduce_precision(score, 8, 7)
    tail = jnp.concatenate(
        [high, score - high, jnp.zeros((SLOTS, QUARTER - 2 * TOK), F32)], axis=1
    ).astype(BF16)
    pay = jnp.concatenate([total.reshape(SLOTS, CAP, QUARTER), tail[:, None, :]], axis=1)
    back = exchange(pay).reshape(PADDED, QUARTER)
    d_tokens, d_probs = combine(slot, ids, probs, code, pick, back)

    gg, gu, gd = grads(at, xs, ds, dg, du, hid)
    same = slot_expert[here] == slot_expert[here ^ 1]

    def joined(own):
        other = swap(own)
        both = own.astype(F32) + other.astype(F32)
        return jnp.where(same, both, own.astype(F32)).astype(BF16)[None]

    return d_tokens, d_probs.T, joined(gg), joined(gu), joined(gd)


def solution(mesh):
    placed = (
        P("expert", "dp"),
        P("expert", "dp"),
        P("expert", None),
        P("expert", None),
        P(),
        P("expert", None, "dp"),
        P("expert", None, "dp"),
        P("expert", "dp", None),
    )
    return jax.shard_map(
        shards,
        mesh=mesh,
        in_specs=placed,
        out_specs=(
            P("expert", "dp"),
            P("expert", None),
            P("expert", None, "dp"),
            P("expert", None, "dp"),
            P("expert", "dp", None),
        ),
        check_vma=False,
    )
```

time: 713 us -> 301 us (0.42)
  local copies, waits for them, and re-layouts: 267 us -> 30.7 us
  blocking collectives: 122 us -> 0 us
  matrix products: 118 us -> 0 us
  Pallas kernels: 0 us -> 41.3 us
  starting transfers between devices: 32.1 us -> 59.1 us
  waiting for transfers between devices: 128 us -> 154 us
  between operations: 15.4 us -> 2.16 us
  other arithmetic: 24.4 us -> 12.7 us
    unnamed x21 -> x54, local copies, waits for them, and re-layouts: 187 us -> 9.96 us
    dot_general x54 -> x0, matrix products: 118 us -> none  [the longest x36 88.4 us: contract(): lax.dot_general(left, right, (((left_dim,), (right_dim,)), ((), ())), pre...]
    all_to_all x2 -> x0, blocking collectives: 110 us -> none  [the longest x1 58.3 us: shards(): lax.all_to_all(pack(cotangent), 'expert', split_axis=0, concat_axis=0, ti...]
    ppermute x3 -> x20, waiting for transfers between devices: 0.01 us -> 65.7 us  [the longest x17 65.7 us: shift(): return lax.ppermute(x, 'dp', [(i, (i + by) % N_DP) for i in range(N_DP)])]
    all_gather x2 -> x0, waiting for transfers between devices: 64.7 us -> none  [the longest x1 64.7 us: shards(): lax.all_gather(part_x, 'dp', axis=2, tiled=True)]
    pallas_call x0 -> x13, Pallas kernels: none -> 41.3 us  [the longest x1 15.4 us: grads(): pl.pallas_call(grads_kernel, out_shape=(jax.ShapeDtypeStruct((WIDTH, SHAR...]
    all_to_all x3, waiting for transfers between devices: 47.3 us -> 88.2 us  [exchange(): lax.all_to_all(rows.reshape(SLOTS, 3, 4, QUARTER), 'expert', split_axis=0...]
    ppermute x3 -> x20, starting transfers between devices: 1.19 us -> 30.3 us  [the longest x17 19.7 us: shift(): return lax.ppermute(x, 'dp', [(i, (i + by) % N_DP) for i in range(N_DP)])]
  transfers between devices with their start and end apart: 9 -> 23, of which waited for: 5 -> 9; matrix products, arithmetic and copies ran while one was open for 14% -> 10% of each run, Pallas kernels for 0% -> 6%
where the time goes in v1:
time: 301 us; the launch traced here: 300 us
  waiting for transfers between devices  154 us (51%)
  starting transfers between devices  59.1 us (20%)
  Pallas kernels  41.3 us (14%)
  local copies, waits for them, and re-layouts  30.7 us (10%)
  other arithmetic  12.7 us (4%)
    all_to_all x3, waiting for transfers between devices, exchange(): lax.all_to_all(rows.reshape(SLOTS, 3, 4, QUARTER), 'expert', split_axis=0...  88.2 us
    ppermute x17, waiting for transfers between devices, shift(): return lax.ppermute(x, 'dp', [(i, (i + by) % N_DP) for i in range(N_DP)])  65.7 us
    all_to_all x3, starting transfers between devices, exchange(): lax.all_to_all(rows.reshape(SLOTS, 3, 4, QUARTER), 'expert', split_axis=0...  28.8 us
    ppermute x17, starting transfers between devices, shift(): return lax.ppermute(x, 'dp', [(i, (i + by) % N_DP) for i in range(N_DP)])  19.7 us
    pallas_call x1, Pallas kernels, grads(): pl.pallas_call(grads_kernel, out_shape=(jax.ShapeDtypeStruct((WIDTH, SHAR...  15.4 us
    pallas_call x8, Pallas kernels, piece(): pl.pallas_call(functools.partial(piece_kernel, len(adds)), out_shape=jax....  12.4 us
    broadcast_in_dim x3, other arithmetic, joined(): return jnp.where(same, both, own.astype(F32)).astype(BF16)[None]  10.6 us
    ppermute x3, starting transfers between devices, swap(): return lax.ppermute(x, 'expert', [(i, i ^ 1) for i in range(SLOTS)])  10.5 us
  transfers between devices with their start and end apart: 23, of which 9 were waited for; matrix products, arithmetic and copies ran while one was open for 10% of the time, Pallas kernels for 6%

profile of v1, /device:TPU:1, one launch (start us, length us, event | category | flops | bytes accessed | tf_op | source)
XLA Modules:
  0.0 299.9 jit_solution(9194649580507214490)
XLA Ops:
  7.1 13.2 %all-to-all-start.1 = ((bf16[64,3,4,896]{3,2,1,0:T(4,128)(2,1)}), bf16[64,3,4,896]{3,2,1,0:T(4,128)(2,1)}, u32[]{:S(2)}, u32[]{:S(2)}) async-start(bf16[64,3,4,896]{3,2,1,0:T(4,128)(2,1)} %reshape.88), calls=%async_computation.1 | async-start | bytes 2752512 | tf_op jit(solution)/shard_map/all_to_all | solution.py:298
  21.5 34.3 %all-to-all-done.1 = bf16[64,3,4,896]{3,2,1,0:T(4,128)(2,1)} async-done(((bf16[64,3,4,896]{3,2,1,0:T(4,128)(2,1)}), bf16[64,3,4,896]{3,2,1,0:T(4,128)(2,1)}, u32[]{:S(2)}, u32[]{:S(2)}) %all-to-all-start.1) | async-done | bytes 1376288 | tf_op jit(solution)/shard_map/all_to_all | solution.py:298
  55.8 6.2 %all-to-all-start = ((bf16[64,3,4,896]{3,2,1,0:T(4,128)(2,1)}), bf16[64,3,4,896]{3,2,1,0:T(4,128)(2,1)S(1)}, u32[]{:S(2)}, u32[]{:S(2)}) async-start(bf16[64,3,4,896]{3,2,1,0:T(4,128)(2,1)} %reshape.85), calls=%async_computation | async-start | bytes 2752512 | tf_op jit(solution)/shard_map/all_to_all | solution.py:298
  68.4 29.1 %all-to-all-done = bf16[64,3,4,896]{3,2,1,0:T(4,128)(2,1)S(1)} async-done(((bf16[64,3,4,896]{3,2,1,0:T(4,128)(2,1)}), bf16[64,3,4,896]{3,2,1,0:T(4,128)(2,1)S(1)}, u32[]{:S(2)}, u32[]{:S(2)}) %all-to-all-start) | async-done | bytes 1376288 | tf_op jit(solution)/shard_map/all_to_all | solution.py:298
  99.8 2.5 reshape.87.own.d0
  109.2 2.5 collective-permute-start.7
  111.8 21.2 %collective-permute-done.below.d1 = bf16[704,896]{1,0:T(8,128)(2,1)S(1)} collective-permute-done((bf16[704,896]{1,0:T(8,128)(2,1)S(1)}, bf16[704,896]{1,0:T(8,128)(2,1)S(1)}, u32[]{:S(2)}, u32[]{:S(2)}) %collective-permute-start) | collective-permute-done | bytes 1261600 | tf_op jit(solution)/shard_map/ppermute | solution.py:290
  135.4 2.4 collective-permute-start.3
  137.8 8.7 %collective-permute-done.6.low.x3 = bf16[352,896]{1,0:T(8,128)(2,1)} collective-permute-done((bf16[352,896]{1,0:T(8,128)(2,1)}, bf16[352,896]{1,0:T(8,128)(2,1)}, u32[]{:S(2)}, u32[]{:S(2)}) %collective-permute-start.6) | collective-permute-done | bytes 630816 | tf_op jit(solution)/shard_map/ppermute | solution.py:290
  149.4 5.5 %shard_map.120 = (bf16[704,256]{1,0:T(8,128)(2,1)S(1)}, f32[704,256]{1,0:T(8,128)S(1)}, f32[704,256]{1,0:T(8,128)S(1)}) custom-call(s32[1]{0:T(128)} %bitcast.3.at_ref, bf16[704,896]{1,0:T(8,128)(2,1)} %reshape.90.own.x0, bf16[704,896]{1,0:T(8,128)(2,1)S(1)} %copy-done.16, bf16[704,896]{1,0:T(8,128)(2,1)} %collective-permute-done.5.above.x2, ...), custom_call_target="tpu_custom_call" | custom-call | flops 2583691264 | bytes 11000000 | tf_op jit(solution)/shard_map/pallas_call | solution.py:162
  154.9 5.2 %collective-permute-done.2.low.d3 = bf16[352,896]{1,0:T(8,128)(2,1)} collective-permute-done((bf16[352,896]{1,0:T(8,128)(2,1)}, bf16[352,896]{1,0:T(8,128)(2,1)}, u32[]{:S(2)}, u32[]{:S(2)}) %collective-permute-start.2) | collective-permute-done | bytes 630816 | tf_op jit(solution)/shard_map/ppermute | solution.py:290
  160.1 5.6 %shard_map.121 = (bf16[704,256]{1,0:T(8,128)(2,1)S(1)}, bf16[704,256]{1,0:T(8,128)(2,1)S(1)}, f32[64,128]{1,0:T(8,128)S(1)}) custom-call(s32[1]{0:T(128)} %bitcast.3.at_ref, bf16[704,896]{1,0:T(8,128)(2,1)S(1)} %copy-done.5, bf16[704,896]{1,0:T(8,128)(2,1)S(1)} %copy-done.7, bf16[704,896]{1,0:T(8,128)(2,1)S(1)} %copy-done.9, ...), custom_call_target="tpu_custom_call" | custom-call | flops 1291845632 | bytes 9000000 | tf_op jit(solution)/shard_map/pallas_call | solution.py:201
  165.7 15.4 %shard_map.131 = (bf16[3584,256]{1,0:T(8,128)(2,1)}, bf16[3584,256]{1,0:T(8,128)(2,1)S(1)}, bf16[256,3584]{1,0:T(8,128)(2,1)S(1)}) custom-call(s32[1]{0:T(128)} %bitcast.3.at_ref, bf16[704,896]{1,0:T(8,128)(2,1)} %reshape.90.own.x0, bf16[704,896]{1,0:T(8,128)(2,1)S(1)} %copy-done.17, bf16[704,896]{1,0:T(8,128)(2,1)} %collective-permute-done.5.above.x2, ...), custom_call_target="tpu_custom_call" | custom-call | flops 3875536896 | bytes 17000000 | tf_op jit(solution)/shard_map/pallas_call | solution.py:273
  182.9 2.7 collective-permute-start.12
  190.9 25.7 %collective-permute-done.15 = f32[64,128]{1,0:T(8,128)S(1)} collective-permute-done((f32[64,128]{1,0:T(8,128)S(1)}, f32[64,128]{1,0:T(8,128)S(1)}, u32[]{:S(2)}, u32[]{:S(2)}) %collective-permute-start.15) | collective-permute-done | bytes 32800 | tf_op jit(solution)/shard_map/ppermute | solution.py:290
  219.2 3.0 collective-permute-start.13
  228.3 3.5 %collective-permute-start.18 = (bf16[3584,256]{1,0:T(8,128)(2,1)}, bf16[3584,256]{1,0:T(8,128)(2,1)}, u32[]{:S(2)}, u32[]{:S(2)}) collective-permute-start(bf16[3584,256]{1,0:T(8,128)(2,1)} %copy-done.13), channel_id=1, source_target_pairs={{0,1},{1,0},{2,3},{3,2},{4,5},{5,4},{6,7},{7,6},{8,9},{9,8},{10,11... | collective-permute-start | bytes 5505032 | tf_op jit(solution)/shard_map/ppermute | solution.py:294
  233.8 6.2 %collective-permute-start.19 = (bf16[256,3584]{1,0:T(8,128)(2,1)}, bf16[256,3584]{1,0:T(8,128)(2,1)}, u32[]{:S(2)}, u32[]{:S(2)}) collective-permute-start(bf16[256,3584]{1,0:T(8,128)(2,1)} %copy-done.11), channel_id=1, source_target_pairs={{0,1},{1,0},{2,3},{3,2},{4,5},{5,4},{6,7},{7,6},{8,9},{9,8},{10,11... | collective-permute-start | bytes 5505032 | tf_op jit(solution)/shard_map/ppermute | solution.py:294
  243.4 3.9 %collective-permute-done.8.refs_0_ = bf16[352,896]{1,0:T(8,128)(2,1)} collective-permute-done((bf16[352,896]{1,0:T(8,128)(2,1)}, bf16[352,896]{1,0:T(8,128)(2,1)}, u32[]{:S(2)}, u32[]{:S(2)}) %collective-permute-start.8) | collective-permute-done | bytes 630816 | tf_op jit(solution)/shard_map/ppermute | solution.py:290
  253.2 9.5 %all-to-all-start.2 = ((bf16[64,3,4,896]{3,2,1,0:T(4,128)(2,1)}), bf16[64,3,4,896]{3,2,1,0:T(4,128)(2,1)S(1)}, u32[]{:S(2)}, u32[]{:S(2)}) async-start(bf16[64,3,4,896]{3,2,1,0:T(4,128)(2,1)} %copy.30), calls=%async_computation.2 | async-start | bytes 2752512 | tf_op jit(solution)/shard_map/all_to_all | solution.py:298
  262.8 3.9 %fusion.5 = bf16[1,3584,256]{2,1,0:T(8,128)(2,1)} fusion(bf16[3584,256]{1,0:T(8,128)(2,1)} %collective-permute-done.17, bf16[3584,256]{1,0:T(8,128)(2,1)} %get-tuple-element.32, pred[]{:T(512)} %bitcast.13), kind=kLoop, calls=%fused_computation.8 | loop fusion | flops 4587520 | bytes 5505025 | tf_op jit(solution)/shard_map/broadcast_in_dim | solution.py:355
  266.7 3.4 %fusion.4 = bf16[1,3584,256]{2,1,0:T(8,128)(2,1)} fusion(bf16[3584,256]{1,0:T(8,128)(2,1)} %collective-permute-done.18, bf16[3584,256]{1,0:T(8,128)(2,1)S(1)} %copy-done.14, pred[]{:T(512)} %bitcast.13), kind=kLoop, calls=%fused_computation.7 | loop fusion | flops 4587520 | bytes 5505025 | tf_op jit(solution)/shard_map/broadcast_in_dim | solution.py:355
  270.2 3.3 %fusion.3 = bf16[1,256,3584]{2,1,0:T(8,128)(2,1)} fusion(bf16[256,3584]{1,0:T(8,128)(2,1)} %collective-permute-done.19, bf16[256,3584]{1,0:T(8,128)(2,1)S(1)} %copy-done.12, pred[]{:T(512)} %bitcast.13), kind=kLoop, calls=%fused_computation.6 | loop fusion | flops 4587520 | bytes 5505025 | tf_op jit(solution)/shard_map/broadcast_in_dim | solution.py:355
  273.4 24.9 %all-to-all-done.2 = bf16[64,3,4,896]{3,2,1,0:T(4,128)(2,1)S(1)} async-done(((bf16[64,3,4,896]{3,2,1,0:T(4,128)(2,1)}), bf16[64,3,4,896]{3,2,1,0:T(4,128)(2,1)S(1)}, u32[]{:S(2)}, u32[]{:S(2)}) %all-to-all-start.2) | async-done | bytes 1376288 | tf_op jit(solution)/shard_map/all_to_all | solution.py:298
  (121 shorter events, 56.2 us)
Async XLA Ops:
  7.1 48.7 %all-to-all-start.1 = ((bf16[64,3,4,896]{3,2,1,0:T(4,128)(2,1)}), bf16[64,3,4,896]{3,2,1,0:T(4,128)(2,1)}, u32[]{:S(2)}, u32[]{:S(2)}) async-start(bf16[64,3,4,896]{3,2,1,0:T(4,128)(2,1)} %reshape.88), calls=%async_computation.1 | async-start | bytes 2752512 | tf_op jit(solution)/shard_map/all_to_all | solution.py:298
  55.8 41.7 %all-to-all-start = ((bf16[64,3,4,896]{3,2,1,0:T(4,128)(2,1)}), bf16[64,3,4,896]{3,2,1,0:T(4,128)(2,1)S(1)}, u32[]{:S(2)}, u32[]{:S(2)}) async-start(bf16[64,3,4,896]{3,2,1,0:T(4,128)(2,1)} %reshape.85), calls=%async_computation | async-start | bytes 2752512 | tf_op jit(solution)/shard_map/all_to_all | solution.py:298
  65.7 39.5 %collective-permute-start.4 = (bf16[704,896]{1,0:T(8,128)(2,1)}, bf16[704,896]{1,0:T(8,128)(2,1)S(1)}, u32[]{:S(2)}, u32[]{:S(2)}) collective-permute-start(bf16[704,896]{1,0:T(8,128)(2,1)} %reshape.90.own.x0), channel_id=1, source_target_pairs={{0,64},{64,128},{128,192},{192,0},{1,65},{65,129},{129,193},{193,1... | collective-permute-start | bytes 3784712 | tf_op jit(solution)/shard_map/ppermute | solution.py:290
  67.0 40.2 %collective-permute-start.5 = (bf16[704,896]{1,0:T(8,128)(2,1)}, bf16[704,896]{1,0:T(8,128)(2,1)}, u32[]{:S(2)}, u32[]{:S(2)}) collective-permute-start(bf16[704,896]{1,0:T(8,128)(2,1)} %reshape.90.own.x0), channel_id=1, source_target_pairs={{0,192},{64,0},{128,64},{192,128},{1,193},{65,1},{129,65},{193,129... | collective-permute-start | bytes 3784712 | tf_op jit(solution)/shard_map/ppermute | solution.py:290
  102.3 30.6 %collective-permute-start = (bf16[704,896]{1,0:T(8,128)(2,1)S(1)}, bf16[704,896]{1,0:T(8,128)(2,1)S(1)}, u32[]{:S(2)}, u32[]{:S(2)}) collective-permute-start(bf16[704,896]{1,0:T(8,128)(2,1)S(1)} %reshape.87.own.d0), channel_id=1, source_target_pairs={{0,64},{64,128},{128,192},{192,0},{1,65},{65,129},{129,193},{193,1... | collective-permute-start | bytes 3784712 | tf_op jit(solution)/shard_map/ppermute | solution.py:290
  103.7 30.3 %collective-permute-start.1 = (bf16[704,896]{1,0:T(8,128)(2,1)S(1)}, bf16[704,896]{1,0:T(8,128)(2,1)S(1)}, u32[]{:S(2)}, u32[]{:S(2)}) collective-permute-start(bf16[704,896]{1,0:T(8,128)(2,1)S(1)} %reshape.87.own.d0), channel_id=1, source_target_pairs={{0,192},{64,0},{128,64},{192,128},{1,193},{65,1},{129,65},{193,129... | collective-permute-start | bytes 3784712 | tf_op jit(solution)/shard_map/ppermute | solution.py:290
  107.1 39.4 %copy-start = (bf16[1,3584,256]{2,1,0:T(8,128)(2,1)S(1)}, bf16[1,3584,256]{2,1,0:T(8,128)(2,1)}, u32[]{:S(2)}) copy-start(bf16[1,3584,256]{2,1,0:T(8,128)(2,1)} %param.13) | copy-start | bytes 5505028
  107.1 39.4 %collective-permute-start.6 = (bf16[352,896]{1,0:T(8,128)(2,1)}, bf16[352,896]{1,0:T(8,128)(2,1)}, u32[]{:S(2)}, u32[]{:S(2)}) collective-permute-start(bf16[352,896]{1,0:T(8,128)(2,1)} %slice.28), channel_id=1, source_target_pairs={{0,64},{64,128},{128,192},{192,0},{1,65},{65,129},{129,193},{193,1... | collective-permute-start | bytes 1892360 | tf_op jit(solution)/shard_map/ppermute | solution.py:290
  109.2 37.3 %collective-permute-start.7 = (bf16[352,896]{1,0:T(8,128)(2,1)}, bf16[352,896]{1,0:T(8,128)(2,1)}, u32[]{:S(2)}, u32[]{:S(2)}) collective-permute-start(bf16[352,896]{1,0:T(8,128)(2,1)} %slice.29), channel_id=1, source_target_pairs={{0,192},{64,0},{128,64},{192,128},{1,193},{65,1},{129,65},{193,129... | collective-permute-start | bytes 1892360 | tf_op jit(solution)/shard_map/ppermute | solution.py:290
  133.9 26.1 %collective-permute-start.2 = (bf16[352,896]{1,0:T(8,128)(2,1)}, bf16[352,896]{1,0:T(8,128)(2,1)}, u32[]{:S(2)}, u32[]{:S(2)}) collective-permute-start(bf16[352,896]{1,0:T(8,128)(2,1)} %slice.25), channel_id=1, source_target_pairs={{0,64},{64,128},{128,192},{192,0},{1,65},{65,129},{129,193},{193,1... | collective-permute-start | bytes 1892360 | tf_op jit(solution)/shard_map/ppermute | solution.py:290
  135.4 24.6 %collective-permute-start.3 = (bf16[352,896]{1,0:T(8,128)(2,1)}, bf16[352,896]{1,0:T(8,128)(2,1)S(1)}, u32[]{:S(2)}, u32[]{:S(2)}) collective-permute-start(bf16[352,896]{1,0:T(8,128)(2,1)} %slice.26), channel_id=1, source_target_pairs={{0,192},{64,0},{128,64},{192,128},{1,193},{65,1},{129,65},{193,129... | collective-permute-start | bytes 1892360 | tf_op jit(solution)/shard_map/ppermute | solution.py:290
  181.1 81.7 %collective-permute-start.17 = (bf16[3584,256]{1,0:T(8,128)(2,1)}, bf16[3584,256]{1,0:T(8,128)(2,1)}, u32[]{:S(2)}, u32[]{:S(2)}) collective-permute-start(bf16[3584,256]{1,0:T(8,128)(2,1)} %get-tuple-element.32), channel_id=1, source_target_pairs={{0,1},{1,0},{2,3},{3,2},{4,5},{5,4},{6,7},{7,6},{8,9},{9,8},{10,11... | collective-permute-start | bytes 5505032 | tf_op jit(solution)/shard_map/ppermute | solution.py:294
  182.9 33.7 %collective-permute-start.12 = (bf16[352,896]{1,0:T(8,128)(2,1)S(1)}, bf16[352,896]{1,0:T(8,128)(2,1)S(1)}, u32[]{:S(2)}, u32[]{:S(2)}) collective-permute-start(bf16[352,896]{1,0:T(8,128)(2,1)S(1)} %shard_map.127), channel_id=1, source_target_pairs={{0,192},{64,0},{128,64},{192,128},{1,193},{65,1},{129,65},{193,129... | collective-permute-start | bytes 1892360 | tf_op jit(solution)/shard_map/ppermute | solution.py:290
  186.5 32.7 %collective-permute-start.9 = (bf16[352,896]{1,0:T(8,128)(2,1)S(1)}, bf16[352,896]{1,0:T(8,128)(2,1)S(1)}, u32[]{:S(2)}, u32[]{:S(2)}) collective-permute-start(bf16[352,896]{1,0:T(8,128)(2,1)S(1)} %shard_map.123), channel_id=1, source_target_pairs={{0,64},{64,128},{128,192},{192,0},{1,65},{65,129},{129,193},{193,1... | collective-permute-start | bytes 1892360 | tf_op jit(solution)/shard_map/ppermute | solution.py:290
  188.3 40.0 %collective-permute-start.11 = (bf16[352,896]{1,0:T(8,128)(2,1)}, bf16[352,896]{1,0:T(8,128)(2,1)S(1)}, u32[]{:S(2)}, u32[]{:S(2)}) collective-permute-start(bf16[352,896]{1,0:T(8,128)(2,1)} %shard_map.126), channel_id=1, source_target_pairs={{0,64},{64,128},{128,192},{192,0},{1,65},{65,129},{129,193},{193,1... | collective-permute-start | bytes 1892360 | tf_op jit(solution)/shard_map/ppermute | solution.py:290
  188.3 28.4 %collective-permute-start.15 = (f32[64,128]{1,0:T(8,128)S(1)}, f32[64,128]{1,0:T(8,128)S(1)}, u32[]{:S(2)}, u32[]{:S(2)}) collective-permute-start(f32[64,128]{1,0:T(8,128)S(1)} %get-tuple-element.29), channel_id=1, source_target_pairs={{0,64},{64,128},{128,192},{192,0},{1,65},{65,129},{129,193},{193,1... | collective-permute-start | bytes 98312 | tf_op jit(solution)/shard_map/ppermute | solution.py:290
  216.6 7.2 %collective-permute-start.16 = (f32[64,128]{1,0:T(8,128)S(1)}, f32[64,128]{1,0:T(8,128)S(1)}, u32[]{:S(2)}, u32[]{:S(2)}) collective-permute-start(f32[64,128]{1,0:T(8,128)S(1)} %get-tuple-element.29), channel_id=1, source_target_pairs={{0,192},{64,0},{128,64},{192,128},{1,193},{65,1},{129,65},{193,129... | collective-permute-start | bytes 98312 | tf_op jit(solution)/shard_map/ppermute | solution.py:290
  216.6 7.2 %collective-permute-start.14 = (f32[64,128]{1,0:T(8,128)S(1)}, f32[64,128]{1,0:T(8,128)S(1)}, u32[]{:S(2)}, u32[]{:S(2)}) collective-permute-start(f32[64,128]{1,0:T(8,128)S(1)} %get-tuple-element.29), channel_id=1, source_target_pairs={{0,128},{64,192},{128,0},{192,64},{1,129},{65,193},{129,1},{193,65... | collective-permute-start | bytes 98312 | tf_op jit(solution)/shard_map/ppermute | solution.py:290
  219.2 14.6 %collective-permute-start.13 = (bf16[352,896]{1,0:T(8,128)(2,1)}, bf16[352,896]{1,0:T(8,128)(2,1)}, u32[]{:S(2)}, u32[]{:S(2)}) collective-permute-start(bf16[352,896]{1,0:T(8,128)(2,1)} %shard_map.128), channel_id=1, source_target_pairs={{0,192},{64,0},{128,64},{192,128},{1,193},{65,1},{129,65},{193,129... | collective-permute-start | bytes 1892360 | tf_op jit(solution)/shard_map/ppermute | solution.py:290
  223.8 23.5 %collective-permute-start.8 = (bf16[352,896]{1,0:T(8,128)(2,1)}, bf16[352,896]{1,0:T(8,128)(2,1)}, u32[]{:S(2)}, u32[]{:S(2)}) collective-permute-start(bf16[352,896]{1,0:T(8,128)(2,1)} %shard_map.122), channel_id=1, source_target_pairs={{0,192},{64,0},{128,64},{192,128},{1,193},{65,1},{129,65},{193,129... | collective-permute-start | bytes 1892360 | tf_op jit(solution)/shard_map/ppermute | solution.py:290
  224.4 22.8 %collective-permute-start.10 = (bf16[352,896]{1,0:T(8,128)(2,1)}, bf16[352,896]{1,0:T(8,128)(2,1)}, u32[]{:S(2)}, u32[]{:S(2)}) collective-permute-start(bf16[352,896]{1,0:T(8,128)(2,1)} %shard_map.124), channel_id=1, source_target_pairs={{0,64},{64,128},{128,192},{192,0},{1,65},{65,129},{129,193},{193,1... | collective-permute-start | bytes 1892360 | tf_op jit(solution)/shard_map/ppermute | solution.py:290
  228.3 38.4 %collective-permute-start.18 = (bf16[3584,256]{1,0:T(8,128)(2,1)}, bf16[3584,256]{1,0:T(8,128)(2,1)}, u32[]{:S(2)}, u32[]{:S(2)}) collective-permute-start(bf16[3584,256]{1,0:T(8,128)(2,1)} %copy-done.13), channel_id=1, source_target_pairs={{0,1},{1,0},{2,3},{3,2},{4,5},{5,4},{6,7},{7,6},{8,9},{9,8},{10,11... | collective-permute-start | bytes 5505032 | tf_op jit(solution)/shard_map/ppermute | solution.py:294
  233.8 36.4 %collective-permute-start.19 = (bf16[256,3584]{1,0:T(8,128)(2,1)}, bf16[256,3584]{1,0:T(8,128)(2,1)}, u32[]{:S(2)}, u32[]{:S(2)}) collective-permute-start(bf16[256,3584]{1,0:T(8,128)(2,1)} %copy-done.11), channel_id=1, source_target_pairs={{0,1},{1,0},{2,3},{3,2},{4,5},{5,4},{6,7},{7,6},{8,9},{9,8},{10,11... | collective-permute-start | bytes 5505032 | tf_op jit(solution)/shard_map/ppermute | solution.py:294
  253.2 45.1 %all-to-all-start.2 = ((bf16[64,3,4,896]{3,2,1,0:T(4,128)(2,1)}), bf16[64,3,4,896]{3,2,1,0:T(4,128)(2,1)S(1)}, u32[]{:S(2)}, u32[]{:S(2)}) async-start(bf16[64,3,4,896]{3,2,1,0:T(4,128)(2,1)} %copy.30), calls=%async_computation.2 | async-start | bytes 2752512 | tf_op jit(solution)/shard_map/all_to_all | solution.py:298
  (26 other events, 177.7 us)

commit v2 on v1

v2 whole, which is shorter than its diff:
```python
import functools

import jax
import jax.numpy as jnp
from jax import lax
from jax.experimental import pallas as pl
from jax.experimental.pallas import tpu as pltpu
from jax.sharding import PartitionSpec as P

F32 = jnp.float32
BF16 = jnp.bfloat16
SLOTS = 64
CAP = 11
BLOCK = 12
TOK = 128
PADDED = SLOTS * BLOCK
HALF = PADDED // 2
QUARTER = 896
WIDTH = 3584
SHARE = 256
N_DP = 4
TILE = 192
TILES = PADDED // TILE
VMEM = pltpu.VMEM
HEAVY = 40_000_000_000


def iota(shape, dim):
    return lax.broadcasted_iota(jnp.int32, shape, dim)


def dot(left, right, left_dim=1, right_dim=0, precision=None):
    return lax.dot_general(
        left, right, (((left_dim,), (right_dim,)), ((), ())),
        precision=precision, preferred_element_type=F32,
    )


def params(mib):
    return pltpu.CompilerParams(vmem_limit_bytes=mib << 20)


def pack_kernel(parity_ref, slot_ref, ids_ref, probs_ref, tok_ref, x_ref, code_ref, pick_ref, scaled_ref):
    slot = slot_ref[...]
    index = iota((SLOTS, TOK), 0)
    second = (index & 1).astype(F32)
    partner = jnp.where(second > 0, pltpu.roll(slot, 1, 0), pltpu.roll(slot, SLOTS - 1, 0))
    paired = slot == partner
    ids = ids_ref[...].astype(F32)
    probs = probs_ref[...].astype(F32)
    chosen = jnp.zeros((SLOTS, TOK), F32)
    weight = jnp.zeros((SLOTS, TOK), F32)
    for k in range(4):
        here = slot == ids[k:k + 1, :]
        chosen = chosen + jnp.where(here, 1.0, 0.0)
        weight = weight + jnp.where(here, probs[k:k + 1, :], 0.0)
    earlier = jnp.where(iota((TOK, TOK), 0) < iota((TOK, TOK), 1), 1.0, 0.0).astype(BF16)
    rank = dot(chosen.astype(BF16), earlier)
    shifted = rank + parity_ref[0].astype(F32)
    half = jnp.floor(shifted * 0.5)
    taken = jnp.where(paired, jnp.where(shifted - 2.0 * half == second, 1.0, 0.0), 1.0) * chosen
    place = jnp.where(paired, half, rank)
    code = jnp.where(taken > 0, place + 1.0, 0.0)
    code_ref[...] = code
    row, col = iota((PADDED, SLOTS), 0), iota((PADDED, SLOTS), 1) * BLOCK
    spread = jnp.where(row >= col, jnp.where(row < col + BLOCK, 1.0, 0.0), 0.0).astype(BF16)
    number = iota((PADDED, TOK), 0).astype(F32)
    within = number - BLOCK * jnp.floor((number + 0.5) * (1.0 / BLOCK)) + 1.0
    pick = jnp.where(dot(spread, code.astype(BF16)) == within, 1.0, 0.0)
    scaled = pick * dot(spread, weight.astype(BF16))
    pick = pick.astype(BF16)
    pick_ref[...] = pick
    scaled_ref[...] = scaled.astype(BF16)
    x_ref[...] = dot(pick, tok_ref[...]).astype(BF16)


def pack(parity, slot, ids, probs, tokens):
    whole = pl.BlockSpec(memory_space=VMEM)
    return pl.pallas_call(
        pack_kernel,
        out_shape=(
            jax.ShapeDtypeStruct((PADDED, QUARTER), BF16),
            jax.ShapeDtypeStruct((SLOTS, TOK), F32),
            jax.ShapeDtypeStruct((PADDED, TOK), BF16),
            jax.ShapeDtypeStruct((PADDED, TOK), BF16),
        ),
        in_specs=[pl.BlockSpec(memory_space=pltpu.SMEM)] + [whole] * 4,
        out_specs=(whole,) * 4,
        compiler_params=params(24),
        cost_estimate=pl.CostEstimate(flops=HEAVY, bytes_accessed=3_000_000, transcendentals=0),
    )(parity, slot, ids, probs, tokens)


def scale_kernel(scaled_ref, cot_ref, out_ref):
    out_ref[...] = dot(scaled_ref[...], cot_ref[...]).astype(BF16)


def scale(scaled, cotangent):
    whole = pl.BlockSpec(memory_space=VMEM)
    return pl.pallas_call(
        scale_kernel,
        out_shape=jax.ShapeDtypeStruct((PADDED, QUARTER), BF16),
        in_specs=[whole] * 2,
        out_specs=whole,
        compiler_params=params(16),
        cost_estimate=pl.CostEstimate(flops=HEAVY, bytes_accessed=2_000_000, transcendentals=0),
    )(scaled, cotangent)


def combine_kernel(slot_ref, ids_ref, probs_ref, code_ref, pick_ref, back_ref, dtok_ref, dprob_ref):
    dtok_ref[...] = dot(pick_ref[...], back_ref[...], 0, 0).astype(BF16)
    chosen = jnp.where(
        iota((SLOTS, PADDED), 1) == iota((SLOTS, PADDED), 0) * BLOCK + CAP, 1.0, 0.0
    ).astype(BF16)
    scores = dot(chosen, back_ref[:, 0:TOK]) + dot(chosen, back_ref[:, TOK:2 * TOK])
    code = code_ref[...]
    placed = jnp.zeros((SLOTS, TOK), F32)
    for r in range(CAP):
        placed = placed + jnp.where(code == r + 1.0, scores[:, r:r + 1], 0.0)
    ids = ids_ref[...].astype(F32)
    probs = probs_ref[...].astype(F32)
    slot = slot_ref[...]
    found = [
        jnp.sum(jnp.where(slot == ids[k:k + 1, :], placed, 0.0), axis=0, keepdims=True)
        for k in range(4)
    ]
    dprob_ref[...] = jnp.concatenate(found, axis=0) / probs


def combine(slot, ids, probs, code, pick, back):
    whole = pl.BlockSpec(memory_space=VMEM)
    return pl.pallas_call(
        combine_kernel,
        out_shape=(
            jax.ShapeDtypeStruct((TOK, QUARTER), BF16),
            jax.ShapeDtypeStruct((4, TOK), F32),
        ),
        in_specs=[whole] * 6,
        out_specs=(whole,) * 2,
        compiler_params=params(24),
        cost_estimate=pl.CostEstimate(flops=200_000_000, bytes_accessed=2_000_000, transcendentals=0),
    )(slot, ids, probs, code, pick, back)


def half_specs(cols):
    low = pl.BlockSpec((TILE, cols), lambda m, at: (jnp.minimum(m, TILES // 2 - 1), 0))
    high = pl.BlockSpec((TILE, cols), lambda m, at: (jnp.maximum(m - TILES // 2, 0), 0))
    return [low, high]


def this_tile(refs):
    lower = pl.program_id(0) < TILES // 2
    return [jnp.where(lower, low[...], high[...]) for low, high in zip(refs[0::2], refs[1::2])]


def offset(at_ref, rel):
    return pl.multiple_of(lax.rem(at_ref[0] + rel, N_DP) * QUARTER, 128)


def weights_kernel(at_ref, wg_ref, wu_ref, wd_ref, *refs):
    for b, out in zip((1, 2, 3), refs):
        where = pl.ds(offset(at_ref, b), QUARTER)
        out[:QUARTER, :] = wg_ref[where, :]
        out[QUARTER:2 * QUARTER, :] = wu_ref[where, :]
        out[2 * QUARTER:, :] = wd_ref[:, where].T


def weights(at, wg, wu, wd):
    whole = pl.BlockSpec(memory_space=VMEM)
    return pl.pallas_call(
        weights_kernel,
        out_shape=(jax.ShapeDtypeStruct((3 * QUARTER, SHARE), BF16),) * 3,
        in_specs=[pl.BlockSpec(memory_space=pltpu.SMEM), whole, whole, whole],
        out_specs=(whole,) * 3,
        compiler_params=params(24),
        cost_estimate=pl.CostEstimate(flops=0, bytes_accessed=9_600_000, transcendentals=0),
    )(at, wg, wu, wd)


def halves_kernel(rows_ref, a1, a2, a3, a4, low_ref, high_ref):
    low_ref[...] = rows_ref[:HALF, :]
    high_ref[...] = rows_ref[HALF:, :]


def halves(rows, after):
    whole = pl.BlockSpec(memory_space=VMEM)
    return pl.pallas_call(
        halves_kernel,
        out_shape=(jax.ShapeDtypeStruct((HALF, QUARTER), BF16),) * 2,
        in_specs=[whole] + [pl.BlockSpec(memory_space=pl.ANY)] * 4,
        out_specs=(whole,) * 2,
        compiler_params=params(16),
        cost_estimate=pl.CostEstimate(flops=HEAVY, bytes_accessed=2_800_000, transcendentals=0),
    )(rows, *after)


def near_kernel(at_ref, *refs):
    wg_ref, wu_ref, out_ref = refs[6:]
    gate = jnp.zeros((TILE, SHARE), F32)
    up = jnp.zeros((TILE, SHARE), F32)
    for rel, part in zip((0, 3, 1), this_tile(refs[:6])):
        where = pl.ds(offset(at_ref, rel), QUARTER)
        gate = gate + dot(part, wg_ref[where, :])
        up = up + dot(part, wu_ref[where, :])
    out_ref[:, :SHARE] = gate
    out_ref[:, SHARE:] = up


def near(at, parts, wg, wu):
    whole = pl.BlockSpec((WIDTH, SHARE), lambda m, at: (0, 0))
    return pl.pallas_call(
        near_kernel,
        out_shape=jax.ShapeDtypeStruct((PADDED, 2 * SHARE), F32),
        grid_spec=pltpu.PrefetchScalarGridSpec(
            num_scalar_prefetch=1, grid=(TILES,),
            in_specs=half_specs(QUARTER) * 3 + [whole, whole],
            out_specs=pl.BlockSpec((TILE, 2 * SHARE), lambda m, at: (m, 0)),
        ),
        compiler_params=params(32),
        cost_estimate=pl.CostEstimate(
            flops=3 * PADDED * WIDTH * SHARE, bytes_accessed=9_000_000, transcendentals=0
        ),
    )(at, *parts, wg, wu)


def forward_kernel(at_ref, low, high, sum_ref, wg_ref, wu_ref, hid_ref, act_ref, ups_ref):
    part = this_tile((low, high))[0]
    gate = sum_ref[:, :SHARE] + dot(part, wg_ref[...])
    up = sum_ref[:, SHARE:] + dot(part, wu_ref[...])
    sig = jax.nn.sigmoid(gate)
    act = gate * sig
    hid_ref[...] = (act * up).astype(BF16)
    act_ref[...] = act
    ups_ref[...] = up * (sig * (1.0 + gate * (1.0 - sig)))


def forward(at, far, summed, wg, wu):
    tile = pl.BlockSpec((TILE, SHARE), lambda m, at: (m, 0))
    rows = pl.BlockSpec((QUARTER, SHARE), lambda m, at: (lax.rem(at[0] + 2, N_DP), 0))
    return pl.pallas_call(
        forward_kernel,
        out_shape=(
            jax.ShapeDtypeStruct((PADDED, SHARE), BF16),
            jax.ShapeDtypeStruct((PADDED, SHARE), F32),
            jax.ShapeDtypeStruct((PADDED, SHARE), F32),
        ),
        grid_spec=pltpu.PrefetchScalarGridSpec(
            num_scalar_prefetch=1, grid=(TILES,),
            in_specs=half_specs(QUARTER)
            + [pl.BlockSpec((TILE, 2 * SHARE), lambda m, at: (m, 0)), rows, rows],
            out_specs=(tile,) * 3,
        ),
        compiler_params=params(32),
        cost_estimate=pl.CostEstimate(
            flops=PADDED * WIDTH * SHARE, bytes_accessed=4_000_000, transcendentals=PADDED * SHARE
        ),
    )(at, *far, summed, wg, wu)


def terms_kernel(at_ref, rows_ref, w0, w1, w2, w3, own_ref, p1, p2, p3):
    rows = rows_ref[...]
    own_ref[...] = dot(rows, w0[...], 1, 1)
    for w, p in ((w1, p1), (w2, p2), (w3, p3)):
        p[...] = dot(rows, w[...]).astype(BF16)


def terms(at, rows, wd, blocks):
    tile = pl.BlockSpec((TILE, SHARE), lambda m, at: (m, 0))
    down = pl.BlockSpec((QUARTER, SHARE), lambda m, at: (2, 0))
    sent = jax.ShapeDtypeStruct((PADDED, SHARE), BF16)
    return pl.pallas_call(
        terms_kernel,
        out_shape=(jax.ShapeDtypeStruct((PADDED, SHARE), F32), sent, sent, sent),
        grid_spec=pltpu.PrefetchScalarGridSpec(
            num_scalar_prefetch=1, grid=(TILES,),
            in_specs=[
                pl.BlockSpec((TILE, QUARTER), lambda m, at: (m, 0)),
                pl.BlockSpec((SHARE, QUARTER), lambda m, at: (0, at[0])),
                down, down, down,
            ],
            out_specs=(tile,) * 4,
        ),
        compiler_params=params(32),
        cost_estimate=pl.CostEstimate(
            flops=2 * PADDED * WIDTH * SHARE, bytes_accessed=5_000_000, transcendentals=0
        ),
    )(at, rows, wd, *blocks)


def within_block(shape):
    number = iota(shape, 0).astype(F32)
    return number - BLOCK * jnp.floor((number + 0.5) * (1.0 / BLOCK))


def slopes_kernel(own, r1, r2, r3, hid_ref, act_ref, ups_ref, low_ref, high_ref):
    d_hidden = own[...] + r1[...].astype(F32) + r2[...].astype(F32) + r3[...].astype(F32)
    dg = d_hidden * ups_ref[...]
    du = d_hidden * act_ref[...]
    score = jnp.sum(hid_ref[...].astype(F32) * d_hidden, axis=1, keepdims=True)
    lanes = jnp.where(iota((TILE, TOK), 1).astype(F32) == within_block((TILE, TOK)), score, 0.0)
    high = lanes.astype(BF16)
    rest = (lanes - high.astype(F32)).astype(BF16)
    row = iota((TILE, TILE), 0).astype(F32)
    start = row - within_block((TILE, TILE))
    col = iota((TILE, TILE), 1).astype(F32)
    spare = within_block((TILE, SHARE)) == CAP
    group = jnp.where(col >= start, jnp.where(col < start + BLOCK, 1.0, 0.0), 0.0).astype(BF16)
    moved = jnp.concatenate([dot(group, high), dot(group, rest)], axis=1)
    both = jnp.concatenate([jnp.where(spare, moved, dg), du], axis=1).astype(BF16)
    m = pl.program_id(0)

    @pl.when(m < TILES // 2)
    def _():
        low_ref[...] = both

    @pl.when(m >= TILES // 2)
    def _():
        high_ref[...] = both


def slopes(own, others, hid, act, ups):
    tile = pl.BlockSpec((TILE, SHARE), lambda m: (m, 0))
    return pl.pallas_call(
        slopes_kernel,
        out_shape=(jax.ShapeDtypeStruct((HALF, 2 * SHARE), BF16),) * 2,
        grid=(TILES,),
        in_specs=[tile] * 7,
        out_specs=(
            pl.BlockSpec((TILE, 2 * SHARE), lambda m: (jnp.minimum(m, TILES // 2 - 1), 0)),
            pl.BlockSpec((TILE, 2 * SHARE), lambda m: (jnp.maximum(m - TILES // 2, 0), 0)),
        ),
        compiler_params=params(24),
        cost_estimate=pl.CostEstimate(flops=50_000_000, bytes_accessed=5_000_000, transcendentals=0),
    )(own, *others, hid, act, ups)


def product(slope, blocks):
    return dot(slope[:, :SHARE], blocks[0], 1, 1) + dot(slope[:, SHARE:], blocks[1], 1, 1)


def back_near_kernel(at_ref, *refs):
    wg_ref, wu_ref, g1, g3, out_ref = refs[6:]
    own, below, above = this_tile(refs[:6])
    total = product(own, (wg_ref[...], wu_ref[...]))
    for slope, g in ((below, g1), (above, g3)):
        total = total + product(slope, (g[:QUARTER, :], g[QUARTER:, :]))
    out_ref[...] = total


def back_kernel(at_ref, *refs):
    sum_ref, g2, out_ref = refs[8:]
    own, below, above, far = this_tile(refs[:8])
    total = sum_ref[...] + product(far, (g2[:QUARTER, :], g2[QUARTER:, :]))
    out_ref[...] = total.astype(BF16)
    parts = [s[:, :SHARE].astype(F32) for s in (own, below, above, far)]
    lanes = (parts[0] + parts[3]) + (parts[1] + parts[2])
    score = lanes[:, :TOK] + lanes[:, TOK:]
    high = score.astype(BF16)
    rest = (score - high.astype(F32)).astype(BF16)
    spare = within_block((TILE, TOK)) == CAP
    out_ref[:, :TOK] = jnp.where(spare, high.astype(F32), total[:, :TOK]).astype(BF16)
    out_ref[:, TOK:2 * TOK] = jnp.where(spare, rest.astype(F32), total[:, TOK:2 * TOK]).astype(BF16)


def back_near(at, parts, wg, wu, blocks):
    mine = pl.BlockSpec((QUARTER, SHARE), lambda m, at: (at[0], 0))
    both = pl.BlockSpec((2 * QUARTER, SHARE), lambda m, at: (0, 0))
    return pl.pallas_call(
        back_near_kernel,
        out_shape=jax.ShapeDtypeStruct((PADDED, QUARTER), F32),
        grid_spec=pltpu.PrefetchScalarGridSpec(
            num_scalar_prefetch=1, grid=(TILES,),
            in_specs=half_specs(2 * SHARE) * 3 + [mine, mine, both, both],
            out_specs=pl.BlockSpec((TILE, QUARTER), lambda m, at: (m, 0)),
        ),
        compiler_params=params(32),
        cost_estimate=pl.CostEstimate(
            flops=3 * PADDED * WIDTH * SHARE, bytes_accessed=8_000_000, transcendentals=0
        ),
    )(at, *parts, wg, wu, blocks[0], blocks[2])


def back_rows(at, parts, summed, block):
    both = pl.BlockSpec((2 * QUARTER, SHARE), lambda m, at: (0, 0))
    tile = pl.BlockSpec((TILE, QUARTER), lambda m, at: (m, 0))
    return pl.pallas_call(
        back_kernel,
        out_shape=jax.ShapeDtypeStruct((PADDED, QUARTER), BF16),
        grid_spec=pltpu.PrefetchScalarGridSpec(
            num_scalar_prefetch=1, grid=(TILES,),
            in_specs=half_specs(2 * SHARE) * 4 + [tile, both], out_specs=tile,
        ),
        compiler_params=params(32),
        cost_estimate=pl.CostEstimate(
            flops=PADDED * WIDTH * SHARE, bytes_accessed=8_000_000, transcendentals=0
        ),
    )(at, *parts, summed, block)


def turn_kernel(*refs):
    half = len(refs) // 3 * 2
    for i, out in enumerate(refs[half:]):
        for c in range(QUARTER // TOK):
            cols = slice(c * TOK, (c + 1) * TOK)
            out[cols, :HALF] = refs[2 * i][:, cols].T
            out[cols, HALF:] = refs[2 * i + 1][:, cols].T


def turn(parts):
    whole = pl.BlockSpec(memory_space=VMEM)
    n = len(parts) // 2
    return pl.pallas_call(
        turn_kernel,
        out_shape=(jax.ShapeDtypeStruct((QUARTER, PADDED), BF16),) * n,
        in_specs=[whole] * (2 * n),
        out_specs=(whole,) * n,
        compiler_params=params(24),
        cost_estimate=pl.CostEstimate(flops=0, bytes_accessed=3_000_000 * n, transcendentals=0),
    )(*parts)


def grads_kernel(at_ref, x0, x1, x2, x3, low_ref, high_ref, gg_ref, gu_ref):
    slope = jnp.concatenate([low_ref[...], high_ref[...]], axis=0)
    step = QUARTER // 4
    for rel, x in zip((0, 3, 1, 2), (x0, x1, x2, x3)):
        base = offset(at_ref, rel)

        def body(c, _, x=x, base=base):
            grad = dot(x[pl.ds(pl.multiple_of(c * step, 32), step), :], slope).astype(BF16)
            to = pl.ds(pl.multiple_of(base + c * step, 32), step)
            gg_ref[to, :] = grad[:, :SHARE]
            gu_ref[to, :] = grad[:, SHARE:]
            return 0

        lax.fori_loop(0, 4, body, 0)


def grads(at, xs, slope):
    whole = pl.BlockSpec(memory_space=VMEM)
    return pl.pallas_call(
        grads_kernel,
        out_shape=(jax.ShapeDtypeStruct((WIDTH, SHARE), BF16),) * 2,
        in_specs=[pl.BlockSpec(memory_space=pltpu.SMEM)] + [whole] * 6,
        out_specs=(whole,) * 2,
        compiler_params=params(32),
        cost_estimate=pl.CostEstimate(
            flops=4 * PADDED * WIDTH * SHARE, bytes_accessed=11_000_000, transcendentals=0
        ),
    )(at, *xs, *slope)


def down_kernel(h0, h1, h2, h3, rows_ref, out_ref):
    for b, h in enumerate((h0, h1, h2, h3)):
        out_ref[b * SHARE:(b + 1) * SHARE, :] = dot(h[...], rows_ref[...], 0, 0).astype(BF16)


def down_grads(hids, rows):
    whole = pl.BlockSpec(memory_space=VMEM)
    return pl.pallas_call(
        down_kernel,
        out_shape=jax.ShapeDtypeStruct((N_DP * SHARE, QUARTER), BF16),
        in_specs=[whole] * 5,
        out_specs=whole,
        compiler_params=params(24),
        cost_estimate=pl.CostEstimate(
            flops=HEAVY, bytes_accessed=5_000_000, transcendentals=0
        ),
    )(*hids, rows)


def join_kernel(n_out, same_ref, mine_ref, other_ref, *outs):
    mine = mine_ref[...].astype(F32)
    both = jnp.where(same_ref[0] > 0, mine + other_ref[...].astype(F32), mine).astype(BF16)
    rows = both.shape[0] // n_out
    for b, out in enumerate(outs):
        out[...] = both[b * rows:(b + 1) * rows]


def join(same, mine, other, n_out):
    rows, cols = mine.shape
    steps = 7 if n_out == 1 else 1
    block = pl.BlockSpec((rows // steps, cols), lambda m, same: (m, 0))
    out = pl.BlockSpec((rows // steps // n_out, cols), lambda m, same: (m, 0))
    return pl.pallas_call(
        functools.partial(join_kernel, n_out),
        out_shape=(jax.ShapeDtypeStruct((rows // n_out, cols), BF16),) * n_out,
        grid_spec=pltpu.PrefetchScalarGridSpec(
            num_scalar_prefetch=1, grid=(steps,),
            in_specs=[block, block], out_specs=(out,) * n_out,
        ),
        compiler_params=params(24),
        cost_estimate=pl.CostEstimate(flops=0, bytes_accessed=0, transcendentals=0),
    )(same, mine, other)


def place_kernel(at_ref, p0, p1, p2, p3, out_ref):
    for rel, p in enumerate((p0, p1, p2, p3)):
        out_ref[:, pl.ds(offset(at_ref, rel), QUARTER)] = p[...]


def placed(at, parts):
    whole = pl.BlockSpec(memory_space=VMEM)
    return pl.pallas_call(
        place_kernel,
        out_shape=jax.ShapeDtypeStruct((SHARE, WIDTH), BF16),
        in_specs=[pl.BlockSpec(memory_space=pltpu.SMEM)] + [whole] * 4,
        out_specs=whole,
        compiler_params=params(16),
        cost_estimate=pl.CostEstimate(flops=0, bytes_accessed=0, transcendentals=0),
    )(at, *parts)


def shift(x, by):
    return lax.ppermute(x, "dp", [(i, (i + by) % N_DP) for i in range(N_DP)])


def swap(x):
    return lax.ppermute(x, "expert", [(i, i ^ 1) for i in range(SLOTS)])


def exchange(rows):
    return lax.all_to_all(
        rows.reshape(SLOTS, 3, 4, QUARTER), "expert", split_axis=0, concat_axis=0, tiled=True
    )


def ring(low, high):
    low_below, high_above = shift(low, 1), shift(high, -1)
    high_below, low_above = shift(high, 1), shift(low, -1)
    far = [shift(low_below, 1), shift(high_above, -1)]
    return [low, high], [low_below, high_below], [low_above, high_above], far


def ordered(arrays):
    return lax.optimization_barrier(arrays)


def shards(tokens, cotangent, expert_ids, gate_probs, slot_expert, w_gate, w_up, w_down):
    here = lax.axis_index("expert")
    at = lax.axis_index("dp").reshape(1)
    parity = (here % 2).reshape(1)
    wg, wu, wd = w_gate[0], w_up[0], w_down[0]
    ids, probs = expert_ids.T, gate_probs.T
    slot = jnp.broadcast_to(slot_expert.astype(F32)[:, None], (SLOTS, TOK))
    x_rows, code, pick, scaled = pack(parity, slot, ids, probs, tokens)
    d_rows = scale(scaled, cotangent)
    sent = weights(at, wg, wu, wd)
    blocks = [shift(w, b) for w, b in zip(sent, (1, 2, 3))]
    x_rows, token = ordered((x_rows, swap(sent[0][:16])))
    x_here = exchange(x_rows).reshape(PADDED, QUARTER)
    x_own, x_below, x_above, x_far = ring(*halves(x_here, (*blocks, token)))
    d_here, x_below, x_above = ordered((exchange(d_rows), x_below, x_above))
    d_here = d_here.reshape(PADDED, QUARTER)

    own, *out = terms(at, d_here, wd, blocks)
    others = [shift(out[b - 1], -b) for b in (2, 1, 3)]
    x_parts, own = ordered((x_own + x_below + x_above, own))
    x_turned = turn(x_parts)
    x_far, x_turned = ordered((x_far, x_turned))
    hid, act, ups = forward(at, x_far, near(at, x_parts, wg, wu), wg, wu)
    s_own, s_below, s_above, s_far = ring(*slopes(own, others, hid, act, ups))
    s_far, far_turned = ordered((s_far, turn(ordered((x_far, hid))[0])))
    summed = back_near(at, s_own + s_below + s_above, wg, wu, blocks)
    pay = back_rows(at, s_own + s_below + s_above + s_far, summed, blocks[1])
    back = exchange(pay).reshape(PADDED, QUARTER)
    d_tokens, d_probs = combine(slot, ids, probs, code, pick, back)

    same = (slot_expert[here] == slot_expert[here ^ 1]).astype(jnp.int32).reshape(1)
    hid = ordered((hid, s_below))[0]
    gg, gu = grads(at, x_turned + far_turned, ordered((s_own, pay))[0])
    gd = down_grads([hid] + [shift(hid, b) for b in (1, 2, 3)], d_here)
    pieces = join(same, gd, swap(gd), N_DP)
    grad_down = placed(at, [pieces[0]] + [shift(pieces[b], -b) for b in (1, 2, 3)])
    grad_gate = join(same, gg, swap(gg), 1)[0]
    grad_up = join(same, gu, swap(gu), 1)[0]
    return d_tokens, d_probs.T, grad_gate[None], grad_up[None], grad_down[None]


def solution(mesh):
    specs = (
        P("expert", "dp"),
        P("expert", "dp"),
        P("expert", None),
        P("expert", None),
        P(),
        P("expert", None, "dp"),
        P("expert", None, "dp"),
        P("expert", "dp", None),
    )
    return jax.shard_map(
        shards,
        mesh=mesh,
        in_specs=specs,
        out_specs=(
            P("expert", "dp"),
            P("expert", None),
            P("expert", None, "dp"),
            P("expert", None, "dp"),
            P("expert", "dp", None),
        ),
        check_vma=False,
    )
```

time: 301 us -> 253 us (0.84)
  waiting for transfers between devices: 154 us -> 79.6 us
  Pallas kernels: 41.3 us -> 59.9 us
  starting transfers between devices: 59.1 us -> 72.4 us
  other arithmetic: 12.7 us -> 0.01 us
  local copies, waits for them, and re-layouts: 30.7 us -> 36.9 us
    all_to_all x3, waiting for transfers between devices: 88.2 us -> 38.6 us  [exchange(): lax.all_to_all(rows.reshape(SLOTS, 3, 4, QUARTER), 'expert', split_axis=0...]
    pallas_call x10 -> x16, Pallas kernels: 23.4 us -> 51 us  [the longest x3 13.5 us: join(): pl.pallas_call(functools.partial(join_kernel, n_out), out_shape=(jax.Shap...]
    ppermute x17 -> x24, waiting for transfers between devices: 65.7 us -> 41 us  [shift(): return lax.ppermute(x, 'dp', [(i, (i + by) % N_DP) for i in range(N_DP)])]
    ppermute x17 -> x24, starting transfers between devices: 19.7 us -> 31.9 us  [shift(): return lax.ppermute(x, 'dp', [(i, (i + by) % N_DP) for i in range(N_DP)])]
    broadcast_in_dim x3 -> x0, other arithmetic: 10.6 us -> none  [joined(): return jnp.where(same, both, own.astype(F32)).astype(BF16)[None]]
    all_to_all x3, starting transfers between devices: 28.8 us -> 38.3 us  [exchange(): lax.all_to_all(rows.reshape(SLOTS, 3, 4, QUARTER), 'expert', split_axis=0...]
    pallas_call x1, Pallas kernels: 15.4 us -> 6.83 us  [grads(): pl.pallas_call(grads_kernel, out_shape=(jax.ShapeDtypeStruct((WIDTH, SHAR...]
    unnamed x54 -> x86, local copies, waits for them, and re-layouts: 9.96 us -> 18.5 us
  transfers between devices with their start and end apart: 23 -> 31, of which waited for: 9 -> 9; matrix products, arithmetic and copies ran while one was open for 10% -> 6% of each run, Pallas kernels for 6% -> 21%
where the time goes in v2:
time: 253 us; the launch traced here: 251 us
  waiting for transfers between devices  79.6 us (31%)
  starting transfers between devices  72.4 us (29%)
  Pallas kernels  59.9 us (24%)
  local copies, waits for them, and re-layouts  36.9 us (15%)
    ppermute x24, waiting for transfers between devices, shift(): return lax.ppermute(x, 'dp', [(i, (i + by) % N_DP) for i in range(N_DP)])  41 us
    all_to_all x3, waiting for transfers between devices, exchange(): lax.all_to_all(rows.reshape(SLOTS, 3, 4, QUARTER), 'expert', split_axis=0...  38.6 us
    all_to_all x3, starting transfers between devices, exchange(): lax.all_to_all(rows.reshape(SLOTS, 3, 4, QUARTER), 'expert', split_axis=0...  38.3 us
    ppermute x24, starting transfers between devices, shift(): return lax.ppermute(x, 'dp', [(i, (i + by) % N_DP) for i in range(N_DP)])  31.9 us
    unnamed x86, local copies, waits for them, and re-layouts  18.5 us
    pallas_call x3, Pallas kernels, join(): pl.pallas_call(functools.partial(join_kernel, n_out), out_shape=(jax.Shap...  13.5 us
    reshape x3, local copies, waits for them, and re-layouts, exchange(): rows.reshape(SLOTS, 3, 4, QUARTER)  8.45 us
    pallas_call x1, Pallas kernels, grads(): pl.pallas_call(grads_kernel, out_shape=(jax.ShapeDtypeStruct((WIDTH, SHAR...  6.83 us
  transfers between devices with their start and end apart: 31, of which 9 were waited for; matrix products, arithmetic and copies ran while one was open for 6% of the time, Pallas kernels for 21%

profile of v2, /device:TPU:1, one launch (start us, length us, event | category | flops | bytes accessed | tf_op | source)
XLA Modules:
  0.0 251.3 jit_solution(12892263405917048331)
XLA Ops:
  17.8 3.6 %reshape.41 = bf16[64,3,4,896]{3,2,1,0:T(4,128)(2,1)} reshape(bf16[768,896]{1,0:T(8,128)(2,1)} %copy-done.23) | data formatting | bytes 2752512 | tf_op jit(solution)/shard_map/reshape | solution.py:523
  21.4 12.3 %all-to-all-start = ((bf16[64,3,4,896]{3,2,1,0:T(4,128)(2,1)}), bf16[64,3,4,896]{3,2,1,0:T(4,128)(2,1)}, u32[]{:S(2)}, u32[]{:S(2)}) async-start(bf16[64,3,4,896]{3,2,1,0:T(4,128)(2,1)} %reshape.41), calls=%async_computation | async-start | bytes 2752512 | tf_op jit(solution)/shard_map/all_to_all | solution.py:522
  35.4 3.6 %reshape.43 = bf16[64,3,4,896]{3,2,1,0:T(4,128)(2,1)} reshape(bf16[768,896]{1,0:T(8,128)(2,1)} %copy-done.24) | data formatting | bytes 2752512 | tf_op jit(solution)/shard_map/reshape | solution.py:523
  38.9 30.3 %all-to-all-done = bf16[64,3,4,896]{3,2,1,0:T(4,128)(2,1)} async-done(((bf16[64,3,4,896]{3,2,1,0:T(4,128)(2,1)}), bf16[64,3,4,896]{3,2,1,0:T(4,128)(2,1)}, u32[]{:S(2)}, u32[]{:S(2)}) %all-to-all-start) | async-done | bytes 1376288 | tf_op jit(solution)/shard_map/all_to_all | solution.py:522
  69.3 6.3 %all-to-all-start.1 = ((bf16[64,3,4,896]{3,2,1,0:T(4,128)(2,1)}), bf16[64,3,4,896]{3,2,1,0:T(4,128)(2,1)}, u32[]{:S(2)}, u32[]{:S(2)}) async-start(bf16[64,3,4,896]{3,2,1,0:T(4,128)(2,1)} %reshape.43), calls=%async_computation.1 | async-start | bytes 2752512 | tf_op jit(solution)/shard_map/all_to_all | solution.py:522
  75.6 3.5 %reshape.42.rows_ref = bf16[768,896]{1,0:T(8,128)(2,1)} reshape(bf16[64,3,4,896]{3,2,1,0:T(4,128)(2,1)} %all-to-all-done) | data formatting | bytes 2752512 | tf_op jit(solution)/shard_map/reshape | solution.py:550
  88.6 11.6 %collective-permute-done.4.refs_2_ = bf16[384,896]{1,0:T(8,128)(2,1)} collective-permute-done((bf16[384,896]{1,0:T(8,128)(2,1)S(1)}, bf16[384,896]{1,0:T(8,128)(2,1)}, u32[]{:S(2)}, u32[]{:S(2)}) %collective-permute-start.4) | collective-permute-done | bytes 688160 | tf_op jit(solution)/shard_map/ppermute | solution.py:514
  102.9 8.3 %all-to-all-done.1 = bf16[64,3,4,896]{3,2,1,0:T(4,128)(2,1)} async-done(((bf16[64,3,4,896]{3,2,1,0:T(4,128)(2,1)}), bf16[64,3,4,896]{3,2,1,0:T(4,128)(2,1)}, u32[]{:S(2)}, u32[]{:S(2)}) %all-to-all-start.1) | async-done | bytes 1376288 | tf_op jit(solution)/shard_map/all_to_all | solution.py:522
  111.1 3.7 %collective-permute-done.5.refs_3_ = bf16[384,896]{1,0:T(8,128)(2,1)S(1)} collective-permute-done((bf16[384,896]{1,0:T(8,128)(2,1)}, bf16[384,896]{1,0:T(8,128)(2,1)S(1)}, u32[]{:S(2)}, u32[]{:S(2)}) %collective-permute-start.5) | collective-permute-done | bytes 688160 | tf_op jit(solution)/shard_map/ppermute | solution.py:514
  120.9 3.7 %shard_map.123 = (f32[768,256]{1,0:T(8,128)S(1)}, bf16[768,256]{1,0:T(8,128)(2,1)S(1)}, bf16[768,256]{1,0:T(8,128)(2,1)S(1)}, bf16[768,256]{1,0:T(8,128)(2,1)S(1)}) custom-call(s32[1]{0:T(128)} %bitcast.3.at_ref, bf16[768,896]{1,0:T(8,128)(2,1)S(1)} %reshape.44.rows_ref, bf16[256,3584]{1,0:T(8,128)(2,1)S(1)} %bitcast.20, bf16[2688,256]{1,0:T(8,128)(2,1)S(1)} %copy-done.7, ...), custom_call_target="tpu_custom_call" | custom-call | flops 1409286144 | bytes 5000000 | tf_op jit(solution)/shard_map/pallas_call | solution.py:271
  134.0 4.9 %shard_map.125.sum_ref = f32[768,512]{1,0:T(8,128)S(1)} custom-call(s32[1]{0:T(128)} %bitcast.3.at_ref, bf16[384,896]{1,0:T(8,128)(2,1)S(1)} %copy-done.13, bf16[384,896]{1,0:T(8,128)(2,1)} %get-tuple-element.83.refs_1_, bf16[384,896]{1,0:T(8,128)(2,1)} %collective-permute-done.4.refs_2_, bf16[384,896]{1,0:T(8,128)(2,1)S(1)} %copy-done.15, ...), custom_call_target="tpu_custom_call" | custom-call | flops 2113929216 | bytes 9000000 | tf_op jit(solution)/shard_map/pallas_call | solution.py:211
  139.0 4.2 %shard_map.126 = (bf16[768,256]{1,0:T(8,128)(2,1)}, f32[768,256]{1,0:T(8,128)S(1)}, f32[768,256]{1,0:T(8,128)S(1)}) custom-call(s32[1]{0:T(128)} %bitcast.3.at_ref, bf16[384,896]{1,0:T(8,128)(2,1)} %collective-permute-done.11.low.refs_0_, bf16[384,896]{1,0:T(8,128)(2,1)} %collective-permute-done.12.high.refs_1_, f32[768,512]{1,0:T(8,128)S(1)} %shard_map.125.sum_ref, ...), custom_call_target="tpu_custom_call" | custom-call | flops 704643072 | bytes 4000000 | tf_op jit(solution)/shard_map/pallas_call | solution.py:240
  143.2 3.2 %collective-permute-done.10.r3 = bf16[768,256]{1,0:T(8,128)(2,1)S(1)} collective-permute-done((bf16[768,256]{1,0:T(8,128)(2,1)S(1)}, bf16[768,256]{1,0:T(8,128)(2,1)S(1)}, u32[]{:S(2)}, u32[]{:S(2)}) %collective-permute-start.10) | collective-permute-done | bytes 393248 | tf_op jit(solution)/shard_map/ppermute | solution.py:514
  154.8 5.1 %collective-permute-done.13.refs_2_ = bf16[384,512]{1,0:T(8,128)(2,1)S(1)} collective-permute-done((bf16[384,512]{1,0:T(8,128)(2,1)S(1)}, bf16[384,512]{1,0:T(8,128)(2,1)S(1)}, u32[]{:S(2)}, u32[]{:S(2)}) %collective-permute-start.13) | collective-permute-done | bytes 393248 | tf_op jit(solution)/shard_map/ppermute | solution.py:514
  162.5 5.7 %collective-permute-done.14.refs_3_ = bf16[384,512]{1,0:T(8,128)(2,1)S(1)} collective-permute-done((bf16[384,512]{1,0:T(8,128)(2,1)S(1)}, bf16[384,512]{1,0:T(8,128)(2,1)S(1)}, u32[]{:S(2)}, u32[]{:S(2)}) %collective-permute-start.14) | collective-permute-done | bytes 393248 | tf_op jit(solution)/shard_map/ppermute | solution.py:514
  173.8 5.3 %shard_map.129.refs_8_ = f32[768,896]{1,0:T(8,128)S(1)} custom-call(s32[1]{0:T(128)} %bitcast.3.at_ref, bf16[384,512]{1,0:T(8,128)(2,1)S(1)} %get-tuple-element.108.refs_0_.low_ref, bf16[384,512]{1,0:T(8,128)(2,1)S(1)} %get-tuple-element.109.refs_1_.high_ref, bf16[384,512]{1,0:T(8,128)(2,1)S(1)} %collective-permute-done.13.refs_2_, ...), custom_call_target="tpu_custom_call" | custom-call | flops 2113929216 | bytes 8000000 | tf_op jit(solution)/shard_map/pallas_call | solution.py:368
  182.4 19.7 %all-to-all-start.2 = ((bf16[64,3,4,896]{3,2,1,0:T(4,128)(2,1)}), bf16[64,3,4,896]{3,2,1,0:T(4,128)(2,1)}, u32[]{:S(2)}, u32[]{:S(2)}) async-start(bf16[64,3,4,896]{3,2,1,0:T(4,128)(2,1)} %reshape.45), calls=%async_computation.2 | async-start | bytes 2752512 | tf_op jit(solution)/shard_map/all_to_all | solution.py:522
  202.2 4.6 %shard_map.135.mine_ref = bf16[1024,896]{1,0:T(8,128)(2,1)} custom-call(bf16[768,256]{1,0:T(8,128)(2,1)} %get-tuple-element.112.hid_ref.h0, bf16[768,256]{1,0:T(8,128)(2,1)} %collective-permute-done.21.h1, bf16[768,256]{1,0:T(8,128)(2,1)} %collective-permute-done.22.h2, bf16[768,256]{1,0:T(8,128)(2,1)} %collective-permute-done.23.h3, ...), custom_call_target="tpu_custom_call" | custom-call | flops 40000000000 | bytes 5000000 | tf_op jit(solution)/shard_map/pallas_call | solution.py:459
  207.3 6.8 %shard_map.132 = (bf16[3584,256]{1,0:T(8,128)(2,1)S(1)}, bf16[3584,256]{1,0:T(8,128)(2,1)}) custom-call(s32[1]{0:T(128)} %bitcast.3.at_ref, bf16[896,768]{1,0:T(8,128)(2,1)S(1)} %copy-done.34, bf16[896,768]{1,0:T(8,128)(2,1)S(1)} %copy-done.36, bf16[896,768]{1,0:T(8,128)(2,1)S(1)} %copy-done.38, bf16[896,768]{1,0:T(8,128)(2,1)S(1)} %copy-done.21, ...), custom_call_target="tpu_custom_call" | custom-call | flops 2818572288 | bytes 11000000 | tf_op jit(solution)/shard_map/pallas_call | solution.py:440
  219.1 3.6 %collective-permute-start.25 = (bf16[256,896]{1,0:T(8,128)(2,1)S(1)}, bf16[256,896]{1,0:T(8,128)(2,1)S(1)}, u32[]{:S(2)}, u32[]{:S(2)}) collective-permute-start(bf16[256,896]{1,0:T(8,128)(2,1)S(1)} %get-tuple-element.114), channel_id=1, source_target_pairs={{0,192},{64,0},{128,64},{192,128},{1,193},{65,1},{129,65},{193,129... | collective-permute-start | bytes 1376264 | tf_op jit(solution)/shard_map/ppermute | solution.py:514
  223.5 5.6 %shard_map.134 = bf16[3584,256]{1,0:T(8,128)(2,1)} custom-call(s32[1]{0:T(128)S(6)} %convert_element_type.8.same_ref, bf16[3584,256]{1,0:T(8,128)(2,1)} %get-tuple-element.111.mine_ref, bf16[3584,256]{1,0:T(8,128)(2,1)} %collective-permute-done.20.other_ref), custom_call_target="tpu_custom_call" | custom-call | tf_op jit(solution)/shard_map/pallas_call | solution.py:484
  229.1 5.3 %shard_map.133 = bf16[3584,256]{1,0:T(8,128)(2,1)} custom-call(s32[1]{0:T(128)S(6)} %convert_element_type.8.same_ref, bf16[3584,256]{1,0:T(8,128)(2,1)S(1)} %get-tuple-element.110.mine_ref, bf16[3584,256]{1,0:T(8,128)(2,1)} %collective-permute-done.19.other_ref), custom_call_target="tpu_custom_call" | custom-call | tf_op jit(solution)/shard_map/pallas_call | solution.py:484
  234.4 8.2 %collective-permute-done.25.p1 = bf16[256,896]{1,0:T(8,128)(2,1)S(1)} collective-permute-done((bf16[256,896]{1,0:T(8,128)(2,1)S(1)}, bf16[256,896]{1,0:T(8,128)(2,1)S(1)}, u32[]{:S(2)}, u32[]{:S(2)}) %collective-permute-start.25) | collective-permute-done | bytes 458784 | tf_op jit(solution)/shard_map/ppermute | solution.py:514
  242.6 3.5 %collective-permute-done.27.p3 = bf16[256,896]{1,0:T(8,128)(2,1)S(1)} collective-permute-done((bf16[256,896]{1,0:T(8,128)(2,1)S(1)}, bf16[256,896]{1,0:T(8,128)(2,1)S(1)}, u32[]{:S(2)}, u32[]{:S(2)}) %collective-permute-start.27) | collective-permute-done | bytes 458784 | tf_op jit(solution)/shard_map/ppermute | solution.py:514
  (153 shorter events, 76.2 us)
Async XLA Ops:
  7.6 71.5 %collective-permute-start.1 = (bf16[2688,256]{1,0:T(8,128)(2,1)}, bf16[2688,256]{1,0:T(8,128)(2,1)S(1)}, u32[]{:S(2)}, u32[]{:S(2)}) collective-permute-start(bf16[2688,256]{1,0:T(8,128)(2,1)} %get-tuple-element.64), channel_id=1, source_target_pairs={{0,64},{64,128},{128,192},{192,0},{1,65},{65,129},{129,193},{193,1... | collective-permute-start | bytes 4128776 | tf_op jit(solution)/shard_map/ppermute | solution.py:514
  11.6 67.5 %collective-permute-start.2 = (bf16[2688,256]{1,0:T(8,128)(2,1)}, bf16[2688,256]{1,0:T(8,128)(2,1)S(1)}, u32[]{:S(2)}, u32[]{:S(2)}) collective-permute-start(bf16[2688,256]{1,0:T(8,128)(2,1)} %get-tuple-element.66), channel_id=1, source_target_pairs={{0,128},{64,192},{128,0},{192,64},{1,129},{65,193},{129,1},{193,65... | collective-permute-start | bytes 4128776 | tf_op jit(solution)/shard_map/ppermute | solution.py:514
  14.0 65.1 %collective-permute-start.3 = (bf16[2688,256]{1,0:T(8,128)(2,1)}, bf16[2688,256]{1,0:T(8,128)(2,1)}, u32[]{:S(2)}, u32[]{:S(2)}) collective-permute-start(bf16[2688,256]{1,0:T(8,128)(2,1)} %get-tuple-element.67), channel_id=1, source_target_pairs={{0,192},{64,0},{128,64},{192,128},{1,193},{65,1},{129,65},{193,129... | collective-permute-start | bytes 4128776 | tf_op jit(solution)/shard_map/ppermute | solution.py:514
  21.4 47.9 %all-to-all-start = ((bf16[64,3,4,896]{3,2,1,0:T(4,128)(2,1)}), bf16[64,3,4,896]{3,2,1,0:T(4,128)(2,1)}, u32[]{:S(2)}, u32[]{:S(2)}) async-start(bf16[64,3,4,896]{3,2,1,0:T(4,128)(2,1)} %reshape.41), calls=%async_computation | async-start | bytes 2752512 | tf_op jit(solution)/shard_map/all_to_all | solution.py:522
  69.3 41.8 %all-to-all-start.1 = ((bf16[64,3,4,896]{3,2,1,0:T(4,128)(2,1)}), bf16[64,3,4,896]{3,2,1,0:T(4,128)(2,1)}, u32[]{:S(2)}, u32[]{:S(2)}) async-start(bf16[64,3,4,896]{3,2,1,0:T(4,128)(2,1)} %reshape.43), calls=%async_computation.1 | async-start | bytes 2752512 | tf_op jit(solution)/shard_map/all_to_all | solution.py:522
  82.4 17.8 %collective-permute-start.4 = (bf16[384,896]{1,0:T(8,128)(2,1)S(1)}, bf16[384,896]{1,0:T(8,128)(2,1)}, u32[]{:S(2)}, u32[]{:S(2)}) collective-permute-start(bf16[384,896]{1,0:T(8,128)(2,1)S(1)} %get-tuple-element.82.refs_0_), channel_id=1, source_target_pairs={{0,64},{64,128},{128,192},{192,0},{1,65},{65,129},{129,193},{193,1... | collective-permute-start | bytes 2064392 | tf_op jit(solution)/shard_map/ppermute | solution.py:514
  82.8 17.4 %collective-permute-start.7 = (bf16[384,896]{1,0:T(8,128)(2,1)}, bf16[384,896]{1,0:T(8,128)(2,1)}, u32[]{:S(2)}, u32[]{:S(2)}) collective-permute-start(bf16[384,896]{1,0:T(8,128)(2,1)} %get-tuple-element.83.refs_1_), channel_id=1, source_target_pairs={{0,192},{64,0},{128,64},{192,128},{1,193},{65,1},{129,65},{193,129... | collective-permute-start | bytes 2064392 | tf_op jit(solution)/shard_map/ppermute | solution.py:514
  85.1 29.8 %collective-permute-start.5 = (bf16[384,896]{1,0:T(8,128)(2,1)}, bf16[384,896]{1,0:T(8,128)(2,1)S(1)}, u32[]{:S(2)}, u32[]{:S(2)}) collective-permute-start(bf16[384,896]{1,0:T(8,128)(2,1)} %get-tuple-element.83.refs_1_), channel_id=1, source_target_pairs={{0,64},{64,128},{128,192},{192,0},{1,65},{65,129},{129,193},{193,1... | collective-permute-start | bytes 2064392 | tf_op jit(solution)/shard_map/ppermute | solution.py:514
  85.1 30.6 %collective-permute-start.6 = (bf16[384,896]{1,0:T(8,128)(2,1)S(1)}, bf16[384,896]{1,0:T(8,128)(2,1)}, u32[]{:S(2)}, u32[]{:S(2)}) collective-permute-start(bf16[384,896]{1,0:T(8,128)(2,1)S(1)} %get-tuple-element.82.refs_0_), channel_id=1, source_target_pairs={{0,192},{64,0},{128,64},{192,128},{1,193},{65,1},{129,65},{193,129... | collective-permute-start | bytes 2064392 | tf_op jit(solution)/shard_map/ppermute | solution.py:514
  100.2 38.8 %collective-permute-start.11 = (bf16[384,896]{1,0:T(8,128)(2,1)}, bf16[384,896]{1,0:T(8,128)(2,1)}, u32[]{:S(2)}, u32[]{:S(2)}) collective-permute-start(bf16[384,896]{1,0:T(8,128)(2,1)} %collective-permute-done.4.refs_2_), channel_id=1, source_target_pairs={{0,64},{64,128},{128,192},{192,0},{1,65},{65,129},{129,193},{193,1... | collective-permute-start | bytes 2064392 | tf_op jit(solution)/shard_map/ppermute | solution.py:514
  100.2 38.8 %collective-permute-start.12 = (bf16[384,896]{1,0:T(8,128)(2,1)}, bf16[384,896]{1,0:T(8,128)(2,1)}, u32[]{:S(2)}, u32[]{:S(2)}) collective-permute-start(bf16[384,896]{1,0:T(8,128)(2,1)} %collective-permute-done.7.refs_5_), channel_id=1, source_target_pairs={{0,192},{64,0},{128,64},{192,128},{1,193},{65,1},{129,65},{193,129... | collective-permute-start | bytes 2064392 | tf_op jit(solution)/shard_map/ppermute | solution.py:514
  124.6 21.8 %collective-permute-start.10 = (bf16[768,256]{1,0:T(8,128)(2,1)S(1)}, bf16[768,256]{1,0:T(8,128)(2,1)S(1)}, u32[]{:S(2)}, u32[]{:S(2)}) collective-permute-start(bf16[768,256]{1,0:T(8,128)(2,1)S(1)} %get-tuple-element.81), channel_id=1, source_target_pairs={{0,64},{64,128},{128,192},{192,0},{1,65},{65,129},{129,193},{193,1... | collective-permute-start | bytes 1179656 | tf_op jit(solution)/shard_map/ppermute | solution.py:514
  124.7 21.7 %collective-permute-start.8 = (bf16[768,256]{1,0:T(8,128)(2,1)S(1)}, bf16[768,256]{1,0:T(8,128)(2,1)S(1)}, u32[]{:S(2)}, u32[]{:S(2)}) collective-permute-start(bf16[768,256]{1,0:T(8,128)(2,1)S(1)} %get-tuple-element.79), channel_id=1, source_target_pairs={{0,128},{64,192},{128,0},{192,64},{1,129},{65,193},{129,1},{193,65... | collective-permute-start | bytes 1179656 | tf_op jit(solution)/shard_map/ppermute | solution.py:514
  127.7 18.7 %collective-permute-start.9 = (bf16[768,256]{1,0:T(8,128)(2,1)S(1)}, bf16[768,256]{1,0:T(8,128)(2,1)S(1)}, u32[]{:S(2)}, u32[]{:S(2)}) collective-permute-start(bf16[768,256]{1,0:T(8,128)(2,1)S(1)} %get-tuple-element.80), channel_id=1, source_target_pairs={{0,192},{64,0},{128,64},{192,128},{1,193},{65,1},{129,65},{193,129... | collective-permute-start | bytes 1179656 | tf_op jit(solution)/shard_map/ppermute | solution.py:514
  152.1 18.4 %collective-permute-start.15 = (bf16[384,512]{1,0:T(8,128)(2,1)S(1)}, bf16[384,512]{1,0:T(8,128)(2,1)S(1)}, u32[]{:S(2)}, u32[]{:S(2)}) collective-permute-start(bf16[384,512]{1,0:T(8,128)(2,1)S(1)} %get-tuple-element.108.refs_0_.low_ref), channel_id=1, source_target_pairs={{0,192},{64,0},{128,64},{192,128},{1,193},{65,1},{129,65},{193,129... | collective-permute-start | bytes 1179656 | tf_op jit(solution)/shard_map/ppermute | solution.py:514
  159.9 19.3 %collective-permute-start.17 = (bf16[384,512]{1,0:T(8,128)(2,1)S(1)}, bf16[384,512]{1,0:T(8,128)(2,1)S(1)}, u32[]{:S(2)}, u32[]{:S(2)}) collective-permute-start(bf16[384,512]{1,0:T(8,128)(2,1)S(1)} %collective-permute-done.13.refs_2_), channel_id=1, source_target_pairs={{0,64},{64,128},{128,192},{192,0},{1,65},{65,129},{129,193},{193,1... | collective-permute-start | bytes 1179656 | tf_op jit(solution)/shard_map/ppermute | solution.py:514
  159.9 19.3 %collective-permute-start.18 = (bf16[384,512]{1,0:T(8,128)(2,1)S(1)}, bf16[384,512]{1,0:T(8,128)(2,1)S(1)}, u32[]{:S(2)}, u32[]{:S(2)}) collective-permute-start(bf16[384,512]{1,0:T(8,128)(2,1)S(1)} %collective-permute-done.16.refs_5_), channel_id=1, source_target_pairs={{0,192},{64,0},{128,64},{192,128},{1,193},{65,1},{129,65},{193,129... | collective-permute-start | bytes 1179656 | tf_op jit(solution)/shard_map/ppermute | solution.py:514
  168.3 33.8 %collective-permute-start.21 = (bf16[768,256]{1,0:T(8,128)(2,1)}, bf16[768,256]{1,0:T(8,128)(2,1)}, u32[]{:S(2)}, u32[]{:S(2)}) collective-permute-start(bf16[768,256]{1,0:T(8,128)(2,1)} %get-tuple-element.112.hid_ref.h0), channel_id=1, source_target_pairs={{0,64},{64,128},{128,192},{192,0},{1,65},{65,129},{129,193},{193,1... | collective-permute-start | bytes 1179656 | tf_op jit(solution)/shard_map/ppermute | solution.py:514
  168.3 33.9 %collective-permute-start.22 = (bf16[768,256]{1,0:T(8,128)(2,1)}, bf16[768,256]{1,0:T(8,128)(2,1)}, u32[]{:S(2)}, u32[]{:S(2)}) collective-permute-start(bf16[768,256]{1,0:T(8,128)(2,1)} %get-tuple-element.112.hid_ref.h0), channel_id=1, source_target_pairs={{0,128},{64,192},{128,0},{192,64},{1,129},{65,193},{129,1},{193,65... | collective-permute-start | bytes 1179656 | tf_op jit(solution)/shard_map/ppermute | solution.py:514
  170.5 31.6 %collective-permute-start.23 = (bf16[768,256]{1,0:T(8,128)(2,1)}, bf16[768,256]{1,0:T(8,128)(2,1)}, u32[]{:S(2)}, u32[]{:S(2)}) collective-permute-start(bf16[768,256]{1,0:T(8,128)(2,1)} %get-tuple-element.112.hid_ref.h0), channel_id=1, source_target_pairs={{0,192},{64,0},{128,64},{192,128},{1,193},{65,1},{129,65},{193,129... | collective-permute-start | bytes 1179656 | tf_op jit(solution)/shard_map/ppermute | solution.py:514
  182.4 65.0 %all-to-all-start.2 = ((bf16[64,3,4,896]{3,2,1,0:T(4,128)(2,1)}), bf16[64,3,4,896]{3,2,1,0:T(4,128)(2,1)}, u32[]{:S(2)}, u32[]{:S(2)}) async-start(bf16[64,3,4,896]{3,2,1,0:T(4,128)(2,1)} %reshape.45), calls=%async_computation.2 | async-start | bytes 2752512 | tf_op jit(solution)/shard_map/all_to_all | solution.py:522
  219.1 23.4 %collective-permute-start.25 = (bf16[256,896]{1,0:T(8,128)(2,1)S(1)}, bf16[256,896]{1,0:T(8,128)(2,1)S(1)}, u32[]{:S(2)}, u32[]{:S(2)}) collective-permute-start(bf16[256,896]{1,0:T(8,128)(2,1)S(1)} %get-tuple-element.114), channel_id=1, source_target_pairs={{0,192},{64,0},{128,64},{192,128},{1,193},{65,1},{129,65},{193,129... | collective-permute-start | bytes 1376264 | tf_op jit(solution)/shard_map/ppermute | solution.py:514
  222.8 19.8 %collective-permute-start.26 = (bf16[256,896]{1,0:T(8,128)(2,1)S(1)}, bf16[256,896]{1,0:T(8,128)(2,1)S(1)}, u32[]{:S(2)}, u32[]{:S(2)}) collective-permute-start(bf16[256,896]{1,0:T(8,128)(2,1)S(1)} %get-tuple-element.115), channel_id=1, source_target_pairs={{0,128},{64,192},{128,0},{192,64},{1,129},{65,193},{129,1},{193,65... | collective-permute-start | bytes 1376264 | tf_op jit(solution)/shard_map/ppermute | solution.py:514
  222.8 23.2 %collective-permute-start.27 = (bf16[256,896]{1,0:T(8,128)(2,1)S(1)}, bf16[256,896]{1,0:T(8,128)(2,1)S(1)}, u32[]{:S(2)}, u32[]{:S(2)}) collective-permute-start(bf16[256,896]{1,0:T(8,128)(2,1)S(1)} %get-tuple-element.116), channel_id=1, source_target_pairs={{0,64},{64,128},{128,192},{192,0},{1,65},{65,129},{129,193},{193,1... | collective-permute-start | bytes 1376264 | tf_op jit(solution)/shard_map/ppermute | solution.py:514
  (50 other events, 357.6 us)

commit v3 on v2

--- a/solution.py
+++ b/solution.py
@@ -157,29 +157,47 @@
     return pl.multiple_of(lax.rem(at_ref[0] + rel, N_DP) * QUARTER, 128)
 
 
-def weights_kernel(at_ref, wg_ref, wu_ref, wd_ref, *refs):
-    for b, out in zip((1, 2, 3), refs):
+def weights_kernel(at_ref, wg_ref, wu_ref, wd_ref, o1, o2, o3, down, sems):
+    copies = []
+    for b, out in zip((1, 2, 3), (o1, o2, o3)):
         where = pl.ds(offset(at_ref, b), QUARTER)
-        out[:QUARTER, :] = wg_ref[where, :]
-        out[QUARTER:2 * QUARTER, :] = wu_ref[where, :]
-        out[2 * QUARTER:, :] = wd_ref[:, where].T
+        for i, (src, dst) in enumerate((
+            (wd_ref.at[:, where], down.at[b - 1]),
+            (wg_ref.at[where, :], out.at[pl.ds(0, QUARTER), :]),
+            (wu_ref.at[where, :], out.at[pl.ds(QUARTER, QUARTER), :]),
+        )):
+            copies.append(pltpu.make_async_copy(src, dst, sems.at[b - 1, i]))
+    for copy in copies:
+        copy.start()
+    for b, out in zip((1, 2, 3), (o1, o2, o3)):
+        copies[3 * b - 3].wait()
+        out[2 * QUARTER:, :] = down[b - 1].T
+    for i, copy in enumerate(copies):
+        if i % 3:
+            copy.wait()
 
 
 def weights(at, wg, wu, wd):
     whole = pl.BlockSpec(memory_space=VMEM)
+    stays = pl.BlockSpec(memory_space=pl.ANY)
     return pl.pallas_call(
         weights_kernel,
         out_shape=(jax.ShapeDtypeStruct((3 * QUARTER, SHARE), BF16),) * 3,
-        in_specs=[pl.BlockSpec(memory_space=pltpu.SMEM), whole, whole, whole],
+        in_specs=[pl.BlockSpec(memory_space=pltpu.SMEM), stays, stays, stays],
         out_specs=(whole,) * 3,
-        compiler_params=params(24),
+        scratch_shapes=[pltpu.VMEM((3, SHARE, QUARTER), BF16), pltpu.SemaphoreType.DMA((3, 3))],
+        compiler_params=params(56),
         cost_estimate=pl.CostEstimate(flops=0, bytes_accessed=9_600_000, transcendentals=0),
     )(at, wg, wu, wd)
 
 
-def halves_kernel(rows_ref, a1, a2, a3, a4, low_ref, high_ref):
-    low_ref[...] = rows_ref[:HALF, :]
-    high_ref[...] = rows_ref[HALF:, :]
+def halves_kernel(rows_ref, a1, a2, a3, a4, low_ref, high_ref, sems):
+    low = pltpu.make_async_copy(rows_ref.at[pl.ds(0, HALF), :], low_ref, sems.at[0])
+    high = pltpu.make_async_copy(rows_ref.at[pl.ds(HALF, HALF), :], high_ref, sems.at[1])
+    low.start()
+    high.start()
+    low.wait()
+    high.wait()
 
 
 def halves(rows, after):
@@ -187,9 +205,10 @@
     return pl.pallas_call(
         halves_kernel,
         out_shape=(jax.ShapeDtypeStruct((HALF, QUARTER), BF16),) * 2,
-        in_specs=[whole] + [pl.BlockSpec(memory_space=pl.ANY)] * 4,
+        in_specs=[pl.BlockSpec(memory_space=pl.ANY)] * 5,
         out_specs=(whole,) * 2,
-        compiler_params=params(16),
+        scratch_shapes=[pltpu.SemaphoreType.DMA((2,))],
+        compiler_params=params(56),
         cost_estimate=pl.CostEstimate(flops=HEAVY, bytes_accessed=2_800_000, transcendentals=0),
     )(rows, *after)
 
@@ -280,7 +299,7 @@
             ],
             out_specs=(tile,) * 4,
         ),
-        compiler_params=params(32),
+        compiler_params=params(56),
         cost_estimate=pl.CostEstimate(
             flops=2 * PADDED * WIDTH * SHARE, bytes_accessed=5_000_000, transcendentals=0
         ),
@@ -292,7 +311,7 @@
     return number - BLOCK * jnp.floor((number + 0.5) * (1.0 / BLOCK))
 
 
-def slopes_kernel(own, r1, r2, r3, hid_ref, act_ref, ups_ref, low_ref, high_ref):
+def slopes_kernel(own, r1, r2, r3, hid_ref, act_ref, ups_ref, out_ref):
     d_hidden = own[...] + r1[...].astype(F32) + r2[...].astype(F32) + r3[...].astype(F32)
     dg = d_hidden * ups_ref[...]
     du = d_hidden * act_ref[...]
@@ -306,29 +325,18 @@
     spare = within_block((TILE, SHARE)) == CAP
     group = jnp.where(col >= start, jnp.where(col < start + BLOCK, 1.0, 0.0), 0.0).astype(BF16)
     moved = jnp.concatenate([dot(group, high), dot(group, rest)], axis=1)
-    both = jnp.concatenate([jnp.where(spare, moved, dg), du], axis=1).astype(BF16)
-    m = pl.program_id(0)
-
-    @pl.when(m < TILES // 2)
-    def _():
-        low_ref[...] = both
-
-    @pl.when(m >= TILES // 2)
-    def _():
-        high_ref[...] = both
+    out_ref[:, :SHARE] = jnp.where(spare, moved, dg).astype(BF16)
+    out_ref[:, SHARE:] = du.astype(BF16)
 
 
 def slopes(own, others, hid, act, ups):
     tile = pl.BlockSpec((TILE, SHARE), lambda m: (m, 0))
     return pl.pallas_call(
         slopes_kernel,
-        out_shape=(jax.ShapeDtypeStruct((HALF, 2 * SHARE), BF16),) * 2,
+        out_shape=jax.ShapeDtypeStruct((PADDED, 2 * SHARE), BF16),
         grid=(TILES,),
         in_specs=[tile] * 7,
-        out_specs=(
-            pl.BlockSpec((TILE, 2 * SHARE), lambda m: (jnp.minimum(m, TILES // 2 - 1), 0)),
-            pl.BlockSpec((TILE, 2 * SHARE), lambda m: (jnp.maximum(m - TILES // 2, 0), 0)),
-        ),
+        out_specs=pl.BlockSpec((TILE, 2 * SHARE), lambda m: (m, 0)),
         compiler_params=params(24),
         cost_estimate=pl.CostEstimate(flops=50_000_000, bytes_accessed=5_000_000, transcendentals=0),
     )(own, *others, hid, act, ups)
@@ -338,18 +346,15 @@
     return dot(slope[:, :SHARE], blocks[0], 1, 1) + dot(slope[:, SHARE:], blocks[1], 1, 1)
 
 
-def back_near_kernel(at_ref, *refs):
-    wg_ref, wu_ref, g1, g3, out_ref = refs[6:]
-    own, below, above = this_tile(refs[:6])
+def back_near_kernel(at_ref, own, below, above, wg_ref, wu_ref, g1, g3, out_ref):
     total = product(own, (wg_ref[...], wu_ref[...]))
     for slope, g in ((below, g1), (above, g3)):
         total = total + product(slope, (g[:QUARTER, :], g[QUARTER:, :]))
     out_ref[...] = total
 
 
-def back_kernel(at_ref, *refs):
-    sum_ref, g2, out_ref = refs[8:]
-    own, below, above, far = this_tile(refs[:8])
+def back_kernel(at_ref, own, below, above, low, high, sum_ref, g2, out_ref):
+    far = this_tile((low, high))[0]
     total = sum_ref[...] + product(far, (g2[:QUARTER, :], g2[QUARTER:, :]))
     out_ref[...] = total.astype(BF16)
     parts = [s[:, :SHARE].astype(F32) for s in (own, below, above, far)]
@@ -363,6 +368,7 @@
 
 
 def back_near(at, parts, wg, wu, blocks):
+    slope = pl.BlockSpec((TILE, 2 * SHARE), lambda m, at: (m, 0))
     mine = pl.BlockSpec((QUARTER, SHARE), lambda m, at: (at[0], 0))
     both = pl.BlockSpec((2 * QUARTER, SHARE), lambda m, at: (0, 0))
     return pl.pallas_call(
@@ -370,7 +376,7 @@
         out_shape=jax.ShapeDtypeStruct((PADDED, QUARTER), F32),
         grid_spec=pltpu.PrefetchScalarGridSpec(
             num_scalar_prefetch=1, grid=(TILES,),
-            in_specs=half_specs(2 * SHARE) * 3 + [mine, mine, both, both],
+            in_specs=[slope] * 3 + [mine, mine, both, both],
             out_specs=pl.BlockSpec((TILE, QUARTER), lambda m, at: (m, 0)),
         ),
         compiler_params=params(32),
@@ -382,13 +388,14 @@
 
 def back_rows(at, parts, summed, block):
     both = pl.BlockSpec((2 * QUARTER, SHARE), lambda m, at: (0, 0))
+    slope = pl.BlockSpec((TILE, 2 * SHARE), lambda m, at: (m, 0))
     tile = pl.BlockSpec((TILE, QUARTER), lambda m, at: (m, 0))
     return pl.pallas_call(
         back_kernel,
         out_shape=jax.ShapeDtypeStruct((PADDED, QUARTER), BF16),
         grid_spec=pltpu.PrefetchScalarGridSpec(
             num_scalar_prefetch=1, grid=(TILES,),
-            in_specs=half_specs(2 * SHARE) * 4 + [tile, both], out_specs=tile,
+            in_specs=[slope] * 3 + half_specs(2 * SHARE) + [tile, both], out_specs=tile,
         ),
         compiler_params=params(32),
         cost_estimate=pl.CostEstimate(
@@ -419,8 +426,8 @@
     )(*parts)
 
 
-def grads_kernel(at_ref, x0, x1, x2, x3, low_ref, high_ref, gg_ref, gu_ref):
-    slope = jnp.concatenate([low_ref[...], high_ref[...]], axis=0)
+def grads_kernel(at_ref, x0, x1, x2, x3, slope_ref, gg_ref, gu_ref):
+    slope = slope_ref[...]
     step = QUARTER // 4
     for rel, x in zip((0, 3, 1, 2), (x0, x1, x2, x3)):
         base = offset(at_ref, rel)
@@ -440,27 +447,27 @@
     return pl.pallas_call(
         grads_kernel,
         out_shape=(jax.ShapeDtypeStruct((WIDTH, SHARE), BF16),) * 2,
-        in_specs=[pl.BlockSpec(memory_space=pltpu.SMEM)] + [whole] * 6,
+        in_specs=[pl.BlockSpec(memory_space=pltpu.SMEM)] + [whole] * 5,
         out_specs=(whole,) * 2,
         compiler_params=params(32),
         cost_estimate=pl.CostEstimate(
             flops=4 * PADDED * WIDTH * SHARE, bytes_accessed=11_000_000, transcendentals=0
         ),
-    )(at, *xs, *slope)
-
-
-def down_kernel(h0, h1, h2, h3, rows_ref, out_ref):
-    for b, h in enumerate((h0, h1, h2, h3)):
-        out_ref[b * SHARE:(b + 1) * SHARE, :] = dot(h[...], rows_ref[...], 0, 0).astype(BF16)
+    )(at, *xs, slope)
+
+
+def down_kernel(h0, h1, h2, h3, rows_ref, *outs):
+    for h, out in zip((h0, h1, h2, h3), outs):
+        out[...] = dot(h[...], rows_ref[...], 0, 0).astype(BF16)
 
 
 def down_grads(hids, rows):
     whole = pl.BlockSpec(memory_space=VMEM)
     return pl.pallas_call(
         down_kernel,
-        out_shape=jax.ShapeDtypeStruct((N_DP * SHARE, QUARTER), BF16),
+        out_shape=(jax.ShapeDtypeStruct((SHARE, QUARTER), BF16),) * N_DP,
         in_specs=[whole] * 5,
-        out_specs=whole,
+        out_specs=(whole,) * N_DP,
         compiler_params=params(24),
         cost_estimate=pl.CostEstimate(
             flops=HEAVY, bytes_accessed=5_000_000, transcendentals=0
@@ -468,29 +475,28 @@
     )(*hids, rows)
 
 
-def join_kernel(n_out, same_ref, mine_ref, other_ref, *outs):
-    mine = mine_ref[...].astype(F32)
-    both = jnp.where(same_ref[0] > 0, mine + other_ref[...].astype(F32), mine).astype(BF16)
-    rows = both.shape[0] // n_out
-    for b, out in enumerate(outs):
-        out[...] = both[b * rows:(b + 1) * rows]
-
-
-def join(same, mine, other, n_out):
-    rows, cols = mine.shape
-    steps = 7 if n_out == 1 else 1
-    block = pl.BlockSpec((rows // steps, cols), lambda m, same: (m, 0))
-    out = pl.BlockSpec((rows // steps // n_out, cols), lambda m, same: (m, 0))
-    return pl.pallas_call(
-        functools.partial(join_kernel, n_out),
-        out_shape=(jax.ShapeDtypeStruct((rows // n_out, cols), BF16),) * n_out,
+def join_kernel(slot_ref, here_ref, *refs):
+    n = len(refs) // 3
+    same = slot_ref[here_ref[0]] == slot_ref[here_ref[0] ^ 1]
+    for mine_ref, other_ref, out_ref in zip(refs[:n], refs[n:2 * n], refs[2 * n:]):
+        mine = mine_ref[...].astype(F32)
+        out_ref[...] = jnp.where(same, mine + other_ref[...].astype(F32), mine).astype(BF16)
+
+
+def join(slot_expert, here, mine, steps):
+    other = [swap(array) for array in mine]
+    rows, cols = mine[0].shape
+    block = pl.BlockSpec((rows // steps, cols), lambda m, slot, here: (m, 0))
+    return pl.pallas_call(
+        join_kernel,
+        out_shape=(jax.ShapeDtypeStruct((rows, cols), BF16),) * len(mine),
         grid_spec=pltpu.PrefetchScalarGridSpec(
-            num_scalar_prefetch=1, grid=(steps,),
-            in_specs=[block, block], out_specs=(out,) * n_out,
+            num_scalar_prefetch=2, grid=(steps,),
+            in_specs=[block] * (2 * len(mine)), out_specs=(block,) * len(mine),
         ),
         compiler_params=params(24),
         cost_estimate=pl.CostEstimate(flops=0, bytes_accessed=0, transcendentals=0),
-    )(same, mine, other)
+    )(slot_expert, here, *mine, *other)
 
 
 def place_kernel(at_ref, p0, p1, p2, p3, out_ref):
@@ -549,30 +555,28 @@
     x_rows, token = ordered((x_rows, swap(sent[0][:16])))
     x_here = exchange(x_rows).reshape(PADDED, QUARTER)
     x_own, x_below, x_above, x_far = ring(*halves(x_here, (*blocks, token)))
-    d_here, x_below, x_above = ordered((exchange(d_rows), x_below, x_above))
-    d_here = d_here.reshape(PADDED, QUARTER)
+    d_here = exchange(d_rows).reshape(PADDED, QUARTER)
 
     own, *out = terms(at, d_here, wd, blocks)
     others = [shift(out[b - 1], -b) for b in (2, 1, 3)]
     x_parts, own = ordered((x_own + x_below + x_above, own))
-    x_turned = turn(x_parts)
-    x_far, x_turned = ordered((x_far, x_turned))
     hid, act, ups = forward(at, x_far, near(at, x_parts, wg, wu), wg, wu)
-    s_own, s_below, s_above, s_far = ring(*slopes(own, others, hid, act, ups))
-    s_far, far_turned = ordered((s_far, turn(ordered((x_far, hid))[0])))
-    summed = back_near(at, s_own + s_below + s_above, wg, wu, blocks)
-    pay = back_rows(at, s_own + s_below + s_above + s_far, summed, blocks[1])
+    slope = slopes(own, others, hid, act, ups)
+    s_below, s_above = shift(slope, 1), shift(slope, -1)
+    x_turned = turn(ordered((x_parts + x_far, slope))[0])
+    s_below, s_above, x_turned = ordered((s_below, s_above, x_turned))
+    s_far = [shift(s_below[:HALF], 1), shift(s_above[HALF:], -1)]
+    s_near = (slope, s_below, s_above)
+    s_far, summed = ordered((s_far, back_near(at, s_near, wg, wu, blocks)))
+    pay = back_rows(at, (*s_near, *s_far), summed, blocks[1])
     back = exchange(pay).reshape(PADDED, QUARTER)
     d_tokens, d_probs = combine(slot, ids, probs, code, pick, back)
 
-    same = (slot_expert[here] == slot_expert[here ^ 1]).astype(jnp.int32).reshape(1)
-    hid = ordered((hid, s_below))[0]
-    gg, gu = grads(at, x_turned + far_turned, ordered((s_own, pay))[0])
-    gd = down_grads([hid] + [shift(hid, b) for b in (1, 2, 3)], d_here)
-    pieces = join(same, gd, swap(gd), N_DP)
-    grad_down = placed(at, [pieces[0]] + [shift(pieces[b], -b) for b in (1, 2, 3)])
-    grad_gate = join(same, gg, swap(gg), 1)[0]
-    grad_up = join(same, gu, swap(gu), 1)[0]
+    hid = ordered((hid, s_far))[0]
+    pieces = down_grads([hid] + [shift(hid, b) for b in (1, 2, 3)], d_here)
+    down = placed(at, [pieces[0]] + [shift(pieces[b], -b) for b in (1, 2, 3)])
+    grad_gate, grad_up = join(slot_expert, here.reshape(1), grads(at, x_turned, ordered((slope, pay))[0]), 4)
+    grad_down = join(slot_expert, here.reshape(1), [down], 2)[0]
     return d_tokens, d_probs.T, grad_gate[None], grad_up[None], grad_down[None]
 
 

time: 253 us -> 239 us (0.945)
  waiting for transfers between devices: 79.6 us -> 98.5 us
  Pallas kernels: 59.9 us -> 47.5 us
  starting transfers between devices: 72.4 us -> 62.5 us
  local copies, waits for them, and re-layouts: 36.9 us -> 28.8 us
    ppermute x24 -> x22, waiting for transfers between devices: 41 us -> 61.2 us  [shift(): return lax.ppermute(x, 'dp', [(i, (i + by) % N_DP) for i in range(N_DP)])]
    pallas_call x5 -> x4, Pallas kernels: 20.9 us -> 9.31 us  [the longest x2 5.04 us: join(): pl.pallas_call(join_kernel, out_shape=(jax.ShapeDtypeStruct((rows, cols),...]
    unnamed x86 -> x70, local copies, waits for them, and re-layouts: 18.5 us -> 9.97 us
    ppermute x24 -> x22, starting transfers between devices: 31.9 us -> 25.4 us  [shift(): return lax.ppermute(x, 'dp', [(i, (i + by) % N_DP) for i in range(N_DP)])]
    all_to_all x3, starting transfers between devices: 38.3 us -> 33.9 us  [exchange(): lax.all_to_all(rows.reshape(SLOTS, 3, 4, QUARTER), 'expert', split_axis=0...]
  transfers between devices with their start and end apart: 31 -> 29, of which waited for: 9 -> 13; matrix products, arithmetic and copies ran while one was open for 6% -> 7% of each run, Pallas kernels for 21% -> 17%
where the time goes in v3:
time: 239 us; the launch traced here: 238 us
  waiting for transfers between devices  98.5 us (41%)
  starting transfers between devices  62.5 us (26%)
  Pallas kernels  47.5 us (20%)
  local copies, waits for them, and re-layouts  28.8 us (12%)
    ppermute x22, waiting for transfers between devices, shift(): return lax.ppermute(x, 'dp', [(i, (i + by) % N_DP) for i in range(N_DP)])  61.2 us
    all_to_all x3, waiting for transfers between devices, exchange(): lax.all_to_all(rows.reshape(SLOTS, 3, 4, QUARTER), 'expert', split_axis=0...  36.9 us
    all_to_all x3, starting transfers between devices, exchange(): lax.all_to_all(rows.reshape(SLOTS, 3, 4, QUARTER), 'expert', split_axis=0...  33.9 us
    ppermute x22, starting transfers between devices, shift(): return lax.ppermute(x, 'dp', [(i, (i + by) % N_DP) for i in range(N_DP)])  25.4 us
    unnamed x70, local copies, waits for them, and re-layouts  9.97 us
    reshape x3, local copies, waits for them, and re-layouts, exchange(): rows.reshape(SLOTS, 3, 4, QUARTER)  8.43 us
    pallas_call x1, Pallas kernels, grads(): pl.pallas_call(grads_kernel, out_shape=(jax.ShapeDtypeStruct((WIDTH, SHAR...  5.63 us
    pallas_call x1, Pallas kernels, terms(): pl.pallas_call(terms_kernel, out_shape=(jax.ShapeDtypeStruct((PADDED, SHA...  5.31 us
  transfers between devices with their start and end apart: 29, of which 13 were waited for; matrix products, arithmetic and copies ran while one was open for 7% of the time, Pallas kernels for 17%

profile of v3, /device:TPU:1, one launch (start us, length us, event | category | flops | bytes accessed | tf_op | source)
XLA Modules:
  0.0 238.4 jit_solution(15205585912713633483)
XLA Ops:
  0.7 4.3 %shard_map.120 = (bf16[2688,256]{1,0:T(8,128)(2,1)}, bf16[2688,256]{1,0:T(8,128)(2,1)}, bf16[2688,256]{1,0:T(8,128)(2,1)}) custom-call(s32[1]{0:T(128)} %bitcast.3.at_ref, bf16[3584,256]{1,0:T(8,128)(2,1)} %bitcast.12, bf16[3584,256]{1,0:T(8,128)(2,1)} %bitcast.16, bf16[256,3584]{1,0:T(8,128)(2,1)} %bitcast.24), custom_call_target="tpu_custom_call" | custom-call | bytes 9600000 | tf_op jit(solution)/shard_map/pallas_call | solution.py:183
  14.6 3.6 %reshape.41 = bf16[64,3,4,896]{3,2,1,0:T(4,128)(2,1)} reshape(bf16[768,896]{1,0:T(8,128)(2,1)} %copy-done.11) | data formatting | bytes 2752512 | tf_op jit(solution)/shard_map/reshape | solution.py:529
  18.2 12.3 %all-to-all-start = ((bf16[64,3,4,896]{3,2,1,0:T(4,128)(2,1)}), bf16[64,3,4,896]{3,2,1,0:T(4,128)(2,1)}, u32[]{:S(2)}, u32[]{:S(2)}) async-start(bf16[64,3,4,896]{3,2,1,0:T(4,128)(2,1)} %reshape.41), calls=%async_computation | async-start | bytes 2752512 | tf_op jit(solution)/shard_map/all_to_all | solution.py:528
  32.2 3.6 %reshape.43 = bf16[64,3,4,896]{3,2,1,0:T(4,128)(2,1)} reshape(bf16[768,896]{1,0:T(8,128)(2,1)} %copy-done.12) | data formatting | bytes 2752512 | tf_op jit(solution)/shard_map/reshape | solution.py:529
  35.7 30.3 %all-to-all-done = bf16[64,3,4,896]{3,2,1,0:T(4,128)(2,1)} async-done(((bf16[64,3,4,896]{3,2,1,0:T(4,128)(2,1)}), bf16[64,3,4,896]{3,2,1,0:T(4,128)(2,1)}, u32[]{:S(2)}, u32[]{:S(2)}) %all-to-all-start) | async-done | bytes 1376288 | tf_op jit(solution)/shard_map/all_to_all | solution.py:528
  66.1 6.3 %all-to-all-start.1 = ((bf16[64,3,4,896]{3,2,1,0:T(4,128)(2,1)}), bf16[64,3,4,896]{3,2,1,0:T(4,128)(2,1)}, u32[]{:S(2)}, u32[]{:S(2)}) async-start(bf16[64,3,4,896]{3,2,1,0:T(4,128)(2,1)} %reshape.43), calls=%async_computation.1 | async-start | bytes 2752512 | tf_op jit(solution)/shard_map/all_to_all | solution.py:528
  72.4 3.5 %reshape.42.rows_ref = bf16[768,896]{1,0:T(8,128)(2,1)} reshape(bf16[64,3,4,896]{3,2,1,0:T(4,128)(2,1)} %all-to-all-done) | data formatting | bytes 2752512 | tf_op jit(solution)/shard_map/reshape | solution.py:556
  84.8 13.9 %collective-permute-done.4.refs_2_ = bf16[384,896]{1,0:T(8,128)(2,1)S(1)} collective-permute-done((bf16[384,896]{1,0:T(8,128)(2,1)}, bf16[384,896]{1,0:T(8,128)(2,1)S(1)}, u32[]{:S(2)}, u32[]{:S(2)}) %collective-permute-start.4) | collective-permute-done | bytes 688160 | tf_op jit(solution)/shard_map/ppermute | solution.py:520
  101.3 6.6 %all-to-all-done.1 = bf16[64,3,4,896]{3,2,1,0:T(4,128)(2,1)} async-done(((bf16[64,3,4,896]{3,2,1,0:T(4,128)(2,1)}), bf16[64,3,4,896]{3,2,1,0:T(4,128)(2,1)}, u32[]{:S(2)}, u32[]{:S(2)}) %all-to-all-start.1) | async-done | bytes 1376288 | tf_op jit(solution)/shard_map/all_to_all | solution.py:528
  107.9 3.5 %reshape.44.rows_ref = bf16[768,896]{1,0:T(8,128)(2,1)} reshape(bf16[64,3,4,896]{3,2,1,0:T(4,128)(2,1)} %all-to-all-done.1) | data formatting | bytes 2752512 | tf_op jit(solution)/shard_map/reshape | solution.py:558
  111.4 5.3 %shard_map.123 = (f32[768,256]{1,0:T(8,128)}, bf16[768,256]{1,0:T(8,128)(2,1)}, bf16[768,256]{1,0:T(8,128)(2,1)}, bf16[768,256]{1,0:T(8,128)(2,1)}) custom-call(s32[1]{0:T(128)} %bitcast.3.at_ref, bf16[768,896]{1,0:T(8,128)(2,1)} %reshape.44.rows_ref, bf16[256,3584]{1,0:T(8,128)(2,1)} %bitcast.25, bf16[2688,256]{1,0:T(8,128)(2,1)} %copy-done.5, ...), custom_call_target="tpu_custom_call" | custom-call | flops 1409286144 | bytes 5000000 | tf_op jit(solution)/shard_map/pallas_call | solution.py:290
  119.6 4.4 %shard_map.124.sum_ref = f32[768,512]{1,0:T(8,128)S(1)} custom-call(s32[1]{0:T(128)} %bitcast.3.at_ref, bf16[384,896]{1,0:T(8,128)(2,1)S(1)} %copy-done.7, bf16[384,896]{1,0:T(8,128)(2,1)S(1)} %copy-done.8, bf16[384,896]{1,0:T(8,128)(2,1)S(1)} %collective-permute-done.4.refs_2_, bf16[384,896]{1,0:T(8,128)(2,1)} %collective-permute-done.5.refs_3_, ...), custom_call_target="tpu_custom_call" | custom-call | flops 2113929216 | bytes 9000000 | tf_op jit(solution)/shard_map/pallas_call | solution.py:230
  124.0 12.3 %collective-permute-done.11.low.refs_6_ = bf16[384,896]{1,0:T(8,128)(2,1)} collective-permute-done((bf16[384,896]{1,0:T(8,128)(2,1)S(1)}, bf16[384,896]{1,0:T(8,128)(2,1)}, u32[]{:S(2)}, u32[]{:S(2)}) %collective-permute-start.11) | collective-permute-done | bytes 688160 | tf_op jit(solution)/shard_map/ppermute | solution.py:520
  136.3 3.4 %shard_map.125 = (bf16[768,256]{1,0:T(8,128)(2,1)S(1)}, f32[768,256]{1,0:T(8,128)S(1)}, f32[768,256]{1,0:T(8,128)S(1)}) custom-call(s32[1]{0:T(128)} %bitcast.3.at_ref, bf16[384,896]{1,0:T(8,128)(2,1)} %collective-permute-done.11.low.refs_6_, bf16[384,896]{1,0:T(8,128)(2,1)} %collective-permute-done.12.high.refs_7_, f32[768,512]{1,0:T(8,128)S(1)} %shard_map.124.sum_ref, ...), custom_call_target="tpu_custom_call" | custom-call | flops 704643072 | bytes 4000000 | tf_op jit(solution)/shard_map/pallas_call | solution.py:259
  139.7 4.2 %collective-permute-done.9.r2 = bf16[768,256]{1,0:T(8,128)(2,1)S(1)} collective-permute-done((bf16[768,256]{1,0:T(8,128)(2,1)}, bf16[768,256]{1,0:T(8,128)(2,1)S(1)}, u32[]{:S(2)}, u32[]{:S(2)}) %collective-permute-start.9) | collective-permute-done | bytes 393248 | tf_op jit(solution)/shard_map/ppermute | solution.py:520
  155.0 9.0 %collective-permute-done.14.above = bf16[768,512]{1,0:T(8,128)(2,1)S(1)} collective-permute-done((bf16[768,512]{1,0:T(8,128)(2,1)S(1)}, bf16[768,512]{1,0:T(8,128)(2,1)S(1)}, u32[]{:S(2)}, u32[]{:S(2)}) %collective-permute-start.14) | collective-permute-done | bytes 786464 | tf_op jit(solution)/shard_map/ppermute | solution.py:520
  163.9 3.0 %collective-permute-done.13.below = bf16[768,512]{1,0:T(8,128)(2,1)S(1)} collective-permute-done((bf16[768,512]{1,0:T(8,128)(2,1)S(1)}, bf16[768,512]{1,0:T(8,128)(2,1)S(1)}, u32[]{:S(2)}, u32[]{:S(2)}) %collective-permute-start.13) | collective-permute-done | bytes 786464 | tf_op jit(solution)/shard_map/ppermute | solution.py:520
  168.6 5.2 %shard_map.128.sum_ref = f32[768,896]{1,0:T(8,128)S(1)} custom-call(s32[1]{0:T(128)} %bitcast.3.at_ref, bf16[768,512]{1,0:T(8,128)(2,1)S(1)} %shard_map.126.own.slope_ref, bf16[768,512]{1,0:T(8,128)(2,1)S(1)} %collective-permute-done.13.below, bf16[768,512]{1,0:T(8,128)(2,1)S(1)} %collective-permute-done.14.above, bf16[3584,256]{1,0:T(8,128)(2,1)S(1)} %bitcast.15, ...), custom_call_target="tpu_custom_call" | custom-call | flops 2113929216 | bytes 8000000 | tf_op jit(solution)/shard_map/pallas_call | solution.py:374
  180.9 15.3 %all-to-all-start.2 = ((bf16[64,3,4,896]{3,2,1,0:T(4,128)(2,1)}), bf16[64,3,4,896]{3,2,1,0:T(4,128)(2,1)}, u32[]{:S(2)}, u32[]{:S(2)}) async-start(bf16[64,3,4,896]{3,2,1,0:T(4,128)(2,1)} %reshape.45), calls=%async_computation.2 | async-start | bytes 2752512 | tf_op jit(solution)/shard_map/all_to_all | solution.py:528
  201.5 3.0 %collective-permute-start.22 = (bf16[256,896]{1,0:T(8,128)(2,1)S(1)}, bf16[256,896]{1,0:T(8,128)(2,1)S(1)}, u32[]{:S(2)}, u32[]{:S(2)}) collective-permute-start(bf16[256,896]{1,0:T(8,128)(2,1)S(1)} %get-tuple-element.118), channel_id=1, source_target_pairs={{0,192},{64,0},{128,64},{192,128},{1,193},{65,1},{129,65},{193,129... | collective-permute-start | bytes 1376264 | tf_op jit(solution)/shard_map/ppermute | solution.py:520
  206.0 5.6 %shard_map.131 = (bf16[3584,256]{1,0:T(8,128)(2,1)S(1)}, bf16[3584,256]{1,0:T(8,128)(2,1)S(1)}) custom-call(s32[1]{0:T(128)} %bitcast.3.at_ref, bf16[896,768]{1,0:T(8,128)(2,1)S(1)} %copy-done.23, bf16[896,768]{1,0:T(8,128)(2,1)S(1)} %copy-done.25, bf16[896,768]{1,0:T(8,128)(2,1)S(1)} %copy-done.27, bf16[896,768]{1,0:T(8,128)(2,1)S(1)} %copy-done.29, ...), custom_call_target="tpu_custom_call" | custom-call | flops 2818572288 | bytes 11000000 | tf_op jit(solution)/shard_map/pallas_call | solution.py:447
  213.2 10.4 %collective-permute-done.22.p1 = bf16[256,896]{1,0:T(8,128)(2,1)S(1)} collective-permute-done((bf16[256,896]{1,0:T(8,128)(2,1)S(1)}, bf16[256,896]{1,0:T(8,128)(2,1)S(1)}, u32[]{:S(2)}, u32[]{:S(2)}) %collective-permute-start.22) | collective-permute-done | bytes 458784 | tf_op jit(solution)/shard_map/ppermute | solution.py:520
  223.6 4.8 %collective-permute-done.24.p3 = bf16[256,896]{1,0:T(8,128)(2,1)S(1)} collective-permute-done((bf16[256,896]{1,0:T(8,128)(2,1)S(1)}, bf16[256,896]{1,0:T(8,128)(2,1)S(1)}, u32[]{:S(2)}, u32[]{:S(2)}) %collective-permute-start.24) | collective-permute-done | bytes 458784 | tf_op jit(solution)/shard_map/ppermute | solution.py:520
  229.1 3.0 %shard_map.132 = (bf16[3584,256]{1,0:T(8,128)(2,1)}, bf16[3584,256]{1,0:T(8,128)(2,1)}) custom-call(s32[64]{0:T(128)S(1)} %copy-done.19, s32[1]{0:T(128)} %bitcast.8.here_ref, bf16[3584,256]{1,0:T(8,128)(2,1)S(1)} %get-tuple-element.112.refs_0_, bf16[3584,256]{1,0:T(8,128)(2,1)S(1)} %get-tuple-element.113.refs_1_, ...), custom_call_target="tpu_custom_call" | custom-call | tf_op jit(solution)/shard_map/pallas_call | solution.py:490
  (132 shorter events, 60.6 us)
Async XLA Ops:
  5.0 70.9 %collective-permute-start.1 = (bf16[2688,256]{1,0:T(8,128)(2,1)}, bf16[2688,256]{1,0:T(8,128)(2,1)S(1)}, u32[]{:S(2)}, u32[]{:S(2)}) collective-permute-start(bf16[2688,256]{1,0:T(8,128)(2,1)} %get-tuple-element.66), channel_id=1, source_target_pairs={{0,64},{64,128},{128,192},{192,0},{1,65},{65,129},{129,193},{193,1... | collective-permute-start | bytes 4128776 | tf_op jit(solution)/shard_map/ppermute | solution.py:520
  9.0 66.8 %collective-permute-start.2 = (bf16[2688,256]{1,0:T(8,128)(2,1)}, bf16[2688,256]{1,0:T(8,128)(2,1)S(1)}, u32[]{:S(2)}, u32[]{:S(2)}) collective-permute-start(bf16[2688,256]{1,0:T(8,128)(2,1)} %get-tuple-element.68), channel_id=1, source_target_pairs={{0,128},{64,192},{128,0},{192,64},{1,129},{65,193},{129,1},{193,65... | collective-permute-start | bytes 4128776 | tf_op jit(solution)/shard_map/ppermute | solution.py:520
  11.5 64.4 %collective-permute-start.3 = (bf16[2688,256]{1,0:T(8,128)(2,1)}, bf16[2688,256]{1,0:T(8,128)(2,1)}, u32[]{:S(2)}, u32[]{:S(2)}) collective-permute-start(bf16[2688,256]{1,0:T(8,128)(2,1)} %get-tuple-element.69), channel_id=1, source_target_pairs={{0,192},{64,0},{128,64},{192,128},{1,193},{65,1},{129,65},{193,129... | collective-permute-start | bytes 4128776 | tf_op jit(solution)/shard_map/ppermute | solution.py:520
  18.2 47.9 %all-to-all-start = ((bf16[64,3,4,896]{3,2,1,0:T(4,128)(2,1)}), bf16[64,3,4,896]{3,2,1,0:T(4,128)(2,1)}, u32[]{:S(2)}, u32[]{:S(2)}) async-start(bf16[64,3,4,896]{3,2,1,0:T(4,128)(2,1)} %reshape.41), calls=%async_computation | async-start | bytes 2752512 | tf_op jit(solution)/shard_map/all_to_all | solution.py:528
  66.1 41.8 %all-to-all-start.1 = ((bf16[64,3,4,896]{3,2,1,0:T(4,128)(2,1)}), bf16[64,3,4,896]{3,2,1,0:T(4,128)(2,1)}, u32[]{:S(2)}, u32[]{:S(2)}) async-start(bf16[64,3,4,896]{3,2,1,0:T(4,128)(2,1)} %reshape.43), calls=%async_computation.1 | async-start | bytes 2752512 | tf_op jit(solution)/shard_map/all_to_all | solution.py:528
  80.6 18.1 %collective-permute-start.4 = (bf16[384,896]{1,0:T(8,128)(2,1)}, bf16[384,896]{1,0:T(8,128)(2,1)S(1)}, u32[]{:S(2)}, u32[]{:S(2)}) collective-permute-start(bf16[384,896]{1,0:T(8,128)(2,1)} %get-tuple-element.88.refs_0_), channel_id=1, source_target_pairs={{0,64},{64,128},{128,192},{192,0},{1,65},{65,129},{129,193},{193,1... | collective-permute-start | bytes 2064392 | tf_op jit(solution)/shard_map/ppermute | solution.py:520
  81.0 17.6 %collective-permute-start.7 = (bf16[384,896]{1,0:T(8,128)(2,1)}, bf16[384,896]{1,0:T(8,128)(2,1)S(1)}, u32[]{:S(2)}, u32[]{:S(2)}) collective-permute-start(bf16[384,896]{1,0:T(8,128)(2,1)} %get-tuple-element.89.refs_1_), channel_id=1, source_target_pairs={{0,192},{64,0},{128,64},{192,128},{1,193},{65,1},{129,65},{193,129... | collective-permute-start | bytes 2064392 | tf_op jit(solution)/shard_map/ppermute | solution.py:520
  83.3 33.5 %collective-permute-start.6 = (bf16[384,896]{1,0:T(8,128)(2,1)}, bf16[384,896]{1,0:T(8,128)(2,1)S(1)}, u32[]{:S(2)}, u32[]{:S(2)}) collective-permute-start(bf16[384,896]{1,0:T(8,128)(2,1)} %get-tuple-element.88.refs_0_), channel_id=1, source_target_pairs={{0,192},{64,0},{128,64},{192,128},{1,193},{65,1},{129,65},{193,129... | collective-permute-start | bytes 2064392 | tf_op jit(solution)/shard_map/ppermute | solution.py:520
  83.3 36.2 %collective-permute-start.5 = (bf16[384,896]{1,0:T(8,128)(2,1)}, bf16[384,896]{1,0:T(8,128)(2,1)}, u32[]{:S(2)}, u32[]{:S(2)}) collective-permute-start(bf16[384,896]{1,0:T(8,128)(2,1)} %get-tuple-element.89.refs_1_), channel_id=1, source_target_pairs={{0,64},{64,128},{128,192},{192,0},{1,65},{65,129},{129,193},{193,1... | collective-permute-start | bytes 2064392 | tf_op jit(solution)/shard_map/ppermute | solution.py:520
  98.6 37.7 %collective-permute-start.11 = (bf16[384,896]{1,0:T(8,128)(2,1)S(1)}, bf16[384,896]{1,0:T(8,128)(2,1)}, u32[]{:S(2)}, u32[]{:S(2)}) collective-permute-start(bf16[384,896]{1,0:T(8,128)(2,1)S(1)} %collective-permute-done.4.refs_2_), channel_id=1, source_target_pairs={{0,64},{64,128},{128,192},{192,0},{1,65},{65,129},{129,193},{193,1... | collective-permute-start | bytes 2064392 | tf_op jit(solution)/shard_map/ppermute | solution.py:520
  98.6 37.7 %collective-permute-start.12 = (bf16[384,896]{1,0:T(8,128)(2,1)S(1)}, bf16[384,896]{1,0:T(8,128)(2,1)}, u32[]{:S(2)}, u32[]{:S(2)}) collective-permute-start(bf16[384,896]{1,0:T(8,128)(2,1)S(1)} %collective-permute-done.7.refs_5_), channel_id=1, source_target_pairs={{0,192},{64,0},{128,64},{192,128},{1,193},{65,1},{129,65},{193,129... | collective-permute-start | bytes 2064392 | tf_op jit(solution)/shard_map/ppermute | solution.py:520
  116.7 23.0 %collective-permute-start.8 = (bf16[768,256]{1,0:T(8,128)(2,1)}, bf16[768,256]{1,0:T(8,128)(2,1)S(1)}, u32[]{:S(2)}, u32[]{:S(2)}) collective-permute-start(bf16[768,256]{1,0:T(8,128)(2,1)} %get-tuple-element.76), channel_id=1, source_target_pairs={{0,128},{64,192},{128,0},{192,64},{1,129},{65,193},{129,1},{193,65... | collective-permute-start | bytes 1179656 | tf_op jit(solution)/shard_map/ppermute | solution.py:520
  116.8 27.1 %collective-permute-start.9 = (bf16[768,256]{1,0:T(8,128)(2,1)}, bf16[768,256]{1,0:T(8,128)(2,1)S(1)}, u32[]{:S(2)}, u32[]{:S(2)}) collective-permute-start(bf16[768,256]{1,0:T(8,128)(2,1)} %get-tuple-element.77), channel_id=1, source_target_pairs={{0,192},{64,0},{128,64},{192,128},{1,193},{65,1},{129,65},{193,129... | collective-permute-start | bytes 1179656 | tf_op jit(solution)/shard_map/ppermute | solution.py:520
  119.5 25.3 %collective-permute-start.10 = (bf16[768,256]{1,0:T(8,128)(2,1)}, bf16[768,256]{1,0:T(8,128)(2,1)S(1)}, u32[]{:S(2)}, u32[]{:S(2)}) collective-permute-start(bf16[768,256]{1,0:T(8,128)(2,1)} %get-tuple-element.78), channel_id=1, source_target_pairs={{0,64},{64,128},{128,192},{192,0},{1,65},{65,129},{129,193},{193,1... | collective-permute-start | bytes 1179656 | tf_op jit(solution)/shard_map/ppermute | solution.py:520
  146.2 17.7 %collective-permute-start.14 = (bf16[768,512]{1,0:T(8,128)(2,1)S(1)}, bf16[768,512]{1,0:T(8,128)(2,1)S(1)}, u32[]{:S(2)}, u32[]{:S(2)}) collective-permute-start(bf16[768,512]{1,0:T(8,128)(2,1)S(1)} %shard_map.126.own.slope_ref), channel_id=1, source_target_pairs={{0,192},{64,0},{128,64},{192,128},{1,193},{65,1},{129,65},{193,129... | collective-permute-start | bytes 2359304 | tf_op jit(solution)/shard_map/ppermute | solution.py:520
  148.7 18.3 %collective-permute-start.13 = (bf16[768,512]{1,0:T(8,128)(2,1)S(1)}, bf16[768,512]{1,0:T(8,128)(2,1)S(1)}, u32[]{:S(2)}, u32[]{:S(2)}) collective-permute-start(bf16[768,512]{1,0:T(8,128)(2,1)S(1)} %shard_map.126.own.slope_ref), channel_id=1, source_target_pairs={{0,64},{64,128},{128,192},{192,0},{1,65},{65,129},{129,193},{193,1... | collective-permute-start | bytes 2359304 | tf_op jit(solution)/shard_map/ppermute | solution.py:520
  176.3 19.9 %collective-permute-start.21 = (bf16[768,256]{1,0:T(8,128)(2,1)S(1)}, bf16[768,256]{1,0:T(8,128)(2,1)S(1)}, u32[]{:S(2)}, u32[]{:S(2)}) collective-permute-start(bf16[768,256]{1,0:T(8,128)(2,1)S(1)} %get-tuple-element.116.hid_ref.h0), channel_id=1, source_target_pairs={{0,192},{64,0},{128,64},{192,128},{1,193},{65,1},{129,65},{193,129... | collective-permute-start | bytes 1179656 | tf_op jit(solution)/shard_map/ppermute | solution.py:520
  176.6 20.4 %collective-permute-start.20 = (bf16[768,256]{1,0:T(8,128)(2,1)S(1)}, bf16[768,256]{1,0:T(8,128)(2,1)}, u32[]{:S(2)}, u32[]{:S(2)}) collective-permute-start(bf16[768,256]{1,0:T(8,128)(2,1)S(1)} %get-tuple-element.116.hid_ref.h0), channel_id=1, source_target_pairs={{0,128},{64,192},{128,0},{192,64},{1,129},{65,193},{129,1},{193,65... | collective-permute-start | bytes 1179656 | tf_op jit(solution)/shard_map/ppermute | solution.py:520
  177.8 19.2 %collective-permute-start.19 = (bf16[768,256]{1,0:T(8,128)(2,1)S(1)}, bf16[768,256]{1,0:T(8,128)(2,1)}, u32[]{:S(2)}, u32[]{:S(2)}) collective-permute-start(bf16[768,256]{1,0:T(8,128)(2,1)S(1)} %get-tuple-element.116.hid_ref.h0), channel_id=1, source_target_pairs={{0,64},{64,128},{128,192},{192,0},{1,65},{65,129},{129,193},{193,1... | collective-permute-start | bytes 1179656 | tf_op jit(solution)/shard_map/ppermute | solution.py:520
  180.9 53.6 %all-to-all-start.2 = ((bf16[64,3,4,896]{3,2,1,0:T(4,128)(2,1)}), bf16[64,3,4,896]{3,2,1,0:T(4,128)(2,1)}, u32[]{:S(2)}, u32[]{:S(2)}) async-start(bf16[64,3,4,896]{3,2,1,0:T(4,128)(2,1)} %reshape.45), calls=%async_computation.2 | async-start | bytes 2752512 | tf_op jit(solution)/shard_map/all_to_all | solution.py:528
  201.5 22.1 %collective-permute-start.22 = (bf16[256,896]{1,0:T(8,128)(2,1)S(1)}, bf16[256,896]{1,0:T(8,128)(2,1)S(1)}, u32[]{:S(2)}, u32[]{:S(2)}) collective-permute-start(bf16[256,896]{1,0:T(8,128)(2,1)S(1)} %get-tuple-element.118), channel_id=1, source_target_pairs={{0,192},{64,0},{128,64},{192,128},{1,193},{65,1},{129,65},{193,129... | collective-permute-start | bytes 1376264 | tf_op jit(solution)/shard_map/ppermute | solution.py:520
  204.5 19.0 %collective-permute-start.23 = (bf16[256,896]{1,0:T(8,128)(2,1)S(1)}, bf16[256,896]{1,0:T(8,128)(2,1)S(1)}, u32[]{:S(2)}, u32[]{:S(2)}) collective-permute-start(bf16[256,896]{1,0:T(8,128)(2,1)S(1)} %get-tuple-element.119), channel_id=1, source_target_pairs={{0,128},{64,192},{128,0},{192,64},{1,129},{65,193},{129,1},{193,65... | collective-permute-start | bytes 1376264 | tf_op jit(solution)/shard_map/ppermute | solution.py:520
  205.2 23.2 %collective-permute-start.24 = (bf16[256,896]{1,0:T(8,128)(2,1)S(1)}, bf16[256,896]{1,0:T(8,128)(2,1)S(1)}, u32[]{:S(2)}, u32[]{:S(2)}) collective-permute-start(bf16[256,896]{1,0:T(8,128)(2,1)S(1)} %get-tuple-element.120), channel_id=1, source_target_pairs={{0,64},{64,128},{128,192},{192,0},{1,65},{65,129},{129,193},{193,1... | collective-permute-start | bytes 1376264 | tf_op jit(solution)/shard_map/ppermute | solution.py:520
  211.7 17.4 %collective-permute-start.17 = (bf16[3584,256]{1,0:T(8,128)(2,1)S(1)}, bf16[3584,256]{1,0:T(8,128)(2,1)S(1)}, u32[]{:S(2)}, u32[]{:S(2)}) collective-permute-start(bf16[3584,256]{1,0:T(8,128)(2,1)S(1)} %get-tuple-element.112.refs_0_), channel_id=1, source_target_pairs={{0,1},{1,0},{2,3},{3,2},{4,5},{5,4},{6,7},{7,6},{8,9},{9,8},{10,11... | collective-permute-start | bytes 5505032 | tf_op jit(solution)/shard_map/ppermute | solution.py:524
  (40 other events, 282.9 us)

commit v4 on v3

--- a/solution.py
+++ b/solution.py
@@ -14,6 +14,7 @@
 BLOCK = 12
 TOK = 128
 PADDED = SLOTS * BLOCK
+FOURS = PADDED // 4
 HALF = PADDED // 2
 QUARTER = 896
 WIDTH = 3584
@@ -71,7 +72,7 @@
     pick = pick.astype(BF16)
     pick_ref[...] = pick
     scaled_ref[...] = scaled.astype(BF16)
-    x_ref[...] = dot(pick, tok_ref[...]).astype(BF16)
+    x_ref[...] = dot(pick, tok_ref[...]).astype(BF16).reshape(FOURS, 4, QUARTER)
 
 
 def pack(parity, slot, ids, probs, tokens):
@@ -79,27 +80,27 @@
     return pl.pallas_call(
         pack_kernel,
         out_shape=(
-            jax.ShapeDtypeStruct((PADDED, QUARTER), BF16),
+            jax.ShapeDtypeStruct((FOURS, 4, QUARTER), BF16),
             jax.ShapeDtypeStruct((SLOTS, TOK), F32),
             jax.ShapeDtypeStruct((PADDED, TOK), BF16),
             jax.ShapeDtypeStruct((PADDED, TOK), BF16),
         ),
         in_specs=[pl.BlockSpec(memory_space=pltpu.SMEM)] + [whole] * 4,
         out_specs=(whole,) * 4,
-        compiler_params=params(24),
+        compiler_params=params(56),
         cost_estimate=pl.CostEstimate(flops=HEAVY, bytes_accessed=3_000_000, transcendentals=0),
     )(parity, slot, ids, probs, tokens)
 
 
 def scale_kernel(scaled_ref, cot_ref, out_ref):
-    out_ref[...] = dot(scaled_ref[...], cot_ref[...]).astype(BF16)
+    out_ref[...] = dot(scaled_ref[...], cot_ref[...]).astype(BF16).reshape(FOURS, 4, QUARTER)
 
 
 def scale(scaled, cotangent):
     whole = pl.BlockSpec(memory_space=VMEM)
     return pl.pallas_call(
         scale_kernel,
-        out_shape=jax.ShapeDtypeStruct((PADDED, QUARTER), BF16),
+        out_shape=jax.ShapeDtypeStruct((FOURS, 4, QUARTER), BF16),
         in_specs=[whole] * 2,
         out_specs=whole,
         compiler_params=params(16),
@@ -108,11 +109,12 @@
 
 
 def combine_kernel(slot_ref, ids_ref, probs_ref, code_ref, pick_ref, back_ref, dtok_ref, dprob_ref):
-    dtok_ref[...] = dot(pick_ref[...], back_ref[...], 0, 0).astype(BF16)
+    back = back_ref[...].reshape(PADDED, QUARTER)
+    dtok_ref[...] = dot(pick_ref[...], back, 0, 0).astype(BF16)
     chosen = jnp.where(
         iota((SLOTS, PADDED), 1) == iota((SLOTS, PADDED), 0) * BLOCK + CAP, 1.0, 0.0
     ).astype(BF16)
-    scores = dot(chosen, back_ref[:, 0:TOK]) + dot(chosen, back_ref[:, TOK:2 * TOK])
+    scores = dot(chosen, back[:, 0:TOK]) + dot(chosen, back[:, TOK:2 * TOK])
     code = code_ref[...]
     placed = jnp.zeros((SLOTS, TOK), F32)
     for r in range(CAP):
@@ -157,7 +159,7 @@
     return pl.multiple_of(lax.rem(at_ref[0] + rel, N_DP) * QUARTER, 128)
 
 
-def weights_kernel(at_ref, wg_ref, wu_ref, wd_ref, o1, o2, o3, down, sems):
+def weights_kernel(at_ref, wg_ref, wu_ref, wd_ref, o1, o2, o3, token, down, sems):
     copies = []
     for b, out in zip((1, 2, 3), (o1, o2, o3)):
         where = pl.ds(offset(at_ref, b), QUARTER)
@@ -172,6 +174,7 @@
     for b, out in zip((1, 2, 3), (o1, o2, o3)):
         copies[3 * b - 3].wait()
         out[2 * QUARTER:, :] = down[b - 1].T
+    token[...] = down[0, :16, :TOK]
     for i, copy in enumerate(copies):
         if i % 3:
             copy.wait()
@@ -182,35 +185,42 @@
     stays = pl.BlockSpec(memory_space=pl.ANY)
     return pl.pallas_call(
         weights_kernel,
-        out_shape=(jax.ShapeDtypeStruct((3 * QUARTER, SHARE), BF16),) * 3,
+        out_shape=(jax.ShapeDtypeStruct((3 * QUARTER, SHARE), BF16),) * 3
+        + (jax.ShapeDtypeStruct((16, TOK), BF16),),
         in_specs=[pl.BlockSpec(memory_space=pltpu.SMEM), stays, stays, stays],
-        out_specs=(whole,) * 3,
+        out_specs=(whole,) * 4,
         scratch_shapes=[pltpu.VMEM((3, SHARE, QUARTER), BF16), pltpu.SemaphoreType.DMA((3, 3))],
         compiler_params=params(56),
         cost_estimate=pl.CostEstimate(flops=0, bytes_accessed=9_600_000, transcendentals=0),
     )(at, wg, wu, wd)
 
 
-def halves_kernel(rows_ref, a1, a2, a3, a4, low_ref, high_ref, sems):
-    low = pltpu.make_async_copy(rows_ref.at[pl.ds(0, HALF), :], low_ref, sems.at[0])
-    high = pltpu.make_async_copy(rows_ref.at[pl.ds(HALF, HALF), :], high_ref, sems.at[1])
-    low.start()
-    high.start()
-    low.wait()
-    high.wait()
+def halves_kernel(rows_ref, after_ref, low_ref, high_ref):
+    rows = rows_ref[...].reshape(HALF, QUARTER)
+
+    @pl.when(pl.program_id(0) == 0)
+    def _():
+        low_ref[...] = rows
+
+    @pl.when(pl.program_id(0) == 1)
+    def _():
+        high_ref[...] = rows
 
 
 def halves(rows, after):
-    whole = pl.BlockSpec(memory_space=VMEM)
+    half = pl.BlockSpec((HALF, QUARTER), lambda m: (0, 0))
     return pl.pallas_call(
         halves_kernel,
         out_shape=(jax.ShapeDtypeStruct((HALF, QUARTER), BF16),) * 2,
-        in_specs=[pl.BlockSpec(memory_space=pl.ANY)] * 5,
-        out_specs=(whole,) * 2,
-        scratch_shapes=[pltpu.SemaphoreType.DMA((2,))],
+        grid=(2,),
+        in_specs=[
+            pl.BlockSpec((FOURS // 2, 4, QUARTER), lambda m: (m, 0, 0)),
+            pl.BlockSpec(memory_space=pl.ANY),
+        ],
+        out_specs=(half,) * 2,
         compiler_params=params(56),
         cost_estimate=pl.CostEstimate(flops=HEAVY, bytes_accessed=2_800_000, transcendentals=0),
-    )(rows, *after)
+    )(rows, after)
 
 
 def near_kernel(at_ref, *refs):
@@ -277,7 +287,7 @@
 
 
 def terms_kernel(at_ref, rows_ref, w0, w1, w2, w3, own_ref, p1, p2, p3):
-    rows = rows_ref[...]
+    rows = rows_ref[...].reshape(TILE, QUARTER)
     own_ref[...] = dot(rows, w0[...], 1, 1)
     for w, p in ((w1, p1), (w2, p2), (w3, p3)):
         p[...] = dot(rows, w[...]).astype(BF16)
@@ -293,7 +303,7 @@
         grid_spec=pltpu.PrefetchScalarGridSpec(
             num_scalar_prefetch=1, grid=(TILES,),
             in_specs=[
-                pl.BlockSpec((TILE, QUARTER), lambda m, at: (m, 0)),
+                pl.BlockSpec((TILE // 4, 4, QUARTER), lambda m, at: (m, 0, 0)),
                 pl.BlockSpec((SHARE, QUARTER), lambda m, at: (0, at[0])),
                 down, down, down,
             ],
@@ -356,15 +366,15 @@
 def back_kernel(at_ref, own, below, above, low, high, sum_ref, g2, out_ref):
     far = this_tile((low, high))[0]
     total = sum_ref[...] + product(far, (g2[:QUARTER, :], g2[QUARTER:, :]))
-    out_ref[...] = total.astype(BF16)
     parts = [s[:, :SHARE].astype(F32) for s in (own, below, above, far)]
     lanes = (parts[0] + parts[3]) + (parts[1] + parts[2])
     score = lanes[:, :TOK] + lanes[:, TOK:]
-    high = score.astype(BF16)
-    rest = (score - high.astype(F32)).astype(BF16)
-    spare = within_block((TILE, TOK)) == CAP
-    out_ref[:, :TOK] = jnp.where(spare, high.astype(F32), total[:, :TOK]).astype(BF16)
-    out_ref[:, TOK:2 * TOK] = jnp.where(spare, rest.astype(F32), total[:, TOK:2 * TOK]).astype(BF16)
+    high = score.astype(BF16).astype(F32)
+    scores = jnp.concatenate([high, score - high], axis=1)
+    spare = within_block((TILE, 2 * TOK)) == CAP
+    first = jnp.where(spare, scores, total[:, :2 * TOK])
+    rows = jnp.concatenate([first, total[:, 2 * TOK:]], axis=1).astype(BF16)
+    out_ref[...] = rows.reshape(TILE // 4, 4, QUARTER)
 
 
 def back_near(at, parts, wg, wu, blocks):
@@ -392,10 +402,11 @@
     tile = pl.BlockSpec((TILE, QUARTER), lambda m, at: (m, 0))
     return pl.pallas_call(
         back_kernel,
-        out_shape=jax.ShapeDtypeStruct((PADDED, QUARTER), BF16),
+        out_shape=jax.ShapeDtypeStruct((FOURS, 4, QUARTER), BF16),
         grid_spec=pltpu.PrefetchScalarGridSpec(
             num_scalar_prefetch=1, grid=(TILES,),
-            in_specs=[slope] * 3 + half_specs(2 * SHARE) + [tile, both], out_specs=tile,
+            in_specs=[slope] * 3 + half_specs(2 * SHARE) + [tile, both],
+            out_specs=pl.BlockSpec((TILE // 4, 4, QUARTER), lambda m, at: (m, 0, 0)),
         ),
         compiler_params=params(32),
         cost_estimate=pl.CostEstimate(
@@ -457,8 +468,9 @@
 
 
 def down_kernel(h0, h1, h2, h3, rows_ref, *outs):
+    rows = rows_ref[...].reshape(PADDED, QUARTER)
     for h, out in zip((h0, h1, h2, h3), outs):
-        out[...] = dot(h[...], rows_ref[...], 0, 0).astype(BF16)
+        out[...] = dot(h[...], rows, 0, 0).astype(BF16)
 
 
 def down_grads(hids, rows):
@@ -527,7 +539,7 @@
 def exchange(rows):
     return lax.all_to_all(
         rows.reshape(SLOTS, 3, 4, QUARTER), "expert", split_axis=0, concat_axis=0, tiled=True
-    )
+    ).reshape(FOURS, 4, QUARTER)
 
 
 def ring(low, high):
@@ -550,12 +562,12 @@
     slot = jnp.broadcast_to(slot_expert.astype(F32)[:, None], (SLOTS, TOK))
     x_rows, code, pick, scaled = pack(parity, slot, ids, probs, tokens)
     d_rows = scale(scaled, cotangent)
-    sent = weights(at, wg, wu, wd)
+    *sent, few = weights(at, wg, wu, wd)
     blocks = [shift(w, b) for w, b in zip(sent, (1, 2, 3))]
-    x_rows, token = ordered((x_rows, swap(sent[0][:16])))
-    x_here = exchange(x_rows).reshape(PADDED, QUARTER)
-    x_own, x_below, x_above, x_far = ring(*halves(x_here, (*blocks, token)))
-    d_here = exchange(d_rows).reshape(PADDED, QUARTER)
+    x_rows, token = ordered((x_rows, swap(few)))
+    x_here = exchange(x_rows)
+    x_own, x_below, x_above, x_far = ring(*halves(x_here, token))
+    d_here = exchange(d_rows)
 
     own, *out = terms(at, d_here, wd, blocks)
     others = [shift(out[b - 1], -b) for b in (2, 1, 3)]
@@ -569,7 +581,7 @@
     s_near = (slope, s_below, s_above)
     s_far, summed = ordered((s_far, back_near(at, s_near, wg, wu, blocks)))
     pay = back_rows(at, (*s_near, *s_far), summed, blocks[1])
-    back = exchange(pay).reshape(PADDED, QUARTER)
+    back = exchange(pay)
     d_tokens, d_probs = combine(slot, ids, probs, code, pick, back)
 
     hid = ordered((hid, s_far))[0]

time: 239 us -> 229 us (0.958)
  local copies, waits for them, and re-layouts: 28.8 us -> 9.04 us
  Pallas kernels: 47.5 us -> 53.8 us
  waiting for transfers between devices: 98.5 us -> 103 us
    reshape x6 -> x0, local copies, waits for them, and re-layouts: 18 us -> none  [the longest x3 8.43 us: exchange(): rows.reshape(SLOTS, 3, 4, QUARTER)]
    all_to_all x3, waiting for transfers between devices: 36.9 us -> 46.2 us  [exchange(): lax.all_to_all(rows.reshape(SLOTS, 3, 4, QUARTER), 'expert', split_axis=0...]
    ppermute x22, waiting for transfers between devices: 61.2 us -> 56.8 us  [shift(): return lax.ppermute(x, 'dp', [(i, (i + by) % N_DP) for i in range(N_DP)])]
    ppermute x22, starting transfers between devices: 25.4 us -> 21.6 us  [shift(): return lax.ppermute(x, 'dp', [(i, (i + by) % N_DP) for i in range(N_DP)])]
    ppermute x4, starting transfers between devices: 3.15 us -> 5.6 us  [swap(): return lax.ppermute(x, 'expert', [(i, i ^ 1) for i in range(SLOTS)])]
    unnamed x70 -> x62, local copies, waits for them, and re-layouts: 9.97 us -> 8.29 us
  transfers between devices with their start and end apart: 29 -> 29, of which waited for: 13 -> 15; matrix products, arithmetic and copies ran while one was open for 7% -> 0% of each run, Pallas kernels for 17% -> 20%
where the time goes in v4:
time: 229 us; the launch traced here: 228 us
  waiting for transfers between devices  103 us (45%)
  starting transfers between devices  60.7 us (27%)
  Pallas kernels  53.8 us (23%)
  local copies, waits for them, and re-layouts  9.04 us (4%)
    ppermute x22, waiting for transfers between devices, shift(): return lax.ppermute(x, 'dp', [(i, (i + by) % N_DP) for i in range(N_DP)])  56.8 us
    all_to_all x3, waiting for transfers between devices, exchange(): lax.all_to_all(rows.reshape(SLOTS, 3, 4, QUARTER), 'expert', split_axis=0...  46.2 us
    all_to_all x3, starting transfers between devices, exchange(): lax.all_to_all(rows.reshape(SLOTS, 3, 4, QUARTER), 'expert', split_axis=0...  33.4 us
    ppermute x22, starting transfers between devices, shift(): return lax.ppermute(x, 'dp', [(i, (i + by) % N_DP) for i in range(N_DP)])  21.6 us
    unnamed x62, local copies, waits for them, and re-layouts  8.29 us
    pallas_call x1, Pallas kernels, grads(): pl.pallas_call(grads_kernel, out_shape=(jax.ShapeDtypeStruct((WIDTH, SHAR...  5.63 us
    ppermute x4, starting transfers between devices, swap(): return lax.ppermute(x, 'expert', [(i, i ^ 1) for i in range(SLOTS)])  5.6 us
    pallas_call x1, Pallas kernels, back_near(): pl.pallas_call(back_near_kernel, out_shape=jax.ShapeDtypeStruct((PADDED,...  5.43 us
  transfers between devices with their start and end apart: 29, of which 15 were waited for; matrix products, arithmetic and copies ran while one was open for 0% of the time, Pallas kernels for 20%

profile of v4, /device:TPU:1, one launch (start us, length us, event | category | flops | bytes accessed | tf_op | source)
XLA Modules:
  0.0 228.0 jit_solution(10437817859887136351)
XLA Ops:
  0.6 4.2 %shard_map.120 = (bf16[2688,256]{1,0:T(8,128)(2,1)}, bf16[2688,256]{1,0:T(8,128)(2,1)}, bf16[2688,256]{1,0:T(8,128)(2,1)}, bf16[16,128]{1,0:T(8,128)(2,1)}) custom-call(s32[1]{0:T(128)} %bitcast.3.at_ref, bf16[3584,256]{1,0:T(8,128)(2,1)} %bitcast.18, bf16[3584,256]{1,0:T(8,128)(2,1)} %bitcast.22, bf16[256,3584]{1,0:T(8,128)(2,1)} %bitcast.35), custom_call_target="tpu_custom_call" | custom-call | bytes 9600000 | tf_op jit(solution)/shard_map/pallas_call | solution.py:186
  4.9 3.3 %collective-permute-start = (bf16[16,128]{1,0:T(8,128)(2,1)}, bf16[16,128]{1,0:T(8,128)(2,1)S(1)}, u32[]{:S(2)}, u32[]{:S(2)}) collective-permute-start(bf16[16,128]{1,0:T(8,128)(2,1)} %get-tuple-element.67), channel_id=1, source_target_pairs={{0,1},{1,0},{2,3},{3,2},{4,5},{5,4},{6,7},{7,6},{8,9},{9,8},{10,11... | collective-permute-start | bytes 12296 | tf_op jit(solution)/shard_map/ppermute | solution.py:536
  12.2 2.9 %shard_map.119 = (bf16[192,4,896]{2,1,0:T(4,128)(2,1)}, f32[64,128]{1,0:T(8,128)}, bf16[768,128]{1,0:T(8,128)(2,1)}, bf16[768,128]{1,0:T(8,128)(2,1)}) custom-call(s32[1]{0:T(128)} %bitcast.2.parity_ref, f32[64,128]{1,0:T(8,128)} %broadcast_in_dim.15.slot_ref, s32[4,128]{1,0:T(4,128)} %bitcast.31, bf16[4,128]{1,0:T(4,128)(2,1)} %bitcast.33, ...), custom_call_target="tpu_custom_call" | custom-call | flops 40000000000 | bytes 3000000 | tf_op jit(solution)/shard_map/pallas_call | solution.py:80
  15.7 12.4 %all-to-all-start = ((bf16[64,3,4,896]{3,2,1,0:T(4,128)(2,1)}), bf16[64,3,4,896]{3,2,1,0:T(4,128)(2,1)S(1)}, u32[]{:S(2)}, u32[]{:S(2)}) async-start(bf16[64,3,4,896]{3,2,1,0:T(4,128)(2,1)} %bitcast.39), calls=%async_computation | async-start | bytes 2752512 | tf_op jit(solution)/shard_map/all_to_all | solution.py:540
  29.7 34.0 %all-to-all-done = bf16[64,3,4,896]{3,2,1,0:T(4,128)(2,1)S(1)} async-done(((bf16[64,3,4,896]{3,2,1,0:T(4,128)(2,1)}), bf16[64,3,4,896]{3,2,1,0:T(4,128)(2,1)S(1)}, u32[]{:S(2)}, u32[]{:S(2)}) %all-to-all-start) | async-done | bytes 1376288 | tf_op jit(solution)/shard_map/all_to_all | solution.py:540
  64.7 6.2 %all-to-all-start.1 = ((bf16[64,3,4,896]{3,2,1,0:T(4,128)(2,1)}), bf16[64,3,4,896]{3,2,1,0:T(4,128)(2,1)S(1)}, u32[]{:S(2)}, u32[]{:S(2)}) async-start(bf16[64,3,4,896]{3,2,1,0:T(4,128)(2,1)} %bitcast.30), calls=%async_computation.1 | async-start | bytes 2752512 | tf_op jit(solution)/shard_map/all_to_all | solution.py:540
  77.6 13.9 %collective-permute-done.1.refs_2_ = bf16[384,896]{1,0:T(8,128)(2,1)} collective-permute-done((bf16[384,896]{1,0:T(8,128)(2,1)}, bf16[384,896]{1,0:T(8,128)(2,1)}, u32[]{:S(2)}, u32[]{:S(2)}) %collective-permute-start.1) | collective-permute-done | bytes 688160 | tf_op jit(solution)/shard_map/ppermute | solution.py:532
  94.2 12.3 %all-to-all-done.1 = bf16[64,3,4,896]{3,2,1,0:T(4,128)(2,1)S(1)} async-done(((bf16[64,3,4,896]{3,2,1,0:T(4,128)(2,1)}), bf16[64,3,4,896]{3,2,1,0:T(4,128)(2,1)S(1)}, u32[]{:S(2)}, u32[]{:S(2)}) %all-to-all-start.1) | async-done | bytes 1376288 | tf_op jit(solution)/shard_map/all_to_all | solution.py:540
  107.6 5.3 %shard_map.123 = (f32[768,256]{1,0:T(8,128)}, bf16[768,256]{1,0:T(8,128)(2,1)}, bf16[768,256]{1,0:T(8,128)(2,1)}, bf16[768,256]{1,0:T(8,128)(2,1)}) custom-call(s32[1]{0:T(128)} %bitcast.3.at_ref, bf16[192,4,896]{2,1,0:T(4,128)(2,1)} %bitcast.27, bf16[256,3584]{1,0:T(8,128)(2,1)} %bitcast.36, bf16[2688,256]{1,0:T(8,128)(2,1)} %collective-permute-done.5.w1.g1, ...), custom_call_target="tpu_custom_call" | custom-call | flops 1409286144 | bytes 5000000 | tf_op jit(solution)/shard_map/pallas_call | solution.py:300
  115.9 4.8 %shard_map.124.sum_ref = f32[768,512]{1,0:T(8,128)S(1)} custom-call(s32[1]{0:T(128)} %bitcast.3.at_ref, bf16[384,896]{1,0:T(8,128)(2,1)S(1)} %copy-done.7, bf16[384,896]{1,0:T(8,128)(2,1)S(1)} %copy-done.8, bf16[384,896]{1,0:T(8,128)(2,1)} %collective-permute-done.1.refs_2_, bf16[384,896]{1,0:T(8,128)(2,1)} %collective-permute-done.2.refs_3_, ...), custom_call_target="tpu_custom_call" | custom-call | flops 2113929216 | bytes 9000000 | tf_op jit(solution)/shard_map/pallas_call | solution.py:240
  120.8 8.6 %collective-permute-done.11.low.refs_6_ = bf16[384,896]{1,0:T(8,128)(2,1)} collective-permute-done((bf16[384,896]{1,0:T(8,128)(2,1)}, bf16[384,896]{1,0:T(8,128)(2,1)}, u32[]{:S(2)}, u32[]{:S(2)}) %collective-permute-start.11) | collective-permute-done | bytes 688160 | tf_op jit(solution)/shard_map/ppermute | solution.py:532
  129.4 4.2 %shard_map.125 = (bf16[768,256]{1,0:T(8,128)(2,1)}, f32[768,256]{1,0:T(8,128)S(1)}, f32[768,256]{1,0:T(8,128)S(1)}) custom-call(s32[1]{0:T(128)} %bitcast.3.at_ref, bf16[384,896]{1,0:T(8,128)(2,1)} %collective-permute-done.11.low.refs_6_, bf16[384,896]{1,0:T(8,128)(2,1)} %collective-permute-done.12.high.refs_7_, f32[768,512]{1,0:T(8,128)S(1)} %shard_map.124.sum_ref, ...), custom_call_target="tpu_custom_call" | custom-call | flops 704643072 | bytes 4000000 | tf_op jit(solution)/shard_map/pallas_call | solution.py:269
  133.5 3.3 %collective-permute-done.9.r2 = bf16[768,256]{1,0:T(8,128)(2,1)S(1)} collective-permute-done((bf16[768,256]{1,0:T(8,128)(2,1)}, bf16[768,256]{1,0:T(8,128)(2,1)S(1)}, u32[]{:S(2)}, u32[]{:S(2)}) %collective-permute-start.9) | collective-permute-done | bytes 393248 | tf_op jit(solution)/shard_map/ppermute | solution.py:532
  137.8 2.9 %shard_map.126.own.slope_ref = bf16[768,512]{1,0:T(8,128)(2,1)S(1)} custom-call(f32[768,256]{1,0:T(8,128)S(1)} %copy-done.11, bf16[768,256]{1,0:T(8,128)(2,1)S(1)} %collective-permute-done.8.r1, bf16[768,256]{1,0:T(8,128)(2,1)S(1)} %collective-permute-done.9.r2, bf16[768,256]{1,0:T(8,128)(2,1)S(1)} %collective-permute-done.10.r3, ...), custom_call_target="tpu_custom_call" | custom-call | flops 50000000 | bytes 5000000 | tf_op jit(solution)/shard_map/pallas_call | solution.py:344
  143.1 3.6 %shard_map.127 = (bf16[896,768]{1,0:T(8,128)(2,1)S(1)}, bf16[896,768]{1,0:T(8,128)(2,1)S(1)}, bf16[896,768]{1,0:T(8,128)(2,1)S(1)}, bf16[896,768]{1,0:T(8,128)(2,1)S(1)}) custom-call(bf16[384,896]{1,0:T(8,128)(2,1)S(1)} %copy-done.7, bf16[384,896]{1,0:T(8,128)(2,1)S(1)} %copy-done.9, bf16[384,896]{1,0:T(8,128)(2,1)} %collective-permute-done.1.refs_2_, ...), custom_call_target="tpu_custom_call" | custom-call | bytes 12000000 | tf_op jit(solution)/shard_map/pallas_call | solution.py:430
  150.0 8.5 %collective-permute-done.14.above = bf16[768,512]{1,0:T(8,128)(2,1)S(1)} collective-permute-done((bf16[768,512]{1,0:T(8,128)(2,1)S(1)}, bf16[768,512]{1,0:T(8,128)(2,1)S(1)}, u32[]{:S(2)}, u32[]{:S(2)}) %collective-permute-start.14) | collective-permute-done | bytes 786464 | tf_op jit(solution)/shard_map/ppermute | solution.py:532
  158.5 3.0 %collective-permute-done.13.below = bf16[768,512]{1,0:T(8,128)(2,1)S(1)} collective-permute-done((bf16[768,512]{1,0:T(8,128)(2,1)S(1)}, bf16[768,512]{1,0:T(8,128)(2,1)S(1)}, u32[]{:S(2)}, u32[]{:S(2)}) %collective-permute-start.13) | collective-permute-done | bytes 786464 | tf_op jit(solution)/shard_map/ppermute | solution.py:532
  163.1 5.4 %shard_map.128.sum_ref = f32[768,896]{1,0:T(8,128)S(1)} custom-call(s32[1]{0:T(128)} %bitcast.3.at_ref, bf16[768,512]{1,0:T(8,128)(2,1)S(1)} %shard_map.126.own.slope_ref, bf16[768,512]{1,0:T(8,128)(2,1)S(1)} %collective-permute-done.13.below, bf16[768,512]{1,0:T(8,128)(2,1)S(1)} %collective-permute-done.14.above, bf16[3584,256]{1,0:T(8,128)(2,1)S(1)} %bitcast.21, ...), custom_call_target="tpu_custom_call" | custom-call | flops 2113929216 | bytes 8000000 | tf_op jit(solution)/shard_map/pallas_call | solution.py:384
  175.4 14.9 %all-to-all-start.2 = ((bf16[64,3,4,896]{3,2,1,0:T(4,128)(2,1)}), bf16[64,3,4,896]{3,2,1,0:T(4,128)(2,1)S(1)}, u32[]{:S(2)}, u32[]{:S(2)}) async-start(bf16[64,3,4,896]{3,2,1,0:T(4,128)(2,1)} %bitcast.29), calls=%async_computation.2 | async-start | bytes 2752512 | tf_op jit(solution)/shard_map/all_to_all | solution.py:540
  191.6 3.5 %shard_map.133 = (bf16[256,896]{1,0:T(8,128)(2,1)S(1)}, bf16[256,896]{1,0:T(8,128)(2,1)S(1)}, bf16[256,896]{1,0:T(8,128)(2,1)S(1)}, bf16[256,896]{1,0:T(8,128)(2,1)S(1)}) custom-call(bf16[768,256]{1,0:T(8,128)(2,1)} %get-tuple-element.118.hid_ref.h0, bf16[768,256]{1,0:T(8,128)(2,1)} %collective-permute-done.19.h1, ...), custom_call_target="tpu_custom_call" | custom-call | flops 40000000000 | bytes 5000000 | tf_op jit(solution)/shard_map/pallas_call | solution.py:478
  198.2 5.6 %shard_map.131 = (bf16[3584,256]{1,0:T(8,128)(2,1)S(1)}, bf16[3584,256]{1,0:T(8,128)(2,1)S(1)}) custom-call(s32[1]{0:T(128)} %bitcast.3.at_ref, bf16[896,768]{1,0:T(8,128)(2,1)S(1)} %copy-done.20, bf16[896,768]{1,0:T(8,128)(2,1)S(1)} %copy-done.22, bf16[896,768]{1,0:T(8,128)(2,1)S(1)} %copy-done.24, bf16[896,768]{1,0:T(8,128)(2,1)S(1)} %copy-done.26, ...), custom_call_target="tpu_custom_call" | custom-call | flops 2818572288 | bytes 11000000 | tf_op jit(solution)/shard_map/pallas_call | solution.py:458
  206.2 3.1 %collective-permute-done.23.p2 = bf16[256,896]{1,0:T(8,128)(2,1)S(1)} collective-permute-done((bf16[256,896]{1,0:T(8,128)(2,1)S(1)}, bf16[256,896]{1,0:T(8,128)(2,1)S(1)}, u32[]{:S(2)}, u32[]{:S(2)}) %collective-permute-start.23) | collective-permute-done | bytes 458784 | tf_op jit(solution)/shard_map/ppermute | solution.py:532
  209.4 11.1 %collective-permute-done.24.p3 = bf16[256,896]{1,0:T(8,128)(2,1)S(1)} collective-permute-done((bf16[256,896]{1,0:T(8,128)(2,1)S(1)}, bf16[256,896]{1,0:T(8,128)(2,1)S(1)}, u32[]{:S(2)}, u32[]{:S(2)}) %collective-permute-start.24) | collective-permute-done | bytes 458784 | tf_op jit(solution)/shard_map/ppermute | solution.py:532
  221.2 3.0 %shard_map.132 = (bf16[3584,256]{1,0:T(8,128)(2,1)}, bf16[3584,256]{1,0:T(8,128)(2,1)}) custom-call(s32[64]{0:T(128)S(1)} %copy-done.17, s32[1]{0:T(128)} %bitcast.14.here_ref, bf16[3584,256]{1,0:T(8,128)(2,1)S(1)} %get-tuple-element.114.refs_0_, bf16[3584,256]{1,0:T(8,128)(2,1)S(1)} %get-tuple-element.115.refs_1_, ...), custom_call_target="tpu_custom_call" | custom-call | tf_op jit(solution)/shard_map/pallas_call | solution.py:502
  (117 shorter events, 47.0 us)
Async XLA Ops:
  8.2 67.9 %collective-permute-start.5 = (bf16[2688,256]{1,0:T(8,128)(2,1)}, bf16[2688,256]{1,0:T(8,128)(2,1)}, u32[]{:S(2)}, u32[]{:S(2)}) collective-permute-start(bf16[2688,256]{1,0:T(8,128)(2,1)} %get-tuple-element.73), channel_id=1, source_target_pairs={{0,64},{64,128},{128,192},{192,0},{1,65},{65,129},{129,193},{193,1... | collective-permute-start | bytes 4128776 | tf_op jit(solution)/shard_map/ppermute | solution.py:532
  8.2 68.0 %collective-permute-start.6 = (bf16[2688,256]{1,0:T(8,128)(2,1)}, bf16[2688,256]{1,0:T(8,128)(2,1)S(1)}, u32[]{:S(2)}, u32[]{:S(2)}) collective-permute-start(bf16[2688,256]{1,0:T(8,128)(2,1)} %get-tuple-element.74), channel_id=1, source_target_pairs={{0,128},{64,192},{128,0},{192,64},{1,129},{65,193},{129,1},{193,65... | collective-permute-start | bytes 4128776 | tf_op jit(solution)/shard_map/ppermute | solution.py:532
  10.4 83.8 %collective-permute-start.7 = (bf16[2688,256]{1,0:T(8,128)(2,1)}, bf16[2688,256]{1,0:T(8,128)(2,1)}, u32[]{:S(2)}, u32[]{:S(2)}) collective-permute-start(bf16[2688,256]{1,0:T(8,128)(2,1)} %get-tuple-element.75), channel_id=1, source_target_pairs={{0,192},{64,0},{128,64},{192,128},{1,193},{65,1},{129,65},{193,129... | collective-permute-start | bytes 4128776 | tf_op jit(solution)/shard_map/ppermute | solution.py:532
  15.7 48.0 %all-to-all-start = ((bf16[64,3,4,896]{3,2,1,0:T(4,128)(2,1)}), bf16[64,3,4,896]{3,2,1,0:T(4,128)(2,1)S(1)}, u32[]{:S(2)}, u32[]{:S(2)}) async-start(bf16[64,3,4,896]{3,2,1,0:T(4,128)(2,1)} %bitcast.39), calls=%async_computation | async-start | bytes 2752512 | tf_op jit(solution)/shard_map/all_to_all | solution.py:540
  64.7 41.7 %all-to-all-start.1 = ((bf16[64,3,4,896]{3,2,1,0:T(4,128)(2,1)}), bf16[64,3,4,896]{3,2,1,0:T(4,128)(2,1)S(1)}, u32[]{:S(2)}, u32[]{:S(2)}) async-start(bf16[64,3,4,896]{3,2,1,0:T(4,128)(2,1)} %bitcast.30), calls=%async_computation.1 | async-start | bytes 2752512 | tf_op jit(solution)/shard_map/all_to_all | solution.py:540
  73.4 18.1 %collective-permute-start.1 = (bf16[384,896]{1,0:T(8,128)(2,1)}, bf16[384,896]{1,0:T(8,128)(2,1)}, u32[]{:S(2)}, u32[]{:S(2)}) collective-permute-start(bf16[384,896]{1,0:T(8,128)(2,1)} %get-tuple-element.90.refs_0_), channel_id=1, source_target_pairs={{0,64},{64,128},{128,192},{192,0},{1,65},{65,129},{129,193},{193,1... | collective-permute-start | bytes 2064392 | tf_op jit(solution)/shard_map/ppermute | solution.py:532
  73.8 17.7 %collective-permute-start.4 = (bf16[384,896]{1,0:T(8,128)(2,1)}, bf16[384,896]{1,0:T(8,128)(2,1)}, u32[]{:S(2)}, u32[]{:S(2)}) collective-permute-start(bf16[384,896]{1,0:T(8,128)(2,1)} %get-tuple-element.91.refs_1_), channel_id=1, source_target_pairs={{0,192},{64,0},{128,64},{192,128},{1,193},{65,1},{129,65},{193,129... | collective-permute-start | bytes 2064392 | tf_op jit(solution)/shard_map/ppermute | solution.py:532
  76.1 37.0 %collective-permute-start.3 = (bf16[384,896]{1,0:T(8,128)(2,1)}, bf16[384,896]{1,0:T(8,128)(2,1)}, u32[]{:S(2)}, u32[]{:S(2)}) collective-permute-start(bf16[384,896]{1,0:T(8,128)(2,1)} %get-tuple-element.90.refs_0_), channel_id=1, source_target_pairs={{0,192},{64,0},{128,64},{192,128},{1,193},{65,1},{129,65},{193,129... | collective-permute-start | bytes 2064392 | tf_op jit(solution)/shard_map/ppermute | solution.py:532
  76.2 39.7 %collective-permute-start.2 = (bf16[384,896]{1,0:T(8,128)(2,1)}, bf16[384,896]{1,0:T(8,128)(2,1)}, u32[]{:S(2)}, u32[]{:S(2)}) collective-permute-start(bf16[384,896]{1,0:T(8,128)(2,1)} %get-tuple-element.91.refs_1_), channel_id=1, source_target_pairs={{0,64},{64,128},{128,192},{192,0},{1,65},{65,129},{129,193},{193,1... | collective-permute-start | bytes 2064392 | tf_op jit(solution)/shard_map/ppermute | solution.py:532
  91.5 37.8 %collective-permute-start.11 = (bf16[384,896]{1,0:T(8,128)(2,1)}, bf16[384,896]{1,0:T(8,128)(2,1)}, u32[]{:S(2)}, u32[]{:S(2)}) collective-permute-start(bf16[384,896]{1,0:T(8,128)(2,1)} %collective-permute-done.1.refs_2_), channel_id=1, source_target_pairs={{0,64},{64,128},{128,192},{192,0},{1,65},{65,129},{129,193},{193,1... | collective-permute-start | bytes 2064392 | tf_op jit(solution)/shard_map/ppermute | solution.py:532
  91.5 37.8 %collective-permute-start.12 = (bf16[384,896]{1,0:T(8,128)(2,1)}, bf16[384,896]{1,0:T(8,128)(2,1)}, u32[]{:S(2)}, u32[]{:S(2)}) collective-permute-start(bf16[384,896]{1,0:T(8,128)(2,1)} %collective-permute-done.4.refs_5_), channel_id=1, source_target_pairs={{0,192},{64,0},{128,64},{192,128},{1,193},{65,1},{129,65},{193,129... | collective-permute-start | bytes 2064392 | tf_op jit(solution)/shard_map/ppermute | solution.py:532
  112.9 20.6 %collective-permute-start.8 = (bf16[768,256]{1,0:T(8,128)(2,1)}, bf16[768,256]{1,0:T(8,128)(2,1)S(1)}, u32[]{:S(2)}, u32[]{:S(2)}) collective-permute-start(bf16[768,256]{1,0:T(8,128)(2,1)} %get-tuple-element.78), channel_id=1, source_target_pairs={{0,128},{64,192},{128,0},{192,64},{1,129},{65,193},{129,1},{193,65... | collective-permute-start | bytes 1179656 | tf_op jit(solution)/shard_map/ppermute | solution.py:532
  113.1 23.7 %collective-permute-start.9 = (bf16[768,256]{1,0:T(8,128)(2,1)}, bf16[768,256]{1,0:T(8,128)(2,1)S(1)}, u32[]{:S(2)}, u32[]{:S(2)}) collective-permute-start(bf16[768,256]{1,0:T(8,128)(2,1)} %get-tuple-element.79), channel_id=1, source_target_pairs={{0,192},{64,0},{128,64},{192,128},{1,193},{65,1},{129,65},{193,129... | collective-permute-start | bytes 1179656 | tf_op jit(solution)/shard_map/ppermute | solution.py:532
  115.9 21.9 %collective-permute-start.10 = (bf16[768,256]{1,0:T(8,128)(2,1)}, bf16[768,256]{1,0:T(8,128)(2,1)S(1)}, u32[]{:S(2)}, u32[]{:S(2)}) collective-permute-start(bf16[768,256]{1,0:T(8,128)(2,1)} %get-tuple-element.80), channel_id=1, source_target_pairs={{0,64},{64,128},{128,192},{192,0},{1,65},{65,129},{129,193},{193,1... | collective-permute-start | bytes 1179656 | tf_op jit(solution)/shard_map/ppermute | solution.py:532
  140.7 17.8 %collective-permute-start.14 = (bf16[768,512]{1,0:T(8,128)(2,1)S(1)}, bf16[768,512]{1,0:T(8,128)(2,1)S(1)}, u32[]{:S(2)}, u32[]{:S(2)}) collective-permute-start(bf16[768,512]{1,0:T(8,128)(2,1)S(1)} %shard_map.126.own.slope_ref), channel_id=1, source_target_pairs={{0,192},{64,0},{128,64},{192,128},{1,193},{65,1},{129,65},{193,129... | collective-permute-start | bytes 2359304 | tf_op jit(solution)/shard_map/ppermute | solution.py:532
  143.1 18.3 %collective-permute-start.13 = (bf16[768,512]{1,0:T(8,128)(2,1)S(1)}, bf16[768,512]{1,0:T(8,128)(2,1)S(1)}, u32[]{:S(2)}, u32[]{:S(2)}) collective-permute-start(bf16[768,512]{1,0:T(8,128)(2,1)S(1)} %shard_map.126.own.slope_ref), channel_id=1, source_target_pairs={{0,64},{64,128},{128,192},{192,0},{1,65},{65,129},{129,193},{193,1... | collective-permute-start | bytes 2359304 | tf_op jit(solution)/shard_map/ppermute | solution.py:532
  170.9 19.4 %collective-permute-start.21 = (bf16[768,256]{1,0:T(8,128)(2,1)}, bf16[768,256]{1,0:T(8,128)(2,1)}, u32[]{:S(2)}, u32[]{:S(2)}) collective-permute-start(bf16[768,256]{1,0:T(8,128)(2,1)} %get-tuple-element.118.hid_ref.h0), channel_id=1, source_target_pairs={{0,192},{64,0},{128,64},{192,128},{1,193},{65,1},{129,65},{193,129... | collective-permute-start | bytes 1179656 | tf_op jit(solution)/shard_map/ppermute | solution.py:532
  171.2 19.1 %collective-permute-start.20 = (bf16[768,256]{1,0:T(8,128)(2,1)}, bf16[768,256]{1,0:T(8,128)(2,1)}, u32[]{:S(2)}, u32[]{:S(2)}) collective-permute-start(bf16[768,256]{1,0:T(8,128)(2,1)} %get-tuple-element.118.hid_ref.h0), channel_id=1, source_target_pairs={{0,128},{64,192},{128,0},{192,64},{1,129},{65,193},{129,1},{193,65... | collective-permute-start | bytes 1179656 | tf_op jit(solution)/shard_map/ppermute | solution.py:532
  172.4 19.2 %collective-permute-start.19 = (bf16[768,256]{1,0:T(8,128)(2,1)}, bf16[768,256]{1,0:T(8,128)(2,1)}, u32[]{:S(2)}, u32[]{:S(2)}) collective-permute-start(bf16[768,256]{1,0:T(8,128)(2,1)} %get-tuple-element.118.hid_ref.h0), channel_id=1, source_target_pairs={{0,64},{64,128},{128,192},{192,0},{1,65},{65,129},{129,193},{193,1... | collective-permute-start | bytes 1179656 | tf_op jit(solution)/shard_map/ppermute | solution.py:532
  175.4 51.3 %all-to-all-start.2 = ((bf16[64,3,4,896]{3,2,1,0:T(4,128)(2,1)}), bf16[64,3,4,896]{3,2,1,0:T(4,128)(2,1)S(1)}, u32[]{:S(2)}, u32[]{:S(2)}) async-start(bf16[64,3,4,896]{3,2,1,0:T(4,128)(2,1)} %bitcast.29), calls=%async_computation.2 | async-start | bytes 2752512 | tf_op jit(solution)/shard_map/all_to_all | solution.py:540
  196.7 12.6 %collective-permute-start.23 = (bf16[256,896]{1,0:T(8,128)(2,1)S(1)}, bf16[256,896]{1,0:T(8,128)(2,1)S(1)}, u32[]{:S(2)}, u32[]{:S(2)}) collective-permute-start(bf16[256,896]{1,0:T(8,128)(2,1)S(1)} %get-tuple-element.121), channel_id=1, source_target_pairs={{0,128},{64,192},{128,0},{192,64},{1,129},{65,193},{129,1},{193,65... | collective-permute-start | bytes 1376264 | tf_op jit(solution)/shard_map/ppermute | solution.py:532
  197.4 23.1 %collective-permute-start.24 = (bf16[256,896]{1,0:T(8,128)(2,1)S(1)}, bf16[256,896]{1,0:T(8,128)(2,1)S(1)}, u32[]{:S(2)}, u32[]{:S(2)}) collective-permute-start(bf16[256,896]{1,0:T(8,128)(2,1)S(1)} %get-tuple-element.122), channel_id=1, source_target_pairs={{0,64},{64,128},{128,192},{192,0},{1,65},{65,129},{129,193},{193,1... | collective-permute-start | bytes 1376264 | tf_op jit(solution)/shard_map/ppermute | solution.py:532
  203.8 17.4 %collective-permute-start.17 = (bf16[3584,256]{1,0:T(8,128)(2,1)S(1)}, bf16[3584,256]{1,0:T(8,128)(2,1)S(1)}, u32[]{:S(2)}, u32[]{:S(2)}) collective-permute-start(bf16[3584,256]{1,0:T(8,128)(2,1)S(1)} %get-tuple-element.114.refs_0_), channel_id=1, source_target_pairs={{0,1},{1,0},{2,3},{3,2},{4,5},{5,4},{6,7},{7,6},{8,9},{9,8},{10,11... | collective-permute-start | bytes 5505032 | tf_op jit(solution)/shard_map/ppermute | solution.py:536
  205.4 15.8 %collective-permute-start.18 = (bf16[3584,256]{1,0:T(8,128)(2,1)S(1)}, bf16[3584,256]{1,0:T(8,128)(2,1)S(1)}, u32[]{:S(2)}, u32[]{:S(2)}) collective-permute-start(bf16[3584,256]{1,0:T(8,128)(2,1)S(1)} %get-tuple-element.115.refs_1_), channel_id=1, source_target_pairs={{0,1},{1,0},{2,3},{3,2},{4,5},{5,4},{6,7},{7,6},{8,9},{9,8},{10,11... | collective-permute-start | bytes 5505032 | tf_op jit(solution)/shard_map/ppermute | solution.py:536
  (36 other events, 257.0 us)

commit v5 on v4

--- a/solution.py
+++ b/solution.py
@@ -563,8 +563,9 @@
     x_rows, code, pick, scaled = pack(parity, slot, ids, probs, tokens)
     d_rows = scale(scaled, cotangent)
     *sent, few = weights(at, wg, wu, wd)
+    x_rows, token = ordered((x_rows, swap(few)))
+    sent[1] = ordered((sent[1], x_rows))[0]
     blocks = [shift(w, b) for w, b in zip(sent, (1, 2, 3))]
-    x_rows, token = ordered((x_rows, swap(few)))
     x_here = exchange(x_rows)
     x_own, x_below, x_above, x_far = ring(*halves(x_here, token))
     d_here = exchange(d_rows)

time: 229 us -> 227 us (level)
  waiting for transfers between devices: 103 us -> 100 us
    ppermute x22, starting transfers between devices: 21.6 us -> 24.5 us  [shift(): return lax.ppermute(x, 'dp', [(i, (i + by) % N_DP) for i in range(N_DP)])]
  transfers between devices with their start and end apart: 29 -> 29, of which waited for: 15 -> 14; matrix products, arithmetic and copies ran while one was open for 0% -> 0% of each run, Pallas kernels for 20% -> 20%
where the time goes in v5:
time: 227 us
  waiting for transfers between devices  100 us (44%)
  starting transfers between devices  61.5 us (27%)
  Pallas kernels  54.7 us (24%)
  local copies, waits for them, and re-layouts  9.03 us (4%)
    ppermute x22, waiting for transfers between devices, shift(): return lax.ppermute(x, 'dp', [(i, (i + by) % N_DP) for i in range(N_DP)])  55.4 us
    all_to_all x3, waiting for transfers between devices, exchange(): lax.all_to_all(rows.reshape(SLOTS, 3, 4, QUARTER), 'expert', split_axis=0...  44.5 us
    all_to_all x3, starting transfers between devices, exchange(): lax.all_to_all(rows.reshape(SLOTS, 3, 4, QUARTER), 'expert', split_axis=0...  31.4 us
    ppermute x22, starting transfers between devices, shift(): return lax.ppermute(x, 'dp', [(i, (i + by) % N_DP) for i in range(N_DP)])  24.5 us
    unnamed x62, local copies, waits for them, and re-layouts  8.29 us
    pallas_call x1, Pallas kernels, grads(): pl.pallas_call(grads_kernel, out_shape=(jax.ShapeDtypeStruct((WIDTH, SHAR...  5.63 us
    ppermute x4, starting transfers between devices, swap(): return lax.ppermute(x, 'expert', [(i, i ^ 1) for i in range(SLOTS)])  5.61 us
    pallas_call x1, Pallas kernels, terms(): pl.pallas_call(terms_kernel, out_shape=(jax.ShapeDtypeStruct((PADDED, SHA...  5.3 us
  transfers between devices with their start and end apart: 29, of which 14 were waited for; matrix products, arithmetic and copies ran while one was open for 0% of the time, Pallas kernels for 20%

profile of v5, /device:TPU:1, one launch (start us, length us, event | category | flops | bytes accessed | tf_op | source)
XLA Modules:
  0.0 226.6 jit_solution(17499532262601689601)
XLA Ops:
  0.6 4.2 %shard_map.120 = (bf16[2688,256]{1,0:T(8,128)(2,1)}, bf16[2688,256]{1,0:T(8,128)(2,1)}, bf16[2688,256]{1,0:T(8,128)(2,1)}, bf16[16,128]{1,0:T(8,128)(2,1)}) custom-call(s32[1]{0:T(128)} %bitcast.3.at_ref, bf16[3584,256]{1,0:T(8,128)(2,1)} %bitcast.18, bf16[3584,256]{1,0:T(8,128)(2,1)} %bitcast.22, bf16[256,3584]{1,0:T(8,128)(2,1)} %bitcast.35), custom_call_target="tpu_custom_call" | custom-call | bytes 9600000 | tf_op jit(solution)/shard_map/pallas_call | solution.py:186
  4.9 3.3 %collective-permute-start = (bf16[16,128]{1,0:T(8,128)(2,1)}, bf16[16,128]{1,0:T(8,128)(2,1)S(1)}, u32[]{:S(2)}, u32[]{:S(2)}) collective-permute-start(bf16[16,128]{1,0:T(8,128)(2,1)} %get-tuple-element.68), channel_id=1, source_target_pairs={{0,1},{1,0},{2,3},{3,2},{4,5},{5,4},{6,7},{7,6},{8,9},{9,8},{10,11... | collective-permute-start | bytes 12296 | tf_op jit(solution)/shard_map/ppermute | solution.py:536
  15.1 10.4 %all-to-all-start = ((bf16[64,3,4,896]{3,2,1,0:T(4,128)(2,1)}), bf16[64,3,4,896]{3,2,1,0:T(4,128)(2,1)S(1)}, u32[]{:S(2)}, u32[]{:S(2)}) async-start(bf16[64,3,4,896]{3,2,1,0:T(4,128)(2,1)} %bitcast.39), calls=%async_computation | async-start | bytes 2752512 | tf_op jit(solution)/shard_map/all_to_all | solution.py:540
  28.8 32.3 %all-to-all-done = bf16[64,3,4,896]{3,2,1,0:T(4,128)(2,1)S(1)} async-done(((bf16[64,3,4,896]{3,2,1,0:T(4,128)(2,1)}), bf16[64,3,4,896]{3,2,1,0:T(4,128)(2,1)S(1)}, u32[]{:S(2)}, u32[]{:S(2)}) %all-to-all-start) | async-done | bytes 1376288 | tf_op jit(solution)/shard_map/all_to_all | solution.py:540
  62.2 6.2 %all-to-all-start.1 = ((bf16[64,3,4,896]{3,2,1,0:T(4,128)(2,1)}), bf16[64,3,4,896]{3,2,1,0:T(4,128)(2,1)S(1)}, u32[]{:S(2)}, u32[]{:S(2)}) async-start(bf16[64,3,4,896]{3,2,1,0:T(4,128)(2,1)} %bitcast.30), calls=%async_computation.1 | async-start | bytes 2752512 | tf_op jit(solution)/shard_map/all_to_all | solution.py:540
  75.0 13.9 %collective-permute-done.1.refs_2_ = bf16[384,896]{1,0:T(8,128)(2,1)} collective-permute-done((bf16[384,896]{1,0:T(8,128)(2,1)}, bf16[384,896]{1,0:T(8,128)(2,1)}, u32[]{:S(2)}, u32[]{:S(2)}) %collective-permute-start.1) | collective-permute-done | bytes 688160 | tf_op jit(solution)/shard_map/ppermute | solution.py:532
  91.7 12.3 %all-to-all-done.1 = bf16[64,3,4,896]{3,2,1,0:T(4,128)(2,1)S(1)} async-done(((bf16[64,3,4,896]{3,2,1,0:T(4,128)(2,1)}), bf16[64,3,4,896]{3,2,1,0:T(4,128)(2,1)S(1)}, u32[]{:S(2)}, u32[]{:S(2)}) %all-to-all-start.1) | async-done | bytes 1376288 | tf_op jit(solution)/shard_map/all_to_all | solution.py:540
  105.0 5.3 %shard_map.123 = (f32[768,256]{1,0:T(8,128)}, bf16[768,256]{1,0:T(8,128)(2,1)}, bf16[768,256]{1,0:T(8,128)(2,1)}, bf16[768,256]{1,0:T(8,128)(2,1)}) custom-call(s32[1]{0:T(128)} %bitcast.3.at_ref, bf16[192,4,896]{2,1,0:T(4,128)(2,1)} %bitcast.27, bf16[256,3584]{1,0:T(8,128)(2,1)} %bitcast.36, bf16[2688,256]{1,0:T(8,128)(2,1)} %copy-done.5, ...), custom_call_target="tpu_custom_call" | custom-call | flops 1409286144 | bytes 5000000 | tf_op jit(solution)/shard_map/pallas_call | solution.py:300
  113.7 4.8 %shard_map.124.sum_ref = f32[768,512]{1,0:T(8,128)S(1)} custom-call(s32[1]{0:T(128)} %bitcast.3.at_ref, bf16[384,896]{1,0:T(8,128)(2,1)S(1)} %copy-done.7, bf16[384,896]{1,0:T(8,128)(2,1)S(1)} %copy-done.8, bf16[384,896]{1,0:T(8,128)(2,1)} %collective-permute-done.1.refs_2_, bf16[384,896]{1,0:T(8,128)(2,1)} %collective-permute-done.2.refs_3_, ...), custom_call_target="tpu_custom_call" | custom-call | flops 2113929216 | bytes 9000000 | tf_op jit(solution)/shard_map/pallas_call | solution.py:240
  118.6 4.2 %shard_map.125 = (bf16[768,256]{1,0:T(8,128)(2,1)}, f32[768,256]{1,0:T(8,128)S(1)}, f32[768,256]{1,0:T(8,128)S(1)}) custom-call(s32[1]{0:T(128)} %bitcast.3.at_ref, bf16[384,896]{1,0:T(8,128)(2,1)} %collective-permute-done.11.low.refs_6_, bf16[384,896]{1,0:T(8,128)(2,1)} %collective-permute-done.12.high.refs_7_, f32[768,512]{1,0:T(8,128)S(1)} %shard_map.124.sum_ref, ...), custom_call_target="tpu_custom_call" | custom-call | flops 704643072 | bytes 4000000 | tf_op jit(solution)/shard_map/pallas_call | solution.py:269
  122.8 4.0 %collective-permute-done.8.r1 = bf16[768,256]{1,0:T(8,128)(2,1)S(1)} collective-permute-done((bf16[768,256]{1,0:T(8,128)(2,1)}, bf16[768,256]{1,0:T(8,128)(2,1)S(1)}, u32[]{:S(2)}, u32[]{:S(2)}) %collective-permute-start.8) | collective-permute-done | bytes 393248 | tf_op jit(solution)/shard_map/ppermute | solution.py:532
  126.9 7.4 %collective-permute-done.9.r2 = bf16[768,256]{1,0:T(8,128)(2,1)S(1)} collective-permute-done((bf16[768,256]{1,0:T(8,128)(2,1)}, bf16[768,256]{1,0:T(8,128)(2,1)S(1)}, u32[]{:S(2)}, u32[]{:S(2)}) %collective-permute-start.9) | collective-permute-done | bytes 393248 | tf_op jit(solution)/shard_map/ppermute | solution.py:532
  140.5 3.6 %shard_map.127 = (bf16[896,768]{1,0:T(8,128)(2,1)S(1)}, bf16[896,768]{1,0:T(8,128)(2,1)S(1)}, bf16[896,768]{1,0:T(8,128)(2,1)S(1)}, bf16[896,768]{1,0:T(8,128)(2,1)S(1)}) custom-call(bf16[384,896]{1,0:T(8,128)(2,1)S(1)} %copy-done.7, bf16[384,896]{1,0:T(8,128)(2,1)S(1)} %copy-done.9, bf16[384,896]{1,0:T(8,128)(2,1)} %collective-permute-done.1.refs_2_, ...), custom_call_target="tpu_custom_call" | custom-call | bytes 12000000 | tf_op jit(solution)/shard_map/pallas_call | solution.py:430
  147.5 8.5 %collective-permute-done.14.above = bf16[768,512]{1,0:T(8,128)(2,1)S(1)} collective-permute-done((bf16[768,512]{1,0:T(8,128)(2,1)S(1)}, bf16[768,512]{1,0:T(8,128)(2,1)S(1)}, u32[]{:S(2)}, u32[]{:S(2)}) %collective-permute-start.14) | collective-permute-done | bytes 786464 | tf_op jit(solution)/shard_map/ppermute | solution.py:532
  155.9 3.0 %collective-permute-done.13.below = bf16[768,512]{1,0:T(8,128)(2,1)S(1)} collective-permute-done((bf16[768,512]{1,0:T(8,128)(2,1)S(1)}, bf16[768,512]{1,0:T(8,128)(2,1)S(1)}, u32[]{:S(2)}, u32[]{:S(2)}) %collective-permute-start.13) | collective-permute-done | bytes 786464 | tf_op jit(solution)/shard_map/ppermute | solution.py:532
  160.5 5.2 %shard_map.128.sum_ref = f32[768,896]{1,0:T(8,128)S(1)} custom-call(s32[1]{0:T(128)} %bitcast.3.at_ref, bf16[768,512]{1,0:T(8,128)(2,1)S(1)} %shard_map.126.own.slope_ref, bf16[768,512]{1,0:T(8,128)(2,1)S(1)} %collective-permute-done.13.below, bf16[768,512]{1,0:T(8,128)(2,1)S(1)} %collective-permute-done.14.above, bf16[3584,256]{1,0:T(8,128)(2,1)S(1)} %bitcast.21, ...), custom_call_target="tpu_custom_call" | custom-call | flops 2113929216 | bytes 8000000 | tf_op jit(solution)/shard_map/pallas_call | solution.py:384
  169.8 3.1 %shard_map.129 = bf16[192,4,896]{2,1,0:T(4,128)(2,1)S(1)} custom-call(s32[1]{0:T(128)} %bitcast.3.at_ref, bf16[768,512]{1,0:T(8,128)(2,1)S(1)} %shard_map.126.own.slope_ref, bf16[768,512]{1,0:T(8,128)(2,1)S(1)} %collective-permute-done.13.below, bf16[768,512]{1,0:T(8,128)(2,1)S(1)} %collective-permute-done.14.above, ...), custom_call_target="tpu_custom_call" | custom-call | flops 704643072 | bytes 8000000 | tf_op jit(solution)/shard_map/pallas_call | solution.py:403
  174.0 14.9 %all-to-all-start.2 = ((bf16[64,3,4,896]{3,2,1,0:T(4,128)(2,1)}), bf16[64,3,4,896]{3,2,1,0:T(4,128)(2,1)S(1)}, u32[]{:S(2)}, u32[]{:S(2)}) async-start(bf16[64,3,4,896]{3,2,1,0:T(4,128)(2,1)} %bitcast.29), calls=%async_computation.2 | async-start | bytes 2752512 | tf_op jit(solution)/shard_map/all_to_all | solution.py:540
  189.0 3.3 %shard_map.133 = (bf16[256,896]{1,0:T(8,128)(2,1)S(1)}, bf16[256,896]{1,0:T(8,128)(2,1)S(1)}, bf16[256,896]{1,0:T(8,128)(2,1)S(1)}, bf16[256,896]{1,0:T(8,128)(2,1)S(1)}) custom-call(bf16[768,256]{1,0:T(8,128)(2,1)} %get-tuple-element.120.hid_ref.h0, bf16[768,256]{1,0:T(8,128)(2,1)} %collective-permute-done.19.h1, ...), custom_call_target="tpu_custom_call" | custom-call | flops 40000000000 | bytes 5000000 | tf_op jit(solution)/shard_map/pallas_call | solution.py:478
  192.4 3.0 %collective-permute-start.22 = (bf16[256,896]{1,0:T(8,128)(2,1)S(1)}, bf16[256,896]{1,0:T(8,128)(2,1)S(1)}, u32[]{:S(2)}, u32[]{:S(2)}) collective-permute-start(bf16[256,896]{1,0:T(8,128)(2,1)S(1)} %get-tuple-element.122), channel_id=1, source_target_pairs={{0,192},{64,0},{128,64},{192,128},{1,193},{65,1},{129,65},{193,129... | collective-permute-start | bytes 1376264 | tf_op jit(solution)/shard_map/ppermute | solution.py:532
  196.8 5.6 %shard_map.131 = (bf16[3584,256]{1,0:T(8,128)(2,1)S(1)}, bf16[3584,256]{1,0:T(8,128)(2,1)S(1)}) custom-call(s32[1]{0:T(128)} %bitcast.3.at_ref, bf16[896,768]{1,0:T(8,128)(2,1)S(1)} %copy-done.20, bf16[896,768]{1,0:T(8,128)(2,1)S(1)} %copy-done.22, bf16[896,768]{1,0:T(8,128)(2,1)S(1)} %copy-done.24, bf16[896,768]{1,0:T(8,128)(2,1)S(1)} %copy-done.26, ...), custom_call_target="tpu_custom_call" | custom-call | flops 2818572288 | bytes 11000000 | tf_op jit(solution)/shard_map/pallas_call | solution.py:458
  204.2 10.1 %collective-permute-done.22.p1 = bf16[256,896]{1,0:T(8,128)(2,1)S(1)} collective-permute-done((bf16[256,896]{1,0:T(8,128)(2,1)S(1)}, bf16[256,896]{1,0:T(8,128)(2,1)S(1)}, u32[]{:S(2)}, u32[]{:S(2)}) %collective-permute-start.22) | collective-permute-done | bytes 458784 | tf_op jit(solution)/shard_map/ppermute | solution.py:532
  214.2 4.9 %collective-permute-done.24.p3 = bf16[256,896]{1,0:T(8,128)(2,1)S(1)} collective-permute-done((bf16[256,896]{1,0:T(8,128)(2,1)S(1)}, bf16[256,896]{1,0:T(8,128)(2,1)S(1)}, u32[]{:S(2)}, u32[]{:S(2)}) %collective-permute-start.24) | collective-permute-done | bytes 458784 | tf_op jit(solution)/shard_map/ppermute | solution.py:532
  219.9 3.0 %shard_map.132 = (bf16[3584,256]{1,0:T(8,128)(2,1)}, bf16[3584,256]{1,0:T(8,128)(2,1)}) custom-call(s32[64]{0:T(128)S(1)} %copy-done.17, s32[1]{0:T(128)} %bitcast.14.here_ref, bf16[3584,256]{1,0:T(8,128)(2,1)S(1)} %get-tuple-element.116.refs_0_, bf16[3584,256]{1,0:T(8,128)(2,1)S(1)} %get-tuple-element.117.refs_1_, ...), custom_call_target="tpu_custom_call" | custom-call | tf_op jit(solution)/shard_map/pallas_call | solution.py:502
  (117 shorter events, 49.2 us)
Async XLA Ops:
  8.2 65.3 %collective-permute-start.5 = (bf16[2688,256]{1,0:T(8,128)(2,1)}, bf16[2688,256]{1,0:T(8,128)(2,1)S(1)}, u32[]{:S(2)}, u32[]{:S(2)}) collective-permute-start(bf16[2688,256]{1,0:T(8,128)(2,1)} %get-tuple-element.74), channel_id=1, source_target_pairs={{0,64},{64,128},{128,192},{192,0},{1,65},{65,129},{129,193},{193,1... | collective-permute-start | bytes 4128776 | tf_op jit(solution)/shard_map/ppermute | solution.py:532
  8.2 65.7 %collective-permute-start.7 = (bf16[2688,256]{1,0:T(8,128)(2,1)}, bf16[2688,256]{1,0:T(8,128)(2,1)}, u32[]{:S(2)}, u32[]{:S(2)}) collective-permute-start(bf16[2688,256]{1,0:T(8,128)(2,1)} %get-tuple-element.77), channel_id=1, source_target_pairs={{0,192},{64,0},{128,64},{192,128},{1,193},{65,1},{129,65},{193,129... | collective-permute-start | bytes 4128776 | tf_op jit(solution)/shard_map/ppermute | solution.py:532
  15.1 46.0 %all-to-all-start = ((bf16[64,3,4,896]{3,2,1,0:T(4,128)(2,1)}), bf16[64,3,4,896]{3,2,1,0:T(4,128)(2,1)S(1)}, u32[]{:S(2)}, u32[]{:S(2)}) async-start(bf16[64,3,4,896]{3,2,1,0:T(4,128)(2,1)} %bitcast.39), calls=%async_computation | async-start | bytes 2752512 | tf_op jit(solution)/shard_map/all_to_all | solution.py:540
  27.1 64.5 %collective-permute-start.6 = (bf16[2688,256]{1,0:T(8,128)(2,1)}, bf16[2688,256]{1,0:T(8,128)(2,1)}, u32[]{:S(2)}, u32[]{:S(2)}) collective-permute-start(bf16[2688,256]{1,0:T(8,128)(2,1)} %get-tuple-element.76), channel_id=1, source_target_pairs={{0,128},{64,192},{128,0},{192,64},{1,129},{65,193},{129,1},{193,65... | collective-permute-start | bytes 4128776 | tf_op jit(solution)/shard_map/ppermute | solution.py:532
  62.2 41.7 %all-to-all-start.1 = ((bf16[64,3,4,896]{3,2,1,0:T(4,128)(2,1)}), bf16[64,3,4,896]{3,2,1,0:T(4,128)(2,1)S(1)}, u32[]{:S(2)}, u32[]{:S(2)}) async-start(bf16[64,3,4,896]{3,2,1,0:T(4,128)(2,1)} %bitcast.30), calls=%async_computation.1 | async-start | bytes 2752512 | tf_op jit(solution)/shard_map/all_to_all | solution.py:540
  70.9 18.1 %collective-permute-start.1 = (bf16[384,896]{1,0:T(8,128)(2,1)}, bf16[384,896]{1,0:T(8,128)(2,1)}, u32[]{:S(2)}, u32[]{:S(2)}) collective-permute-start(bf16[384,896]{1,0:T(8,128)(2,1)} %get-tuple-element.92.refs_0_), channel_id=1, source_target_pairs={{0,64},{64,128},{128,192},{192,0},{1,65},{65,129},{129,193},{193,1... | collective-permute-start | bytes 2064392 | tf_op jit(solution)/shard_map/ppermute | solution.py:532
  71.0 18.0 %collective-permute-start.4 = (bf16[384,896]{1,0:T(8,128)(2,1)}, bf16[384,896]{1,0:T(8,128)(2,1)}, u32[]{:S(2)}, u32[]{:S(2)}) collective-permute-start(bf16[384,896]{1,0:T(8,128)(2,1)} %get-tuple-element.93.refs_1_), channel_id=1, source_target_pairs={{0,192},{64,0},{128,64},{192,128},{1,193},{65,1},{129,65},{193,129... | collective-permute-start | bytes 2064392 | tf_op jit(solution)/shard_map/ppermute | solution.py:532
  73.6 38.7 %collective-permute-start.3 = (bf16[384,896]{1,0:T(8,128)(2,1)}, bf16[384,896]{1,0:T(8,128)(2,1)}, u32[]{:S(2)}, u32[]{:S(2)}) collective-permute-start(bf16[384,896]{1,0:T(8,128)(2,1)} %get-tuple-element.92.refs_0_), channel_id=1, source_target_pairs={{0,192},{64,0},{128,64},{192,128},{1,193},{65,1},{129,65},{193,129... | collective-permute-start | bytes 2064392 | tf_op jit(solution)/shard_map/ppermute | solution.py:532
  73.9 39.1 %collective-permute-start.2 = (bf16[384,896]{1,0:T(8,128)(2,1)}, bf16[384,896]{1,0:T(8,128)(2,1)}, u32[]{:S(2)}, u32[]{:S(2)}) collective-permute-start(bf16[384,896]{1,0:T(8,128)(2,1)} %get-tuple-element.93.refs_1_), channel_id=1, source_target_pairs={{0,64},{64,128},{128,192},{192,0},{1,65},{65,129},{129,193},{193,1... | collective-permute-start | bytes 2064392 | tf_op jit(solution)/shard_map/ppermute | solution.py:532
  89.0 29.6 %collective-permute-start.11 = (bf16[384,896]{1,0:T(8,128)(2,1)}, bf16[384,896]{1,0:T(8,128)(2,1)}, u32[]{:S(2)}, u32[]{:S(2)}) collective-permute-start(bf16[384,896]{1,0:T(8,128)(2,1)} %collective-permute-done.1.refs_2_), channel_id=1, source_target_pairs={{0,64},{64,128},{128,192},{192,0},{1,65},{65,129},{129,193},{193,1... | collective-permute-start | bytes 2064392 | tf_op jit(solution)/shard_map/ppermute | solution.py:532
  89.0 29.6 %collective-permute-start.12 = (bf16[384,896]{1,0:T(8,128)(2,1)}, bf16[384,896]{1,0:T(8,128)(2,1)}, u32[]{:S(2)}, u32[]{:S(2)}) collective-permute-start(bf16[384,896]{1,0:T(8,128)(2,1)} %collective-permute-done.4.refs_5_), channel_id=1, source_target_pairs={{0,192},{64,0},{128,64},{192,128},{1,193},{65,1},{129,65},{193,129... | collective-permute-start | bytes 2064392 | tf_op jit(solution)/shard_map/ppermute | solution.py:532
  110.3 16.5 %collective-permute-start.8 = (bf16[768,256]{1,0:T(8,128)(2,1)}, bf16[768,256]{1,0:T(8,128)(2,1)S(1)}, u32[]{:S(2)}, u32[]{:S(2)}) collective-permute-start(bf16[768,256]{1,0:T(8,128)(2,1)} %get-tuple-element.80), channel_id=1, source_target_pairs={{0,128},{64,192},{128,0},{192,64},{1,129},{65,193},{129,1},{193,65... | collective-permute-start | bytes 1179656 | tf_op jit(solution)/shard_map/ppermute | solution.py:532
  112.2 22.0 %collective-permute-start.9 = (bf16[768,256]{1,0:T(8,128)(2,1)}, bf16[768,256]{1,0:T(8,128)(2,1)S(1)}, u32[]{:S(2)}, u32[]{:S(2)}) collective-permute-start(bf16[768,256]{1,0:T(8,128)(2,1)} %get-tuple-element.81), channel_id=1, source_target_pairs={{0,192},{64,0},{128,64},{192,128},{1,193},{65,1},{129,65},{193,129... | collective-permute-start | bytes 1179656 | tf_op jit(solution)/shard_map/ppermute | solution.py:532
  113.0 22.2 %collective-permute-start.10 = (bf16[768,256]{1,0:T(8,128)(2,1)}, bf16[768,256]{1,0:T(8,128)(2,1)S(1)}, u32[]{:S(2)}, u32[]{:S(2)}) collective-permute-start(bf16[768,256]{1,0:T(8,128)(2,1)} %get-tuple-element.82), channel_id=1, source_target_pairs={{0,64},{64,128},{128,192},{192,0},{1,65},{65,129},{129,193},{193,1... | collective-permute-start | bytes 1179656 | tf_op jit(solution)/shard_map/ppermute | solution.py:532
  138.1 17.8 %collective-permute-start.14 = (bf16[768,512]{1,0:T(8,128)(2,1)S(1)}, bf16[768,512]{1,0:T(8,128)(2,1)S(1)}, u32[]{:S(2)}, u32[]{:S(2)}) collective-permute-start(bf16[768,512]{1,0:T(8,128)(2,1)S(1)} %shard_map.126.own.slope_ref), channel_id=1, source_target_pairs={{0,192},{64,0},{128,64},{192,128},{1,193},{65,1},{129,65},{193,129... | collective-permute-start | bytes 2359304 | tf_op jit(solution)/shard_map/ppermute | solution.py:532
  140.5 18.3 %collective-permute-start.13 = (bf16[768,512]{1,0:T(8,128)(2,1)S(1)}, bf16[768,512]{1,0:T(8,128)(2,1)S(1)}, u32[]{:S(2)}, u32[]{:S(2)}) collective-permute-start(bf16[768,512]{1,0:T(8,128)(2,1)S(1)} %shard_map.126.own.slope_ref), channel_id=1, source_target_pairs={{0,64},{64,128},{128,192},{192,0},{1,65},{65,129},{129,193},{193,1... | collective-permute-start | bytes 2359304 | tf_op jit(solution)/shard_map/ppermute | solution.py:532
  168.3 20.6 %collective-permute-start.21 = (bf16[768,256]{1,0:T(8,128)(2,1)}, bf16[768,256]{1,0:T(8,128)(2,1)}, u32[]{:S(2)}, u32[]{:S(2)}) collective-permute-start(bf16[768,256]{1,0:T(8,128)(2,1)} %get-tuple-element.120.hid_ref.h0), channel_id=1, source_target_pairs={{0,192},{64,0},{128,64},{192,128},{1,193},{65,1},{129,65},{193,129... | collective-permute-start | bytes 1179656 | tf_op jit(solution)/shard_map/ppermute | solution.py:532
  168.6 20.4 %collective-permute-start.20 = (bf16[768,256]{1,0:T(8,128)(2,1)}, bf16[768,256]{1,0:T(8,128)(2,1)}, u32[]{:S(2)}, u32[]{:S(2)}) collective-permute-start(bf16[768,256]{1,0:T(8,128)(2,1)} %get-tuple-element.120.hid_ref.h0), channel_id=1, source_target_pairs={{0,128},{64,192},{128,0},{192,64},{1,129},{65,193},{129,1},{193,65... | collective-permute-start | bytes 1179656 | tf_op jit(solution)/shard_map/ppermute | solution.py:532
  169.8 19.2 %collective-permute-start.19 = (bf16[768,256]{1,0:T(8,128)(2,1)}, bf16[768,256]{1,0:T(8,128)(2,1)}, u32[]{:S(2)}, u32[]{:S(2)}) collective-permute-start(bf16[768,256]{1,0:T(8,128)(2,1)} %get-tuple-element.120.hid_ref.h0), channel_id=1, source_target_pairs={{0,64},{64,128},{128,192},{192,0},{1,65},{65,129},{129,193},{193,1... | collective-permute-start | bytes 1179656 | tf_op jit(solution)/shard_map/ppermute | solution.py:532
  174.0 51.3 %all-to-all-start.2 = ((bf16[64,3,4,896]{3,2,1,0:T(4,128)(2,1)}), bf16[64,3,4,896]{3,2,1,0:T(4,128)(2,1)S(1)}, u32[]{:S(2)}, u32[]{:S(2)}) async-start(bf16[64,3,4,896]{3,2,1,0:T(4,128)(2,1)} %bitcast.29), calls=%async_computation.2 | async-start | bytes 2752512 | tf_op jit(solution)/shard_map/all_to_all | solution.py:540
  192.4 21.9 %collective-permute-start.22 = (bf16[256,896]{1,0:T(8,128)(2,1)S(1)}, bf16[256,896]{1,0:T(8,128)(2,1)S(1)}, u32[]{:S(2)}, u32[]{:S(2)}) collective-permute-start(bf16[256,896]{1,0:T(8,128)(2,1)S(1)} %get-tuple-element.122), channel_id=1, source_target_pairs={{0,192},{64,0},{128,64},{192,128},{1,193},{65,1},{129,65},{193,129... | collective-permute-start | bytes 1376264 | tf_op jit(solution)/shard_map/ppermute | solution.py:532
  195.3 18.9 %collective-permute-start.23 = (bf16[256,896]{1,0:T(8,128)(2,1)S(1)}, bf16[256,896]{1,0:T(8,128)(2,1)S(1)}, u32[]{:S(2)}, u32[]{:S(2)}) collective-permute-start(bf16[256,896]{1,0:T(8,128)(2,1)S(1)} %get-tuple-element.123), channel_id=1, source_target_pairs={{0,128},{64,192},{128,0},{192,64},{1,129},{65,193},{129,1},{193,65... | collective-permute-start | bytes 1376264 | tf_op jit(solution)/shard_map/ppermute | solution.py:532
  196.1 23.1 %collective-permute-start.24 = (bf16[256,896]{1,0:T(8,128)(2,1)S(1)}, bf16[256,896]{1,0:T(8,128)(2,1)S(1)}, u32[]{:S(2)}, u32[]{:S(2)}) collective-permute-start(bf16[256,896]{1,0:T(8,128)(2,1)S(1)} %get-tuple-element.124), channel_id=1, source_target_pairs={{0,64},{64,128},{128,192},{192,0},{1,65},{65,129},{129,193},{193,1... | collective-permute-start | bytes 1376264 | tf_op jit(solution)/shard_map/ppermute | solution.py:532
  202.5 17.4 %collective-permute-start.17 = (bf16[3584,256]{1,0:T(8,128)(2,1)S(1)}, bf16[3584,256]{1,0:T(8,128)(2,1)S(1)}, u32[]{:S(2)}, u32[]{:S(2)}) collective-permute-start(bf16[3584,256]{1,0:T(8,128)(2,1)S(1)} %get-tuple-element.116.refs_0_), channel_id=1, source_target_pairs={{0,1},{1,0},{2,3},{3,2},{4,5},{5,4},{6,7},{7,6},{8,9},{9,8},{10,11... | collective-permute-start | bytes 5505032 | tf_op jit(solution)/shard_map/ppermute | solution.py:536
  (36 other events, 258.7 us)

commit v6 on v5

--- a/solution.py
+++ b/solution.py
@@ -408,7 +408,7 @@
             in_specs=[slope] * 3 + half_specs(2 * SHARE) + [tile, both],
             out_specs=pl.BlockSpec((TILE // 4, 4, QUARTER), lambda m, at: (m, 0, 0)),
         ),
-        compiler_params=params(32),
+        compiler_params=params(56),
         cost_estimate=pl.CostEstimate(
             flops=PADDED * WIDTH * SHARE, bytes_accessed=8_000_000, transcendentals=0
         ),

time: 227 us -> 227 us (level)
    pallas_call x1, Pallas kernels: 3.05 us -> 5.88 us  [back_rows(): pl.pallas_call(back_kernel, out_shape=jax.ShapeDtypeStruct((FOURS, 4, QUA...]
    unnamed x62 -> x74, local copies, waits for them, and re-layouts: 8.29 us -> 8.77 us
  transfers between devices with their start and end apart: 29 -> 29, of which waited for: 14 -> 12; matrix products, arithmetic and copies ran while one was open for 0% -> 0% of each run, Pallas kernels for 20% -> 21%
where the time goes in v6:
time: 227 us
  waiting for transfers between devices  99.5 us (44%)
  starting transfers between devices  61.6 us (27%)
  Pallas kernels  54.9 us (24%)
  local copies, waits for them, and re-layouts  9.52 us (4%)
    ppermute x22, waiting for transfers between devices, shift(): return lax.ppermute(x, 'dp', [(i, (i + by) % N_DP) for i in range(N_DP)])  54.5 us
    all_to_all x3, waiting for transfers between devices, exchange(): lax.all_to_all(rows.reshape(SLOTS, 3, 4, QUARTER), 'expert', split_axis=0...  44.5 us
    all_to_all x3, starting transfers between devices, exchange(): lax.all_to_all(rows.reshape(SLOTS, 3, 4, QUARTER), 'expert', split_axis=0...  31.4 us
    ppermute x22, starting transfers between devices, shift(): return lax.ppermute(x, 'dp', [(i, (i + by) % N_DP) for i in range(N_DP)])  24.5 us
    unnamed x74, local copies, waits for them, and re-layouts  8.77 us
    pallas_call x1, Pallas kernels, back_rows(): pl.pallas_call(back_kernel, out_shape=jax.ShapeDtypeStruct((FOURS, 4, QUA...  5.88 us
    pallas_call x1, Pallas kernels, grads(): pl.pallas_call(grads_kernel, out_shape=(jax.ShapeDtypeStruct((WIDTH, SHAR...  5.63 us
    ppermute x4, starting transfers between devices, swap(): return lax.ppermute(x, 'expert', [(i, i ^ 1) for i in range(SLOTS)])  5.61 us
  transfers between devices with their start and end apart: 29, of which 12 were waited for; matrix products, arithmetic and copies ran while one was open for 0% of the time, Pallas kernels for 21%

profile of v6, /device:TPU:1, one launch (start us, length us, event | category | flops | bytes accessed | tf_op | source)
XLA Modules:
  0.0 226.5 jit_solution(17508214549455439980)
XLA Ops:
  0.6 4.3 %shard_map.120 = (bf16[2688,256]{1,0:T(8,128)(2,1)}, bf16[2688,256]{1,0:T(8,128)(2,1)}, bf16[2688,256]{1,0:T(8,128)(2,1)}, bf16[16,128]{1,0:T(8,128)(2,1)}) custom-call(s32[1]{0:T(128)} %bitcast.3.at_ref, bf16[3584,256]{1,0:T(8,128)(2,1)} %bitcast.18, bf16[3584,256]{1,0:T(8,128)(2,1)} %bitcast.22, bf16[256,3584]{1,0:T(8,128)(2,1)} %bitcast.34), custom_call_target="tpu_custom_call" | custom-call | bytes 9600000 | tf_op jit(solution)/shard_map/pallas_call | solution.py:186
  4.9 3.3 %collective-permute-start = (bf16[16,128]{1,0:T(8,128)(2,1)}, bf16[16,128]{1,0:T(8,128)(2,1)S(1)}, u32[]{:S(2)}, u32[]{:S(2)}) collective-permute-start(bf16[16,128]{1,0:T(8,128)(2,1)} %get-tuple-element.68), channel_id=1, source_target_pairs={{0,1},{1,0},{2,3},{3,2},{4,5},{5,4},{6,7},{7,6},{8,9},{9,8},{10,11... | collective-permute-start | bytes 12296 | tf_op jit(solution)/shard_map/ppermute | solution.py:536
  15.1 10.4 %all-to-all-start = ((bf16[64,3,4,896]{3,2,1,0:T(4,128)(2,1)}), bf16[64,3,4,896]{3,2,1,0:T(4,128)(2,1)S(1)}, u32[]{:S(2)}, u32[]{:S(2)}) async-start(bf16[64,3,4,896]{3,2,1,0:T(4,128)(2,1)} %bitcast.39), calls=%async_computation | async-start | bytes 2752512 | tf_op jit(solution)/shard_map/all_to_all | solution.py:540
  28.8 32.3 %all-to-all-done = bf16[64,3,4,896]{3,2,1,0:T(4,128)(2,1)S(1)} async-done(((bf16[64,3,4,896]{3,2,1,0:T(4,128)(2,1)}), bf16[64,3,4,896]{3,2,1,0:T(4,128)(2,1)S(1)}, u32[]{:S(2)}, u32[]{:S(2)}) %all-to-all-start) | async-done | bytes 1376288 | tf_op jit(solution)/shard_map/all_to_all | solution.py:540
  62.2 6.2 %all-to-all-start.1 = ((bf16[64,3,4,896]{3,2,1,0:T(4,128)(2,1)}), bf16[64,3,4,896]{3,2,1,0:T(4,128)(2,1)S(1)}, u32[]{:S(2)}, u32[]{:S(2)}) async-start(bf16[64,3,4,896]{3,2,1,0:T(4,128)(2,1)} %bitcast.29), calls=%async_computation.1 | async-start | bytes 2752512 | tf_op jit(solution)/shard_map/all_to_all | solution.py:540
  75.0 13.9 %collective-permute-done.1.refs_2_ = bf16[384,896]{1,0:T(8,128)(2,1)} collective-permute-done((bf16[384,896]{1,0:T(8,128)(2,1)}, bf16[384,896]{1,0:T(8,128)(2,1)}, u32[]{:S(2)}, u32[]{:S(2)}) %collective-permute-start.1) | collective-permute-done | bytes 688160 | tf_op jit(solution)/shard_map/ppermute | solution.py:532
  91.6 12.3 %all-to-all-done.1 = bf16[64,3,4,896]{3,2,1,0:T(4,128)(2,1)S(1)} async-done(((bf16[64,3,4,896]{3,2,1,0:T(4,128)(2,1)}), bf16[64,3,4,896]{3,2,1,0:T(4,128)(2,1)S(1)}, u32[]{:S(2)}, u32[]{:S(2)}) %all-to-all-start.1) | async-done | bytes 1376288 | tf_op jit(solution)/shard_map/all_to_all | solution.py:540
  105.0 5.3 %shard_map.123 = (f32[768,256]{1,0:T(8,128)}, bf16[768,256]{1,0:T(8,128)(2,1)}, bf16[768,256]{1,0:T(8,128)(2,1)}, bf16[768,256]{1,0:T(8,128)(2,1)}) custom-call(s32[1]{0:T(128)} %bitcast.3.at_ref, bf16[192,4,896]{2,1,0:T(4,128)(2,1)} %bitcast.27, bf16[256,3584]{1,0:T(8,128)(2,1)} %bitcast.35, bf16[2688,256]{1,0:T(8,128)(2,1)} %copy-done.7, ...), custom_call_target="tpu_custom_call" | custom-call | flops 1409286144 | bytes 5000000 | tf_op jit(solution)/shard_map/pallas_call | solution.py:300
  113.7 4.8 %shard_map.124.sum_ref = f32[768,512]{1,0:T(8,128)S(1)} custom-call(s32[1]{0:T(128)} %bitcast.3.at_ref, bf16[384,896]{1,0:T(8,128)(2,1)S(1)} %copy-done.11, bf16[384,896]{1,0:T(8,128)(2,1)S(1)} %copy-done.12, bf16[384,896]{1,0:T(8,128)(2,1)} %collective-permute-done.1.refs_2_, bf16[384,896]{1,0:T(8,128)(2,1)} %collective-permute-done.2.refs_3_, ...), custom_call_target="tpu_custom_call" | custom-call | flops 2113929216 | bytes 9000000 | tf_op jit(solution)/shard_map/pallas_call | solution.py:240
  118.6 3.5 %shard_map.125 = (bf16[768,256]{1,0:T(8,128)(2,1)S(1)}, f32[768,256]{1,0:T(8,128)S(1)}, f32[768,256]{1,0:T(8,128)S(1)}) custom-call(s32[1]{0:T(128)} %bitcast.3.at_ref, bf16[384,896]{1,0:T(8,128)(2,1)} %collective-permute-done.11.low.refs_6_, bf16[384,896]{1,0:T(8,128)(2,1)} %collective-permute-done.12.high.refs_7_, f32[768,512]{1,0:T(8,128)S(1)} %shard_map.124.sum_ref, ...), custom_call_target="tpu_custom_call" | custom-call | flops 704643072 | bytes 4000000 | tf_op jit(solution)/shard_map/pallas_call | solution.py:269
  122.0 4.8 %collective-permute-done.8.r1 = bf16[768,256]{1,0:T(8,128)(2,1)S(1)} collective-permute-done((bf16[768,256]{1,0:T(8,128)(2,1)}, bf16[768,256]{1,0:T(8,128)(2,1)S(1)}, u32[]{:S(2)}, u32[]{:S(2)}) %collective-permute-start.8) | collective-permute-done | bytes 393248 | tf_op jit(solution)/shard_map/ppermute | solution.py:532
  126.9 7.4 %collective-permute-done.9.r2 = bf16[768,256]{1,0:T(8,128)(2,1)S(1)} collective-permute-done((bf16[768,256]{1,0:T(8,128)(2,1)}, bf16[768,256]{1,0:T(8,128)(2,1)S(1)}, u32[]{:S(2)}, u32[]{:S(2)}) %collective-permute-start.9) | collective-permute-done | bytes 393248 | tf_op jit(solution)/shard_map/ppermute | solution.py:532
  139.0 3.6 %shard_map.127 = (bf16[896,768]{1,0:T(8,128)(2,1)S(1)}, bf16[896,768]{1,0:T(8,128)(2,1)S(1)}, bf16[896,768]{1,0:T(8,128)(2,1)S(1)}, bf16[896,768]{1,0:T(8,128)(2,1)S(1)}) custom-call(bf16[384,896]{1,0:T(8,128)(2,1)S(1)} %copy-done.11, bf16[384,896]{1,0:T(8,128)(2,1)S(1)} %copy-done.13, bf16[384,896]{1,0:T(8,128)(2,1)} %collective-permute-done.1.refs_2_, ...), custom_call_target="tpu_custom_call" | custom-call | bytes 12000000 | tf_op jit(solution)/shard_map/pallas_call | solution.py:430
  146.0 8.4 %collective-permute-done.14.above = bf16[768,512]{1,0:T(8,128)(2,1)S(1)} collective-permute-done((bf16[768,512]{1,0:T(8,128)(2,1)S(1)}, bf16[768,512]{1,0:T(8,128)(2,1)S(1)}, u32[]{:S(2)}, u32[]{:S(2)}) %collective-permute-start.14) | collective-permute-done | bytes 786464 | tf_op jit(solution)/shard_map/ppermute | solution.py:532
  154.4 3.0 %collective-permute-done.13.below = bf16[768,512]{1,0:T(8,128)(2,1)S(1)} collective-permute-done((bf16[768,512]{1,0:T(8,128)(2,1)S(1)}, bf16[768,512]{1,0:T(8,128)(2,1)S(1)}, u32[]{:S(2)}, u32[]{:S(2)}) %collective-permute-start.13) | collective-permute-done | bytes 786464 | tf_op jit(solution)/shard_map/ppermute | solution.py:532
  159.0 5.2 %shard_map.128.sum_ref = f32[768,896]{1,0:T(8,128)S(1)} custom-call(s32[1]{0:T(128)} %bitcast.3.at_ref, bf16[768,512]{1,0:T(8,128)(2,1)S(1)} %shard_map.126.own.slope_ref, bf16[768,512]{1,0:T(8,128)(2,1)S(1)} %collective-permute-done.13.below, bf16[768,512]{1,0:T(8,128)(2,1)S(1)} %collective-permute-done.14.above, bf16[3584,256]{1,0:T(8,128)(2,1)S(1)} %bitcast.21, ...), custom_call_target="tpu_custom_call" | custom-call | flops 2113929216 | bytes 8000000 | tf_op jit(solution)/shard_map/pallas_call | solution.py:384
  168.3 5.9 %shard_map.129 = bf16[192,4,896]{2,1,0:T(4,128)(2,1)} custom-call(s32[1]{0:T(128)} %bitcast.3.at_ref, bf16[768,512]{1,0:T(8,128)(2,1)} %copy-done.3, bf16[768,512]{1,0:T(8,128)(2,1)} %copy-done.10, bf16[768,512]{1,0:T(8,128)(2,1)} %copy-done.9, bf16[384,512]{1,0:T(8,128)(2,1)} %copy-done.35, bf16[384,512]{1,0:T(8,128)(2,1)} %copy-done.34, ...), custom_call_target="tpu_custom_call" | custom-call | flops 704643072 | bytes 8000000 | tf_op jit(solution)/shard_map/pallas_call | solution.py:403
  174.2 14.9 %all-to-all-start.2 = ((bf16[64,3,4,896]{3,2,1,0:T(4,128)(2,1)}), bf16[64,3,4,896]{3,2,1,0:T(4,128)(2,1)S(1)}, u32[]{:S(2)}, u32[]{:S(2)}) async-start(bf16[64,3,4,896]{3,2,1,0:T(4,128)(2,1)} %bitcast.36), calls=%async_computation.2 | async-start | bytes 2752512 | tf_op jit(solution)/shard_map/all_to_all | solution.py:540
  189.1 3.1 %shard_map.133 = (bf16[256,896]{1,0:T(8,128)(2,1)S(1)}, bf16[256,896]{1,0:T(8,128)(2,1)S(1)}, bf16[256,896]{1,0:T(8,128)(2,1)S(1)}, bf16[256,896]{1,0:T(8,128)(2,1)S(1)}) custom-call(bf16[768,256]{1,0:T(8,128)(2,1)S(1)} %get-tuple-element.120.hid_ref.h0, bf16[768,256]{1,0:T(8,128)(2,1)} %collective-permute-done.19.h1, ...), custom_call_target="tpu_custom_call" | custom-call | flops 40000000000 | bytes 5000000 | tf_op jit(solution)/shard_map/pallas_call | solution.py:478
  192.3 3.0 %collective-permute-start.22 = (bf16[256,896]{1,0:T(8,128)(2,1)S(1)}, bf16[256,896]{1,0:T(8,128)(2,1)S(1)}, u32[]{:S(2)}, u32[]{:S(2)}) collective-permute-start(bf16[256,896]{1,0:T(8,128)(2,1)S(1)} %get-tuple-element.122), channel_id=1, source_target_pairs={{0,192},{64,0},{128,64},{192,128},{1,193},{65,1},{129,65},{193,129... | collective-permute-start | bytes 1376264 | tf_op jit(solution)/shard_map/ppermute | solution.py:532
  196.8 5.6 %shard_map.131 = (bf16[3584,256]{1,0:T(8,128)(2,1)S(1)}, bf16[3584,256]{1,0:T(8,128)(2,1)S(1)}) custom-call(s32[1]{0:T(128)} %bitcast.3.at_ref, bf16[896,768]{1,0:T(8,128)(2,1)S(1)} %copy-done.24, bf16[896,768]{1,0:T(8,128)(2,1)S(1)} %copy-done.26, bf16[896,768]{1,0:T(8,128)(2,1)S(1)} %copy-done.28, bf16[896,768]{1,0:T(8,128)(2,1)S(1)} %copy-done.30, ...), custom_call_target="tpu_custom_call" | custom-call | flops 2818572288 | bytes 11000000 | tf_op jit(solution)/shard_map/pallas_call | solution.py:458
  204.1 10.1 %collective-permute-done.22.p1 = bf16[256,896]{1,0:T(8,128)(2,1)S(1)} collective-permute-done((bf16[256,896]{1,0:T(8,128)(2,1)S(1)}, bf16[256,896]{1,0:T(8,128)(2,1)S(1)}, u32[]{:S(2)}, u32[]{:S(2)}) %collective-permute-start.22) | collective-permute-done | bytes 458784 | tf_op jit(solution)/shard_map/ppermute | solution.py:532
  214.2 4.9 %collective-permute-done.24.p3 = bf16[256,896]{1,0:T(8,128)(2,1)S(1)} collective-permute-done((bf16[256,896]{1,0:T(8,128)(2,1)S(1)}, bf16[256,896]{1,0:T(8,128)(2,1)S(1)}, u32[]{:S(2)}, u32[]{:S(2)}) %collective-permute-start.24) | collective-permute-done | bytes 458784 | tf_op jit(solution)/shard_map/ppermute | solution.py:532
  219.8 3.0 %shard_map.132 = (bf16[3584,256]{1,0:T(8,128)(2,1)}, bf16[3584,256]{1,0:T(8,128)(2,1)}) custom-call(s32[64]{0:T(128)S(1)} %copy-done.21, s32[1]{0:T(128)} %bitcast.14.here_ref, bf16[3584,256]{1,0:T(8,128)(2,1)S(1)} %get-tuple-element.116.refs_0_, bf16[3584,256]{1,0:T(8,128)(2,1)S(1)} %get-tuple-element.117.refs_1_, ...), custom_call_target="tpu_custom_call" | custom-call | tf_op jit(solution)/shard_map/pallas_call | solution.py:502
  (129 shorter events, 46.5 us)
Async XLA Ops:
  8.2 65.3 %collective-permute-start.5 = (bf16[2688,256]{1,0:T(8,128)(2,1)}, bf16[2688,256]{1,0:T(8,128)(2,1)S(1)}, u32[]{:S(2)}, u32[]{:S(2)}) collective-permute-start(bf16[2688,256]{1,0:T(8,128)(2,1)} %get-tuple-element.74), channel_id=1, source_target_pairs={{0,64},{64,128},{128,192},{192,0},{1,65},{65,129},{129,193},{193,1... | collective-permute-start | bytes 4128776 | tf_op jit(solution)/shard_map/ppermute | solution.py:532
  8.2 65.6 %collective-permute-start.7 = (bf16[2688,256]{1,0:T(8,128)(2,1)}, bf16[2688,256]{1,0:T(8,128)(2,1)}, u32[]{:S(2)}, u32[]{:S(2)}) collective-permute-start(bf16[2688,256]{1,0:T(8,128)(2,1)} %get-tuple-element.77), channel_id=1, source_target_pairs={{0,192},{64,0},{128,64},{192,128},{1,193},{65,1},{129,65},{193,129... | collective-permute-start | bytes 4128776 | tf_op jit(solution)/shard_map/ppermute | solution.py:532
  15.1 46.0 %all-to-all-start = ((bf16[64,3,4,896]{3,2,1,0:T(4,128)(2,1)}), bf16[64,3,4,896]{3,2,1,0:T(4,128)(2,1)S(1)}, u32[]{:S(2)}, u32[]{:S(2)}) async-start(bf16[64,3,4,896]{3,2,1,0:T(4,128)(2,1)} %bitcast.39), calls=%async_computation | async-start | bytes 2752512 | tf_op jit(solution)/shard_map/all_to_all | solution.py:540
  27.1 64.5 %collective-permute-start.6 = (bf16[2688,256]{1,0:T(8,128)(2,1)}, bf16[2688,256]{1,0:T(8,128)(2,1)}, u32[]{:S(2)}, u32[]{:S(2)}) collective-permute-start(bf16[2688,256]{1,0:T(8,128)(2,1)} %get-tuple-element.76), channel_id=1, source_target_pairs={{0,128},{64,192},{128,0},{192,64},{1,129},{65,193},{129,1},{193,65... | collective-permute-start | bytes 4128776 | tf_op jit(solution)/shard_map/ppermute | solution.py:532
  62.2 41.7 %all-to-all-start.1 = ((bf16[64,3,4,896]{3,2,1,0:T(4,128)(2,1)}), bf16[64,3,4,896]{3,2,1,0:T(4,128)(2,1)S(1)}, u32[]{:S(2)}, u32[]{:S(2)}) async-start(bf16[64,3,4,896]{3,2,1,0:T(4,128)(2,1)} %bitcast.29), calls=%async_computation.1 | async-start | bytes 2752512 | tf_op jit(solution)/shard_map/all_to_all | solution.py:540
  70.9 18.1 %collective-permute-start.1 = (bf16[384,896]{1,0:T(8,128)(2,1)}, bf16[384,896]{1,0:T(8,128)(2,1)}, u32[]{:S(2)}, u32[]{:S(2)}) collective-permute-start(bf16[384,896]{1,0:T(8,128)(2,1)} %get-tuple-element.92.refs_0_), channel_id=1, source_target_pairs={{0,64},{64,128},{128,192},{192,0},{1,65},{65,129},{129,193},{193,1... | collective-permute-start | bytes 2064392 | tf_op jit(solution)/shard_map/ppermute | solution.py:532
  71.0 18.0 %collective-permute-start.4 = (bf16[384,896]{1,0:T(8,128)(2,1)}, bf16[384,896]{1,0:T(8,128)(2,1)}, u32[]{:S(2)}, u32[]{:S(2)}) collective-permute-start(bf16[384,896]{1,0:T(8,128)(2,1)} %get-tuple-element.93.refs_1_), channel_id=1, source_target_pairs={{0,192},{64,0},{128,64},{192,128},{1,193},{65,1},{129,65},{193,129... | collective-permute-start | bytes 2064392 | tf_op jit(solution)/shard_map/ppermute | solution.py:532
  73.6 38.6 %collective-permute-start.3 = (bf16[384,896]{1,0:T(8,128)(2,1)}, bf16[384,896]{1,0:T(8,128)(2,1)}, u32[]{:S(2)}, u32[]{:S(2)}) collective-permute-start(bf16[384,896]{1,0:T(8,128)(2,1)} %get-tuple-element.92.refs_0_), channel_id=1, source_target_pairs={{0,192},{64,0},{128,64},{192,128},{1,193},{65,1},{129,65},{193,129... | collective-permute-start | bytes 2064392 | tf_op jit(solution)/shard_map/ppermute | solution.py:532
  73.9 39.1 %collective-permute-start.2 = (bf16[384,896]{1,0:T(8,128)(2,1)}, bf16[384,896]{1,0:T(8,128)(2,1)}, u32[]{:S(2)}, u32[]{:S(2)}) collective-permute-start(bf16[384,896]{1,0:T(8,128)(2,1)} %get-tuple-element.93.refs_1_), channel_id=1, source_target_pairs={{0,64},{64,128},{128,192},{192,0},{1,65},{65,129},{129,193},{193,1... | collective-permute-start | bytes 2064392 | tf_op jit(solution)/shard_map/ppermute | solution.py:532
  89.0 29.6 %collective-permute-start.11 = (bf16[384,896]{1,0:T(8,128)(2,1)}, bf16[384,896]{1,0:T(8,128)(2,1)}, u32[]{:S(2)}, u32[]{:S(2)}) collective-permute-start(bf16[384,896]{1,0:T(8,128)(2,1)} %collective-permute-done.1.refs_2_), channel_id=1, source_target_pairs={{0,64},{64,128},{128,192},{192,0},{1,65},{65,129},{129,193},{193,1... | collective-permute-start | bytes 2064392 | tf_op jit(solution)/shard_map/ppermute | solution.py:532
  89.0 29.6 %collective-permute-start.12 = (bf16[384,896]{1,0:T(8,128)(2,1)}, bf16[384,896]{1,0:T(8,128)(2,1)}, u32[]{:S(2)}, u32[]{:S(2)}) collective-permute-start(bf16[384,896]{1,0:T(8,128)(2,1)} %collective-permute-done.4.refs_5_), channel_id=1, source_target_pairs={{0,192},{64,0},{128,64},{192,128},{1,193},{65,1},{129,65},{193,129... | collective-permute-start | bytes 2064392 | tf_op jit(solution)/shard_map/ppermute | solution.py:532
  110.3 16.5 %collective-permute-start.8 = (bf16[768,256]{1,0:T(8,128)(2,1)}, bf16[768,256]{1,0:T(8,128)(2,1)S(1)}, u32[]{:S(2)}, u32[]{:S(2)}) collective-permute-start(bf16[768,256]{1,0:T(8,128)(2,1)} %get-tuple-element.80), channel_id=1, source_target_pairs={{0,128},{64,192},{128,0},{192,64},{1,129},{65,193},{129,1},{193,65... | collective-permute-start | bytes 1179656 | tf_op jit(solution)/shard_map/ppermute | solution.py:532
  112.2 22.0 %collective-permute-start.9 = (bf16[768,256]{1,0:T(8,128)(2,1)}, bf16[768,256]{1,0:T(8,128)(2,1)S(1)}, u32[]{:S(2)}, u32[]{:S(2)}) collective-permute-start(bf16[768,256]{1,0:T(8,128)(2,1)} %get-tuple-element.81), channel_id=1, source_target_pairs={{0,192},{64,0},{128,64},{192,128},{1,193},{65,1},{129,65},{193,129... | collective-permute-start | bytes 1179656 | tf_op jit(solution)/shard_map/ppermute | solution.py:532
  113.0 22.2 %collective-permute-start.10 = (bf16[768,256]{1,0:T(8,128)(2,1)}, bf16[768,256]{1,0:T(8,128)(2,1)S(1)}, u32[]{:S(2)}, u32[]{:S(2)}) collective-permute-start(bf16[768,256]{1,0:T(8,128)(2,1)} %get-tuple-element.82), channel_id=1, source_target_pairs={{0,64},{64,128},{128,192},{192,0},{1,65},{65,129},{129,193},{193,1... | collective-permute-start | bytes 1179656 | tf_op jit(solution)/shard_map/ppermute | solution.py:532
  136.5 17.8 %collective-permute-start.14 = (bf16[768,512]{1,0:T(8,128)(2,1)S(1)}, bf16[768,512]{1,0:T(8,128)(2,1)S(1)}, u32[]{:S(2)}, u32[]{:S(2)}) collective-permute-start(bf16[768,512]{1,0:T(8,128)(2,1)S(1)} %shard_map.126.own.slope_ref), channel_id=1, source_target_pairs={{0,192},{64,0},{128,64},{192,128},{1,193},{65,1},{129,65},{193,129... | collective-permute-start | bytes 2359304 | tf_op jit(solution)/shard_map/ppermute | solution.py:532
  139.0 18.3 %collective-permute-start.13 = (bf16[768,512]{1,0:T(8,128)(2,1)S(1)}, bf16[768,512]{1,0:T(8,128)(2,1)S(1)}, u32[]{:S(2)}, u32[]{:S(2)}) collective-permute-start(bf16[768,512]{1,0:T(8,128)(2,1)S(1)} %shard_map.126.own.slope_ref), channel_id=1, source_target_pairs={{0,64},{64,128},{128,192},{192,0},{1,65},{65,129},{129,193},{193,1... | collective-permute-start | bytes 2359304 | tf_op jit(solution)/shard_map/ppermute | solution.py:532
  166.8 22.3 %collective-permute-start.21 = (bf16[768,256]{1,0:T(8,128)(2,1)S(1)}, bf16[768,256]{1,0:T(8,128)(2,1)S(1)}, u32[]{:S(2)}, u32[]{:S(2)}) collective-permute-start(bf16[768,256]{1,0:T(8,128)(2,1)S(1)} %get-tuple-element.120.hid_ref.h0), channel_id=1, source_target_pairs={{0,192},{64,0},{128,64},{192,128},{1,193},{65,1},{129,65},{193,129... | collective-permute-start | bytes 1179656 | tf_op jit(solution)/shard_map/ppermute | solution.py:532
  167.3 21.9 %collective-permute-start.20 = (bf16[768,256]{1,0:T(8,128)(2,1)S(1)}, bf16[768,256]{1,0:T(8,128)(2,1)}, u32[]{:S(2)}, u32[]{:S(2)}) collective-permute-start(bf16[768,256]{1,0:T(8,128)(2,1)S(1)} %get-tuple-element.120.hid_ref.h0), channel_id=1, source_target_pairs={{0,128},{64,192},{128,0},{192,64},{1,129},{65,193},{129,1},{193,65... | collective-permute-start | bytes 1179656 | tf_op jit(solution)/shard_map/ppermute | solution.py:532
  168.3 20.9 %collective-permute-start.19 = (bf16[768,256]{1,0:T(8,128)(2,1)S(1)}, bf16[768,256]{1,0:T(8,128)(2,1)}, u32[]{:S(2)}, u32[]{:S(2)}) collective-permute-start(bf16[768,256]{1,0:T(8,128)(2,1)S(1)} %get-tuple-element.120.hid_ref.h0), channel_id=1, source_target_pairs={{0,64},{64,128},{128,192},{192,0},{1,65},{65,129},{129,193},{193,1... | collective-permute-start | bytes 1179656 | tf_op jit(solution)/shard_map/ppermute | solution.py:532
  174.2 51.1 %all-to-all-start.2 = ((bf16[64,3,4,896]{3,2,1,0:T(4,128)(2,1)}), bf16[64,3,4,896]{3,2,1,0:T(4,128)(2,1)S(1)}, u32[]{:S(2)}, u32[]{:S(2)}) async-start(bf16[64,3,4,896]{3,2,1,0:T(4,128)(2,1)} %bitcast.36), calls=%async_computation.2 | async-start | bytes 2752512 | tf_op jit(solution)/shard_map/all_to_all | solution.py:540
  192.3 21.9 %collective-permute-start.22 = (bf16[256,896]{1,0:T(8,128)(2,1)S(1)}, bf16[256,896]{1,0:T(8,128)(2,1)S(1)}, u32[]{:S(2)}, u32[]{:S(2)}) collective-permute-start(bf16[256,896]{1,0:T(8,128)(2,1)S(1)} %get-tuple-element.122), channel_id=1, source_target_pairs={{0,192},{64,0},{128,64},{192,128},{1,193},{65,1},{129,65},{193,129... | collective-permute-start | bytes 1376264 | tf_op jit(solution)/shard_map/ppermute | solution.py:532
  195.3 18.9 %collective-permute-start.23 = (bf16[256,896]{1,0:T(8,128)(2,1)S(1)}, bf16[256,896]{1,0:T(8,128)(2,1)S(1)}, u32[]{:S(2)}, u32[]{:S(2)}) collective-permute-start(bf16[256,896]{1,0:T(8,128)(2,1)S(1)} %get-tuple-element.123), channel_id=1, source_target_pairs={{0,128},{64,192},{128,0},{192,64},{1,129},{65,193},{129,1},{193,65... | collective-permute-start | bytes 1376264 | tf_op jit(solution)/shard_map/ppermute | solution.py:532
  196.0 23.1 %collective-permute-start.24 = (bf16[256,896]{1,0:T(8,128)(2,1)S(1)}, bf16[256,896]{1,0:T(8,128)(2,1)S(1)}, u32[]{:S(2)}, u32[]{:S(2)}) collective-permute-start(bf16[256,896]{1,0:T(8,128)(2,1)S(1)} %get-tuple-element.124), channel_id=1, source_target_pairs={{0,64},{64,128},{128,192},{192,0},{1,65},{65,129},{129,193},{193,1... | collective-permute-start | bytes 1376264 | tf_op jit(solution)/shard_map/ppermute | solution.py:532
  202.4 17.4 %collective-permute-start.17 = (bf16[3584,256]{1,0:T(8,128)(2,1)S(1)}, bf16[3584,256]{1,0:T(8,128)(2,1)S(1)}, u32[]{:S(2)}, u32[]{:S(2)}) collective-permute-start(bf16[3584,256]{1,0:T(8,128)(2,1)S(1)} %get-tuple-element.116.refs_0_), channel_id=1, source_target_pairs={{0,1},{1,0},{2,3},{3,2},{4,5},{5,4},{6,7},{7,6},{8,9},{9,8},{10,11... | collective-permute-start | bytes 5505032 | tf_op jit(solution)/shard_map/ppermute | solution.py:536
  (42 other events, 307.5 us)
